TPU v7x, 32 devices: a whole 2x2x4 slice. The times are simulated.
32 devices in a mesh: grp: 2 (over y), seq: 8 (over z, x), doc: 2 (over core).
Axes of the slice: x: 2, y: 2, z: 4, core: 2. Of those that a mesh axis runs over, the one named last changes fastest.
Arguments:
- state: bfloat16 [32, 3, 1024, 1024], P(('grp', 'seq', 'doc')), parts along dimension 0, may hold values from -0.1875 to 0.1875
- keys: bfloat16 [2, 32, 384, 1024], P(None, ('grp', 'seq', 'doc')), parts along dimension 1, may hold values from -6 to 6
- values: bfloat16 [2, 32, 384, 1024], P(None, ('grp', 'seq', 'doc')), parts along dimension 1, may hold values from -6 to 6
- queries: bfloat16 [2, 32, 384, 1024], P(None, ('grp', 'seq', 'doc')), parts along dimension 1, may hold values from -6 to 6
- rates: float32 [2, 32, 384], P(None, 'grp'), parts along dimension 1, may hold values from 0.001 to 0.01
- remaining: int32 [32], P('grp'), parts along dimension 0, may hold values from 1 to 2
- first_owner: int32 [32], P('grp'), parts along dimension 0, may hold values from 0 to 15, each once
- migration: int32 [32], P('grp'), parts along dimension 0, may hold values from 0 to 15, as said below
Outputs:
- round_one: bfloat16 [32, 384, 1024], P(('grp', 'seq', 'doc')), parts along dimension 0
- round_two: bfloat16 [32, 384, 1024], P(('grp', 'seq', 'doc')), parts along dimension 0
There are 2 independent parts, one for each index of `grp`. A program takes and returns all parts, laid end to end along the dimension named above; each array names one. Nothing has to cross between parts.
Inputs may be any that keep to these rules, and one draw needn't show every extreme that they name: first_owner is a permutation: document d starts with the fast weights state[first_owner[d]]. migration is a permutation that leaves all but exactly 4 owners in place. `remaining`: a document has a round-two block exactly where its entry is 2.
All inputs are finite; a program needn't handle non-finite values.
Results may differ from a plain program's by a relative error of at most 0.012.
Values may be sent and summed in bfloat16 or wider, within the bound.
No kernel may reach another device: no remote copies, remote signals or barrier semaphores. Data moves between devices by JAX's collectives and lax.ppermute only.
A program may use at most 128 MiB of HBM per device.

v0:
```python
import jax
import jax.numpy as jnp
from jax import lax
from jax.sharding import PartitionSpec as P

EPSILON = 1e-06


def shortened(array):

    def short(part):
        return part.astype(jnp.bfloat16) if part.dtype == jnp.float32 else part

    return jax.tree.map(short, array)


def swiglu_apply(weights, inputs):
    gate_pre = jnp.dot(inputs, weights[0], preferred_element_type=jnp.float32)
    upward = jnp.dot(inputs, weights[1], preferred_element_type=jnp.float32)
    hidden = (jax.nn.silu(gate_pre) * upward).astype(jnp.bfloat16)
    return jnp.dot(hidden, weights[2], preferred_element_type=jnp.float32)


def renorm(weight, gradient):
    before = weight.astype(jnp.float32)
    stepped = before - gradient
    factor = jnp.sqrt(jnp.mean(before * before, axis=0) + EPSILON) / jnp.sqrt(
        jnp.mean(stepped * stepped, axis=0) + EPSILON
    )
    return (stepped * factor[None, :]).astype(jnp.bfloat16)


def fast_update(weights, keys_rows, values_rows, rate_rows):
    gate_pre = jnp.dot(keys_rows, weights[0], preferred_element_type=jnp.float32)
    upward = jnp.dot(keys_rows, weights[1], preferred_element_type=jnp.float32)
    sigmoid_gate = jax.nn.sigmoid(gate_pre)
    active = gate_pre * sigmoid_gate
    hidden = (active * upward).astype(jnp.bfloat16)
    scaled_values = (rate_rows[:, None] * values_rows.astype(jnp.float32)).astype(jnp.bfloat16)
    grad_down = -jnp.dot(hidden.T, scaled_values, preferred_element_type=jnp.float32)
    grad_hidden = -jnp.dot(scaled_values, weights[2].T, preferred_element_type=jnp.float32)
    slope = sigmoid_gate * (1.0 + gate_pre * (1.0 - sigmoid_gate))
    grad_gate = (grad_hidden * upward * slope).astype(jnp.bfloat16)
    grad_up = (grad_hidden * active).astype(jnp.bfloat16)
    grad_first = jnp.dot(keys_rows.T, grad_gate, preferred_element_type=jnp.float32)
    grad_third = jnp.dot(keys_rows.T, grad_up, preferred_element_type=jnp.float32)
    return jnp.stack(
        [
            renorm(weights[0], grad_first),
            renorm(weights[1], grad_third),
            renorm(weights[2], grad_down),
        ]
    )


def inverse_of(permuted):
    count = permuted.shape[0]
    labels = jnp.arange(count, dtype=jnp.int32)
    return jnp.sum(jnp.where(permuted[None, :] == labels[:, None], labels[None, :], 0), axis=1)


def move_rows(items):
    return jax.tree.map(
        lambda part, own: part.astype(own.dtype),
        lax.all_to_all(shortened(items), ("seq", "doc"), split_axis=0, concat_axis=0, tiled=True),
        items,
    )


def send_back(pieces):
    return lax.all_to_all(pieces, ("seq", "doc"), split_axis=0, concat_axis=0, tiled=True)


def move_result(pieces):
    return lax.all_to_all(pieces, ("seq", "doc"), split_axis=0, concat_axis=0, tiled=True)


def body(state, keys, values, queries, rates, remaining, first_owner, migration):
    devices = lax.axis_size(("seq", "doc"))
    myself = lax.axis_index(("seq", "doc"))
    doc_first = inverse_of(first_owner)
    source_of = inverse_of(migration)
    weights = state[0]
    width = weights.shape[-1]
    block_rows = keys.shape[2]
    piece_rows = block_rows // devices

    def to_owners(section, doc_for_owner):
        blocks = (keys[section, 0], values[section, 0], queries[section, 0])
        split = tuple((member.reshape(devices, piece_rows, width) for member in blocks))
        dealt = move_rows(split)
        reordered = tuple((jnp.take(member, doc_for_owner, axis=0) for member in dealt))
        collected = move_rows(reordered)
        return tuple((member.reshape(block_rows, width) for member in collected))

    def run_round(section, weights_in, doc_for_owner):
        doc_here = doc_for_owner[myself]
        keys_here, values_here, queries_here = to_owners(section, doc_for_owner)
        rate_here = lax.dynamic_index_in_dim(rates[section], doc_here, 0, keepdims=False)
        updated = fast_update(weights_in, keys_here, values_here, rate_here)
        return (updated, swiglu_apply(updated, queries_here), doc_here)

    updated, result_one, doc_one = run_round(0, weights, doc_first)
    outgoing = result_one.astype(jnp.bfloat16).reshape(devices, piece_rows, width)
    dealt_out = send_back(outgoing)
    returned = send_back(jnp.take(dealt_out, first_owner, axis=0))
    round_one = returned.reshape(1, block_rows, width)
    unused, result_two, doc_two = run_round(1, updated, doc_first)
    is_live = remaining[doc_two] >= 2
    masked = jnp.where(is_live, result_two, jnp.float32(0.0)).astype(jnp.bfloat16)
    dealt = move_result(masked.reshape(devices, piece_rows, width))
    regrouped = move_result(jnp.take(dealt, source_of, axis=0))
    round_two = regrouped.reshape(1, block_rows, width)
    return (round_one, round_two)


def solution(mesh):
    return jax.shard_map(
        body,
        mesh=mesh,
        in_specs=(
            P(("grp", "seq", "doc"), None, None, None),
            P(None, ("grp", "seq", "doc"), None, None),
            P(None, ("grp", "seq", "doc"), None, None),
            P(None, ("grp", "seq", "doc"), None, None),
            P(None, "grp", None),
            P("grp"),
            P("grp"),
            P("grp"),
        ),
        out_specs=(P(("grp", "seq", "doc"), None, None), P(("grp", "seq", "doc"), None, None)),
        check_vma=False,
    )
```

profile of v0, /device:TPU:1, one launch (start us, length us, event | category | flops | bytes accessed | tf_op | source)
XLA Modules:
  0.0 401.0 jit_solution(10262056367907416155)
XLA Ops:
  0.6 2.5 fusion.50
  3.1 7.3 %all-to-all-start.4 = ((bf16[16,24,1024]{2,1,0:T(8,128)(2,1)}), bf16[16,24,1024]{2,1,0:T(8,128)(2,1)S(1)}, u32[]{:S(2)}, u32[]{:S(2)}) async-start(bf16[16,24,1024]{2,1,0:T(8,128)(2,1)} %bitcast.6), calls=%async_computation.4 | async-start | bytes 1572864 | tf_op jit(solution)/shard_map/all_to_all | solution.py:65
  11.7 17.3 %all-to-all-done.4 = bf16[16,24,1024]{2,1,0:T(8,128)(2,1)S(1)} async-done(((bf16[16,24,1024]{2,1,0:T(8,128)(2,1)}), bf16[16,24,1024]{2,1,0:T(8,128)(2,1)S(1)}, u32[]{:S(2)}, u32[]{:S(2)}) %all-to-all-start.4) | async-done | bytes 786464 | tf_op jit(solution)/shard_map/all_to_all | solution.py:65
  29.0 5.6 %all-to-all-start.8 = ((bf16[16,24,1024]{2,1,0:T(8,128)(2,1)}), bf16[16,24,1024]{2,1,0:T(8,128)(2,1)S(1)}, u32[]{:S(2)}, u32[]{:S(2)}) async-start(bf16[16,24,1024]{2,1,0:T(8,128)(2,1)} %bitcast.14), calls=%async_computation.8 | async-start | bytes 1572864 | tf_op jit(solution)/shard_map/all_to_all | solution.py:65
  34.7 2.7 fusion.51
  37.3 15.9 %all-to-all-done.8 = bf16[16,24,1024]{2,1,0:T(8,128)(2,1)S(1)} async-done(((bf16[16,24,1024]{2,1,0:T(8,128)(2,1)}), bf16[16,24,1024]{2,1,0:T(8,128)(2,1)S(1)}, u32[]{:S(2)}, u32[]{:S(2)}) %all-to-all-start.8) | async-done | bytes 786464 | tf_op jit(solution)/shard_map/all_to_all | solution.py:65
  53.2 26.4 %all_to_all.80 = bf16[16,24,1024]{2,1,0:T(8,128)(2,1)S(1)} all-to-all(bf16[16,24,1024]{2,1,0:T(8,128)(2,1)} %bitcast.71), channel_id=1, replica_groups=mesh['grp'=2,'seq'=8,'doc'=2] {'seq','doc'}, dimensions={0} | all-to-all | bytes 1572864 | tf_op jit(solution)/shard_map/all_to_all | solution.py:65
  79.6 24.2 %all_to_all.81 = bf16[16,24,1024]{2,1,0:T(8,128)(2,1)} all-to-all(bf16[16,24,1024]{2,1,0:T(8,128)(2,1)S(1)} %bitcast.69), channel_id=1, replica_groups=mesh['grp'=2,'seq'=8,'doc'=2] {'seq','doc'}, dimensions={0} | all-to-all | bytes 1572864 | tf_op jit(solution)/shard_map/all_to_all | solution.py:65
  103.8 24.1 %all_to_all.82 = bf16[16,24,1024]{2,1,0:T(8,128)(2,1)} all-to-all(bf16[16,24,1024]{2,1,0:T(8,128)(2,1)S(1)} %bitcast.70), channel_id=1, replica_groups=mesh['grp'=2,'seq'=8,'doc'=2] {'seq','doc'}, dimensions={0} | all-to-all | bytes 1572864 | tf_op jit(solution)/shard_map/all_to_all | solution.py:65
  127.9 4.2 %all-to-all-start.2 = ((bf16[16,24,1024]{2,1,0:T(8,128)(2,1)}), bf16[16,24,1024]{2,1,0:T(8,128)(2,1)}, u32[]{:S(2)}, u32[]{:S(2)}) async-start(bf16[16,24,1024]{2,1,0:T(8,128)(2,1)} %bitcast.3), calls=%async_computation.2 | async-start | bytes 1572864 | tf_op jit(solution)/shard_map/all_to_all | solution.py:65
  135.8 2.6 gather_fusion
  138.4 12.0 %all-to-all-done.2 = bf16[16,24,1024]{2,1,0:T(8,128)(2,1)} async-done(((bf16[16,24,1024]{2,1,0:T(8,128)(2,1)}), bf16[16,24,1024]{2,1,0:T(8,128)(2,1)}, u32[]{:S(2)}, u32[]{:S(2)}) %all-to-all-start.2) | async-done | bytes 786464 | tf_op jit(solution)/shard_map/all_to_all | solution.py:65
  150.4 2.6 gather_fusion.1
  153.0 3.4 broadcast_select_fusion.4
  156.4 26.2 %all_to_all.83 = bf16[16,24,1024]{2,1,0:T(8,128)(2,1)S(1)} all-to-all(bf16[16,24,1024]{2,1,0:T(8,128)(2,1)S(1)} %get-tuple-element.27), channel_id=1, replica_groups=mesh['grp'=2,'seq'=8,'doc'=2] {'seq','doc'}, dimensions={0} | all-to-all | bytes 1572864 | tf_op jit(solution)/shard_map/all_to_all | solution.py:65
  182.6 3.6 all-to-all-start.5
  190.1 3.8 fusion.13
  193.9 3.7 fusion.9
  197.6 7.1 %all-to-all-done.5 = bf16[16,24,1024]{2,1,0:T(8,128)(2,1)S(1)} async-done(((bf16[16,24,1024]{2,1,0:T(8,128)(2,1)}), bf16[16,24,1024]{2,1,0:T(8,128)(2,1)S(1)}, u32[]{:S(2)}, u32[]{:S(2)}) %all-to-all-start.5) | async-done | bytes 786464 | tf_op jit(solution)/shard_map/all_to_all | solution.py:65
  204.7 5.6 %all-to-all-start.11 = ((bf16[16,24,1024]{2,1,0:T(8,128)(2,1)}), bf16[16,24,1024]{2,1,0:T(8,128)(2,1)S(1)}, u32[]{:S(2)}, u32[]{:S(2)}) async-start(bf16[16,24,1024]{2,1,0:T(8,128)(2,1)} %get-tuple-element.29), calls=%async_computation.11 | async-start | bytes 1572864 | tf_op jit(solution)/shard_map/all_to_all | solution.py:65
  211.6 2.7 fusion.22
  214.3 3.4 fusion.29
  217.7 3.5 fusion.28
  221.2 7.7 %all-to-all-done.11 = bf16[16,24,1024]{2,1,0:T(8,128)(2,1)S(1)} async-done(((bf16[16,24,1024]{2,1,0:T(8,128)(2,1)}), bf16[16,24,1024]{2,1,0:T(8,128)(2,1)S(1)}, u32[]{:S(2)}, u32[]{:S(2)}) %all-to-all-start.11) | async-done | bytes 786464 | tf_op jit(solution)/shard_map/all_to_all | solution.py:65
  228.9 5.6 %all-to-all-start.13 = ((bf16[16,24,1024]{2,1,0:T(8,128)(2,1)}), bf16[16,24,1024]{2,1,0:T(8,128)(2,1)S(1)}, u32[]{:S(2)}, u32[]{:S(2)}) async-start(bf16[16,24,1024]{2,1,0:T(8,128)(2,1)} %get-tuple-element.30), calls=%async_computation.13 | async-start | bytes 1572864 | tf_op jit(solution)/shard_map/all_to_all | solution.py:65
  234.5 9.1 %fusion.1 = (f32[1024]{0:T(1024)S(1)}, f32[1024]{0:T(1024)S(1)}, f32[1024]{0:T(1024)S(1)}, f32[1024]{0:T(1024)S(1)}, f32[1024]{0:T(1024)S(1)}, /*index=5*/f32[1024]{0:T(1024)S(1)}, f32[1024,1024]{1,0:T(8,128)S(1)}) fusion(bf16[1,3,1024,1024]{3,2,1,0:T(8,128)(2,1)} %param.10, f32[1024,1024]{1,0:T(8,128)} %fusion.29, f32[1024,1024]{1,0:T(8,128)} %fusion.28, ...), kind=kOutput, calls=%fused_computation.21 | convolution fusion | flops 827582464 | bytes 22831104 | tf_op jit(solution)/shard_map/dot_general | solution.py:40
  243.7 5.5 %multiply_convert_fusion.5 = (bf16[1024,1024]{1,0:T(8,128)(2,1)S(1)}, bf16[1024,1024]{1,0:T(8,128)(2,1)}) fusion(f32[1024,1024]{1,0:T(8,128)S(1)} %copy-done, f32[1024]{0:T(1024)S(1)} %get-tuple-element.37, bf16[1,3,1024,1024]{3,2,1,0:T(8,128)(2,1)} %param.10, f32[1024]{0:T(1024)S(1)} %get-tuple-element.36, f32[1024,1024]{1,0:T(8,128)S(1)} %get-tuple-element.32), kind=kLoop, calls=%fused_computation.36 | loop fusion | flops 9437184 | bytes 16785408 | tf_op jit(solution)/shard_map/convert_element_type | solution.py:30
  249.1 2.2 fusion.55
  251.3 1.8 all-to-all-done.13
  253.1 5.6 %all-to-all-start.9 = ((bf16[16,24,1024]{2,1,0:T(8,128)(2,1)}), bf16[16,24,1024]{2,1,0:T(8,128)(2,1)}, u32[]{:S(2)}, u32[]{:S(2)}) async-start(bf16[16,24,1024]{2,1,0:T(8,128)(2,1)} %get-tuple-element.26), calls=%async_computation.9 | async-start | bytes 1572864 | tf_op jit(solution)/shard_map/all_to_all | solution.py:65
  259.0 2.8 convolution_negate_fusion
  262.3 4.8 %fusion.4 = (f32[1024]{0:T(1024)S(1)}, f32[1024]{0:T(1024)S(1)}, bf16[1024,1024]{1,0:T(8,128)(2,1)S(1)}, f32[1024,1024]{1,0:T(8,128)}) fusion(f32[1024]{0:T(1024)S(1)} %rsqrt_multiply_fusion.4, f32[1024,1024]{1,0:T(8,128)S(1)} %copy-done.15, bf16[1,3,1024,1024]{3,2,1,0:T(8,128)(2,1)} %param.10, bf16[384,1024]{1,0:T(8,128)(2,1)S(1)} %bitcast.73, ...), kind=kOutput, calls=%fused_computation.24 | convolution fusion | flops 818149376 | bytes 16527360 | tf_op jit(solution)/shard_map/dot_general | solution.py:46
  268.4 3.8 fusion.3
  272.2 3.8 fusion.5
  277.4 5.6 %all-to-all-start.1 = ((bf16[16,24,1024]{2,1,0:T(8,128)(2,1)}), bf16[16,24,1024]{2,1,0:T(8,128)(2,1)S(1)}, u32[]{:S(2)}, u32[]{:S(2)}) async-start(bf16[16,24,1024]{2,1,0:T(8,128)(2,1)} %get-tuple-element.31), calls=%async_computation.1 | async-start | bytes 1572864 | tf_op jit(solution)/shard_map/all_to_all | solution.py:65
  283.0 4.6 %fusion.6 = f32[384,1024]{1,0:T(8,128)} fusion(bf16[384,1024]{1,0:T(8,128)(2,1)} %bitcast.15, f32[1024,1024]{1,0:T(8,128)} %get-tuple-element.35, bf16[1024,1024]{1,0:T(8,128)(2,1)S(1)} %get-tuple-element.16, f32[1024]{0:T(1024)S(1)} %rsqrt_multiply_fusion.2), kind=kOutput, calls=%fused_computation.38 | convolution fusion | flops 809500672 | bytes 8654848 | tf_op jit(solution)/shard_map/dot_general | solution.py:18
  287.6 8.3 %select_convert_fusion = bf16[384,1024]{1,0:T(8,128)(2,1)} fusion(f32[1024,1024]{1,0:T(8,128)} %get-tuple-element.34, bf16[1024,1024]{1,0:T(8,128)(2,1)} %get-tuple-element.17, f32[1024]{0:T(1024)S(1)} %rsqrt_multiply_fusion, pred[]{:T(512)} %bitcast.13, f32[384,1024]{1,0:T(8,128)} %fusion.6, bf16[384,1024]{1,0:T(8,128)(2,1)} %bitcast.15, ...), kind=kOutput, calls=%fused_computation.54 | convolution fusion | flops 1623195648 | bytes 15736833 | tf_op jit(solution)/shard_map/dot_general | solution.py:21
  295.9 5.6 %all-to-all-done.1 = bf16[16,24,1024]{2,1,0:T(8,128)(2,1)S(1)} async-done(((bf16[16,24,1024]{2,1,0:T(8,128)(2,1)}), bf16[16,24,1024]{2,1,0:T(8,128)(2,1)S(1)}, u32[]{:S(2)}, u32[]{:S(2)}) %all-to-all-start.1) | async-done | bytes 786464 | tf_op jit(solution)/shard_map/all_to_all | solution.py:65
  302.4 5.6 %all-to-all-start.14 = ((bf16[16,24,1024]{2,1,0:T(8,128)(2,1)}), bf16[16,24,1024]{2,1,0:T(8,128)(2,1)S(1)}, u32[]{:S(2)}, u32[]{:S(2)}) async-start(bf16[16,24,1024]{2,1,0:T(8,128)(2,1)} %bitcast.82), calls=%async_computation.14 | async-start | bytes 1572864 | tf_op jit(solution)/shard_map/all_to_all | solution.py:75
  308.1 3.3 fusion.53
  311.3 5.7 %convolution_convert_fusion = bf16[384,1024]{1,0:T(8,128)(2,1)} fusion(bf16[1024,1024]{1,0:T(8,128)(2,1)} %get-tuple-element.17, f32[384,1024]{1,0:T(8,128)} %fusion.53, bf16[384,1024]{1,0:T(8,128)(2,1)} %bitcast.81, bf16[1024,1024]{1,0:T(8,128)(2,1)} %copy-done.13), kind=kOutput, calls=%fused_computation.70 | convolution fusion | flops 1613365248 | bytes 7340032 | tf_op jit(solution)/shard_map/dot_general | solution.py:21
  317.0 9.6 %all-to-all-done.14 = bf16[16,24,1024]{2,1,0:T(8,128)(2,1)S(1)} async-done(((bf16[16,24,1024]{2,1,0:T(8,128)(2,1)}), bf16[16,24,1024]{2,1,0:T(8,128)(2,1)S(1)}, u32[]{:S(2)}, u32[]{:S(2)}) %all-to-all-start.14) | async-done | bytes 786464 | tf_op jit(solution)/shard_map/all_to_all | solution.py:75
  326.6 5.6 %all-to-all-start.6 = ((bf16[16,24,1024]{2,1,0:T(8,128)(2,1)}), bf16[16,24,1024]{2,1,0:T(8,128)(2,1)S(1)}, u32[]{:S(2)}, u32[]{:S(2)}) async-start(bf16[16,24,1024]{2,1,0:T(8,128)(2,1)} %bitcast.11), calls=%async_computation.6 | async-start | bytes 1572864 | tf_op jit(solution)/shard_map/all_to_all | solution.py:71
  334.1 16.8 %all-to-all-done.6 = bf16[16,24,1024]{2,1,0:T(8,128)(2,1)S(1)} async-done(((bf16[16,24,1024]{2,1,0:T(8,128)(2,1)}), bf16[16,24,1024]{2,1,0:T(8,128)(2,1)S(1)}, u32[]{:S(2)}, u32[]{:S(2)}) %all-to-all-start.6) | async-done | bytes 786464 | tf_op jit(solution)/shard_map/all_to_all | solution.py:71
  350.8 5.6 %all-to-all-start.15 = ((bf16[16,24,1024]{2,1,0:T(8,128)(2,1)}), bf16[16,24,1024]{2,1,0:T(8,128)(2,1)S(1)}, u32[]{:S(2)}, u32[]{:S(2)}) async-start(bf16[16,24,1024]{2,1,0:T(8,128)(2,1)} %broadcast_select_fusion), calls=%async_computation.15 | async-start | bytes 1572864 | tf_op jit(solution)/shard_map/all_to_all | solution.py:75
  358.1 16.9 %all-to-all-done.15 = bf16[16,24,1024]{2,1,0:T(8,128)(2,1)S(1)} async-done(((bf16[16,24,1024]{2,1,0:T(8,128)(2,1)}), bf16[16,24,1024]{2,1,0:T(8,128)(2,1)S(1)}, u32[]{:S(2)}, u32[]{:S(2)}) %all-to-all-start.15) | async-done | bytes 786464 | tf_op jit(solution)/shard_map/all_to_all | solution.py:75
  375.0 5.6 %all-to-all-start.7 = ((bf16[16,24,1024]{2,1,0:T(8,128)(2,1)}), bf16[16,24,1024]{2,1,0:T(8,128)(2,1)S(1)}, u32[]{:S(2)}, u32[]{:S(2)}) async-start(bf16[16,24,1024]{2,1,0:T(8,128)(2,1)} %broadcast_select_fusion.1), calls=%async_computation.7 | async-start | bytes 1572864 | tf_op jit(solution)/shard_map/all_to_all | solution.py:71
  380.6 18.6 %all-to-all-done.7 = bf16[16,24,1024]{2,1,0:T(8,128)(2,1)S(1)} async-done(((bf16[16,24,1024]{2,1,0:T(8,128)(2,1)}), bf16[16,24,1024]{2,1,0:T(8,128)(2,1)S(1)}, u32[]{:S(2)}, u32[]{:S(2)}) %all-to-all-start.7) | async-done | bytes 786464 | tf_op jit(solution)/shard_map/all_to_all | solution.py:71
  (74 shorter events, 17.2 us)
Async XLA Ops:
  0.6 9.8 %copy-start.3 = (bf16[2,1,384,1024]{3,2,1,0:T(8,128)(2,1)S(1)}, bf16[2,1,384,1024]{3,2,1,0:T(8,128)(2,1)}, u32[]{:S(2)}) copy-start(bf16[2,1,384,1024]{3,2,1,0:T(8,128)(2,1)} %param.13) | copy-start | bytes 4718596
  3.1 25.9 %all-to-all-start.4 = ((bf16[16,24,1024]{2,1,0:T(8,128)(2,1)}), bf16[16,24,1024]{2,1,0:T(8,128)(2,1)S(1)}, u32[]{:S(2)}, u32[]{:S(2)}) async-start(bf16[16,24,1024]{2,1,0:T(8,128)(2,1)} %bitcast.6), calls=%async_computation.4 | async-start | bytes 1572864 | tf_op jit(solution)/shard_map/all_to_all | solution.py:65
  29.0 24.2 %all-to-all-start.8 = ((bf16[16,24,1024]{2,1,0:T(8,128)(2,1)}), bf16[16,24,1024]{2,1,0:T(8,128)(2,1)S(1)}, u32[]{:S(2)}, u32[]{:S(2)}) async-start(bf16[16,24,1024]{2,1,0:T(8,128)(2,1)} %bitcast.14), calls=%async_computation.8 | async-start | bytes 1572864 | tf_op jit(solution)/shard_map/all_to_all | solution.py:65
  53.2 50.6 %copy-start.1 = (bf16[1,1,384,1024]{3,2,1,0:T(8,128)(2,1)S(1)}, bf16[1,1,384,1024]{3,2,1,0:T(8,128)(2,1)}, u32[]{:S(2)}) copy-start(bf16[1,1,384,1024]{3,2,1,0:T(8,128)(2,1)} %get-tuple-element.19) | copy-start | bytes 2359300
  79.6 52.5 %copy-start.12 = (s32[16]{0:T(128)S(1)}, s32[16]{0:T(128)}, u32[]{:S(2)}) copy-start(s32[16]{0:T(128)} %param.16) | copy-start | bytes 196
  127.9 22.5 %all-to-all-start.2 = ((bf16[16,24,1024]{2,1,0:T(8,128)(2,1)}), bf16[16,24,1024]{2,1,0:T(8,128)(2,1)}, u32[]{:S(2)}, u32[]{:S(2)}) async-start(bf16[16,24,1024]{2,1,0:T(8,128)(2,1)} %bitcast.3), calls=%async_computation.2 | async-start | bytes 1572864 | tf_op jit(solution)/shard_map/all_to_all | solution.py:65
  156.4 32.2 %copy-start.9 = (f32[2,16,384]{2,1,0:T(8,128)S(1)}, f32[2,16,384]{2,1,0:T(8,128)}, u32[]{:S(2)}) copy-start(f32[2,16,384]{2,1,0:T(8,128)} %param.14) | copy-start | bytes 147460
  156.4 32.4 %copy-start.10 = (s32[16]{0:T(128)S(1)}, s32[16]{0:T(128)}, u32[]{:S(2)}) copy-start(s32[16]{0:T(128)} %param.15) | copy-start | bytes 196
  182.6 22.1 %all-to-all-start.5 = ((bf16[16,24,1024]{2,1,0:T(8,128)(2,1)}), bf16[16,24,1024]{2,1,0:T(8,128)(2,1)S(1)}, u32[]{:S(2)}, u32[]{:S(2)}) async-start(bf16[16,24,1024]{2,1,0:T(8,128)(2,1)} %get-tuple-element.28), calls=%async_computation.5 | async-start | bytes 1572864 | tf_op jit(solution)/shard_map/all_to_all | solution.py:65
  204.7 24.2 %all-to-all-start.11 = ((bf16[16,24,1024]{2,1,0:T(8,128)(2,1)}), bf16[16,24,1024]{2,1,0:T(8,128)(2,1)S(1)}, u32[]{:S(2)}, u32[]{:S(2)}) async-start(bf16[16,24,1024]{2,1,0:T(8,128)(2,1)} %get-tuple-element.29), calls=%async_computation.11 | async-start | bytes 1572864 | tf_op jit(solution)/shard_map/all_to_all | solution.py:65
  211.6 2.7 copy-start.16
  214.3 3.4 copy-start.17
  217.7 16.8 %copy-start.8 = (bf16[384,1024]{1,0:T(8,128)(2,1)S(1)}, bf16[384,1024]{1,0:T(8,128)(2,1)}, u32[]{:S(2)}) copy-start(bf16[384,1024]{1,0:T(8,128)(2,1)} %fusion.19) | copy-start | bytes 2359300
  228.9 14.7 %copy-start.4 = (bf16[16,24,1024]{2,1,0:T(8,128)(2,1)}, bf16[16,24,1024]{2,1,0:T(8,128)(2,1)S(1)}, u32[]{:S(2)}) copy-start(bf16[16,24,1024]{2,1,0:T(8,128)(2,1)S(1)} %all-to-all-done.11) | copy-start | bytes 2359300
  228.9 24.2 %all-to-all-start.13 = ((bf16[16,24,1024]{2,1,0:T(8,128)(2,1)}), bf16[16,24,1024]{2,1,0:T(8,128)(2,1)S(1)}, u32[]{:S(2)}, u32[]{:S(2)}) async-start(bf16[16,24,1024]{2,1,0:T(8,128)(2,1)} %get-tuple-element.30), calls=%async_computation.13 | async-start | bytes 1572864 | tf_op jit(solution)/shard_map/all_to_all | solution.py:65
  234.5 9.1 %copy-start = (f32[1024,1024]{1,0:T(8,128)S(1)}, f32[1024,1024]{1,0:T(8,128)}, u32[]{:S(2)}) copy-start(f32[1024,1024]{1,0:T(8,128)} %fusion.28) | copy-start | bytes 12582916
  243.6 5.5 %copy-start.5 = (bf16[16,24,1024]{2,1,0:T(8,128)(2,1)S(1)}, bf16[16,24,1024]{2,1,0:T(8,128)(2,1)}, u32[]{:S(2)}) copy-start(bf16[16,24,1024]{2,1,0:T(8,128)(2,1)} %copy-done.4) | copy-start | bytes 2359300
  253.1 24.3 %all-to-all-start.9 = ((bf16[16,24,1024]{2,1,0:T(8,128)(2,1)}), bf16[16,24,1024]{2,1,0:T(8,128)(2,1)}, u32[]{:S(2)}, u32[]{:S(2)}) async-start(bf16[16,24,1024]{2,1,0:T(8,128)(2,1)} %get-tuple-element.26), calls=%async_computation.9 | async-start | bytes 1572864 | tf_op jit(solution)/shard_map/all_to_all | solution.py:65
  258.7 3.0 copy-start.15
  258.9 2.8 copy-start.6
  258.9 3.4 copy-start.14
  267.1 1.3 copy-start.13
  268.4 3.8 copy-start.2
  277.4 24.2 %all-to-all-start.1 = ((bf16[16,24,1024]{2,1,0:T(8,128)(2,1)}), bf16[16,24,1024]{2,1,0:T(8,128)(2,1)S(1)}, u32[]{:S(2)}, u32[]{:S(2)}) async-start(bf16[16,24,1024]{2,1,0:T(8,128)(2,1)} %get-tuple-element.31), calls=%async_computation.1 | async-start | bytes 1572864 | tf_op jit(solution)/shard_map/all_to_all | solution.py:65
  301.6 0.9 copy-start.7
  302.4 24.2 %all-to-all-start.14 = ((bf16[16,24,1024]{2,1,0:T(8,128)(2,1)}), bf16[16,24,1024]{2,1,0:T(8,128)(2,1)S(1)}, u32[]{:S(2)}, u32[]{:S(2)}) async-start(bf16[16,24,1024]{2,1,0:T(8,128)(2,1)} %bitcast.82), calls=%async_computation.14 | async-start | bytes 1572864 | tf_op jit(solution)/shard_map/all_to_all | solution.py:75
  311.3 20.9 %copy-start.11 = (s32[16]{0:T(128)S(1)}, s32[16]{0:T(128)}, u32[]{:S(2)}) copy-start(s32[16]{0:T(128)} %param.17) | copy-start | bytes 196
  326.6 24.2 %all-to-all-start.6 = ((bf16[16,24,1024]{2,1,0:T(8,128)(2,1)}), bf16[16,24,1024]{2,1,0:T(8,128)(2,1)S(1)}, u32[]{:S(2)}, u32[]{:S(2)}) async-start(bf16[16,24,1024]{2,1,0:T(8,128)(2,1)} %bitcast.11), calls=%async_computation.6 | async-start | bytes 1572864 | tf_op jit(solution)/shard_map/all_to_all | solution.py:71
  350.8 24.2 %all-to-all-start.15 = ((bf16[16,24,1024]{2,1,0:T(8,128)(2,1)}), bf16[16,24,1024]{2,1,0:T(8,128)(2,1)S(1)}, u32[]{:S(2)}, u32[]{:S(2)}) async-start(bf16[16,24,1024]{2,1,0:T(8,128)(2,1)} %broadcast_select_fusion), calls=%async_computation.15 | async-start | bytes 1572864 | tf_op jit(solution)/shard_map/all_to_all | solution.py:75
  375.0 24.2 %all-to-all-start.7 = ((bf16[16,24,1024]{2,1,0:T(8,128)(2,1)}), bf16[16,24,1024]{2,1,0:T(8,128)(2,1)S(1)}, u32[]{:S(2)}, u32[]{:S(2)}) async-start(bf16[16,24,1024]{2,1,0:T(8,128)(2,1)} %broadcast_select_fusion.1), calls=%async_computation.7 | async-start | bytes 1572864 | tf_op jit(solution)/shard_map/all_to_all | solution.py:71
where the time goes:
time: 403 us; the launch traced here: 401 us
  waiting for transfers between devices  131 us (33%)
  blocking collectives  101 us (25%)
  matrix products  66.2 us (16%)
  starting transfers between devices  65.8 us (16%)
  local copies, waits for them, and re-layouts  21.4 us (5%)
  other arithmetic  12.8 us (3%)
    all_to_all x4, blocking collectives, move_rows(): lax.all_to_all(shortened(items), ('seq', 'doc'), split_axis=0, concat_axi...  101 us
    all_to_all x8, waiting for transfers between devices, move_rows(): lax.all_to_all(shortened(items), ('seq', 'doc'), split_axis=0, concat_axi...  68.7 us
    all_to_all x8, starting transfers between devices, move_rows(): lax.all_to_all(shortened(items), ('seq', 'doc'), split_axis=0, concat_axi...  43.3 us
    all_to_all x2, waiting for transfers between devices, send_back(): lax.all_to_all(pieces, ('seq', 'doc'), split_axis=0, concat_axis=0, tiled...  35.3 us
    all_to_all x2, waiting for transfers between devices, move_result(): lax.all_to_all(pieces, ('seq', 'doc'), split_axis=0, concat_axis=0, tiled...  26.5 us
    dot_general x2, matrix products, swiglu_apply(): return jnp.dot(hidden, weights[2], preferred_element_type=jnp.float32)  14 us
    dot_general x2, matrix products, fast_update(): jnp.dot(hidden.T, scaled_values, preferred_element_type=jnp.float32)  12.9 us
    all_to_all x2, starting transfers between devices, send_back(): lax.all_to_all(pieces, ('seq', 'doc'), split_axis=0, concat_axis=0, tiled...  11.3 us
  transfers between devices with their start and end apart: 12, of which 12 were waited for; matrix products, arithmetic and copies ran while one was open for 22% of the time, Pallas kernels for 0%

commit v1 on v0

v1 whole, which is shorter than its diff:
```python
import functools

import jax
import jax.numpy as jnp
from jax import lax
from jax.experimental import pallas as pl
from jax.experimental.pallas import tpu as pltpu
from jax.sharding import Mesh, PartitionSpec as P

EPSILON = 1e-06
LEVEL = ("x", "core")
GROUP = ("z", "x", "core")
EXTRA = 2


def swiglu_apply(weights, inputs):
    gate_pre = jnp.dot(inputs, weights[0], preferred_element_type=jnp.float32)
    upward = jnp.dot(inputs, weights[1], preferred_element_type=jnp.float32)
    hidden = (jax.nn.silu(gate_pre) * upward).astype(jnp.bfloat16)
    return jnp.dot(hidden, weights[2], preferred_element_type=jnp.float32)


def renorm(weight, gradient):
    before = weight.astype(jnp.float32)
    stepped = before - gradient
    factor = jnp.sqrt(jnp.mean(before * before, axis=0) + EPSILON) / jnp.sqrt(
        jnp.mean(stepped * stepped, axis=0) + EPSILON
    )
    return (stepped * factor[None, :]).astype(jnp.bfloat16)


def fast_update(weights, keys_rows, values_rows, rate_rows):
    gate_pre = jnp.dot(keys_rows, weights[0], preferred_element_type=jnp.float32)
    upward = jnp.dot(keys_rows, weights[1], preferred_element_type=jnp.float32)
    sigmoid_gate = jax.nn.sigmoid(gate_pre)
    active = gate_pre * sigmoid_gate
    hidden = (active * upward).astype(jnp.bfloat16)
    scaled_values = (rate_rows[:, None] * values_rows.astype(jnp.float32)).astype(jnp.bfloat16)
    grad_down = -jnp.dot(hidden.T, scaled_values, preferred_element_type=jnp.float32)
    grad_hidden = -jnp.dot(scaled_values, weights[2].T, preferred_element_type=jnp.float32)
    slope = sigmoid_gate * (1.0 + gate_pre * (1.0 - sigmoid_gate))
    grad_gate = (grad_hidden * upward * slope).astype(jnp.bfloat16)
    grad_up = (grad_hidden * active).astype(jnp.bfloat16)
    grad_first = jnp.dot(keys_rows.T, grad_gate, preferred_element_type=jnp.float32)
    grad_third = jnp.dot(keys_rows.T, grad_up, preferred_element_type=jnp.float32)
    return (
        renorm(weights[0], grad_first),
        renorm(weights[1], grad_third),
        renorm(weights[2], grad_down),
    )


def inverse_of(permuted):
    count = permuted.shape[0]
    labels = jnp.arange(count, dtype=jnp.int32)
    return jnp.sum(jnp.where(permuted[None, :] == labels[:, None], labels[None, :], 0), axis=1)


def schedule_kernel(levels, lanes, horizon, items_ref, sends_ref, finals_ref):
    problems, _, count = items_ref.shape
    rows = 2 * levels
    shape = (rows, count)
    row = lax.broadcasted_iota(jnp.int32, shape, 0)
    item = lax.broadcasted_iota(jnp.int32, shape, 1)
    right = row < levels
    level = jnp.where(right, row, row - levels)
    heading = jnp.where(right, 1, -1)
    column = lax.broadcasted_iota(jnp.int32, (rows, 128), 1)
    for problem in range(problems):
        source = jnp.broadcast_to(items_ref[problem, 0:1, :], shape)
        target = jnp.broadcast_to(items_ref[problem, 1:2, :], shape)
        lane = jnp.broadcast_to(items_ref[problem, 2:3, :], shape)
        live = jnp.broadcast_to(items_ref[problem, 3:4, :], shape)
        present = jnp.where(level == source, live, 0) * jnp.where((target - source) * heading > 0, 1, 0)
        index = lane
        following = jnp.where(right, level + 1, level - 1)
        urgency = jnp.abs(target - level) * count + item + 1
        final = items_ref[problem, 2:3, :]
        sends = jnp.zeros((rows, 128), jnp.int32)
        for step in range(horizon):
            key = jnp.where(present > 0, urgency, 0)
            best = jnp.max(key, axis=1, keepdims=True)
            chosen = jnp.where((key == best) & (present > 0), 1, 0)
            sent = jnp.sum(chosen * index, axis=1, keepdims=True)
            busy = jnp.sum(chosen, axis=1, keepdims=True)
            sends = jnp.where(column == step, sent, sends)
            sends = jnp.where((column == 127) & (busy > 0), step + 1, sends)
            arrived = jnp.where(target == following, chosen, 0)
            mark = jnp.where(right, lanes + step, lanes + horizon + step)
            landed = jnp.max(arrived * mark, axis=0, keepdims=True)
            final = jnp.where(landed > 0, landed, final)
            moving = chosen - arrived
            moved = pltpu.roll(jnp.where(right, moving, 0), 1, 0)
            moved += pltpu.roll(jnp.where(right, 0, moving), rows - 1, 0)
            present = present - chosen + moved
            index = jnp.where(moved > 0, lanes + step, index)
        left = jnp.max(present, axis=1, keepdims=True)
        sends = jnp.where((column == 127) & (left > 0), horizon + 1, sends)
        sends_ref[problem] = sends
        finals_ref[problem] = final


def plan_routes(levels, lanes, horizon, my_level, sources, targets, live):
    problems, count = targets.shape
    sources = jnp.broadcast_to(sources, targets.shape)
    items = jnp.stack([sources // lanes, targets // lanes, sources % lanes, live], axis=1)
    sends, finals = pl.pallas_call(
        functools.partial(schedule_kernel, levels, lanes, horizon),
        out_shape=(
            jax.ShapeDtypeStruct((problems, 2 * levels, 128), jnp.int32),
            jax.ShapeDtypeStruct((problems, 1, count), jnp.int32),
        ),
        name="plan_routes",
    )(items)
    steps = jnp.max(sends[:, :, 127], axis=1)
    to_right = lax.dynamic_index_in_dim(sends, my_level, 1, keepdims=False)[:, :horizon]
    to_left = lax.dynamic_index_in_dim(sends, levels + my_level, 1, keepdims=False)[:, :horizon]
    kept_by = my_level * lanes + jnp.arange(lanes, dtype=jnp.int32)
    kept = jnp.sum(jnp.where(targets[:, None, :] == kept_by[None, :, None], finals, 0), axis=2)
    return to_right, to_left, kept, steps


def pick_kernel(layout, sizes, *refs):
    index_ref = refs[0]
    ins = refs[1 : 1 + len(sizes)]
    outs = refs[1 + len(sizes) : -1]
    sems = refs[-1]
    candidates = []
    for ref, size in zip(ins, sizes):
        candidates.extend([ref] if size is None else [ref.at[lane] for lane in range(size)])
    slots = []
    for number, (slot_count, allowed) in enumerate(layout):
        for slot in range(max(slot_count, 1)):
            place = outs[number] if slot_count == 0 else outs[number].at[slot]
            slots.append((place, allowed))
    for slot, (place, allowed) in enumerate(slots):
        wanted = index_ref[slot]
        for value, position in allowed:

            @pl.when(wanted == value)
            def _():
                pltpu.make_async_copy(candidates[position], place, sems.at[slot]).start()

    for slot, (place, allowed) in enumerate(slots):
        pltpu.make_async_copy(candidates[allowed[0][1]], place, sems.at[slot]).wait()


def pick(indices, own, arrays, layout):
    item = own.shape[1:]
    sizes = [own.shape[0]] + [None] * len(arrays)
    total = sum(max(slot_count, 1) for slot_count, _ in layout)
    return pl.pallas_call(
        functools.partial(pick_kernel, layout, sizes),
        out_shape=tuple(
            jax.ShapeDtypeStruct(((slot_count,) if slot_count else ()) + item, own.dtype) for slot_count, _ in layout
        ),
        in_specs=[pl.BlockSpec(memory_space=pltpu.SMEM)] + [pl.BlockSpec(memory_space=pl.ANY)] * (1 + len(arrays)),
        out_specs=tuple(pl.BlockSpec(memory_space=pl.ANY) for _ in layout),
        scratch_shapes=[pltpu.SemaphoreType.DMA((total,))],
        name="pick_items",
    )(indices, own, *arrays)


def step_along(own, rights, lefts, step, to_right, to_left, levels):
    lanes = own.shape[0]
    count = len(rights)
    from_own = [(lane, lane) for lane in range(lanes)]
    layout = (
        (0, from_own + [(lanes + t, lanes + t) for t in range(count)]),
        (0, from_own + [(lanes + t, lanes + count + t) for t in range(count)]),
    )
    indices = jnp.stack([to_right[step], to_left[step]])
    out_right, out_left = pick(indices, own, rights + lefts, layout)
    in_right = lax.ppermute(out_right, "z", [(i, i + 1) for i in range(levels - 1)])
    in_left = lax.ppermute(out_left, "z", [(i + 1, i) for i in range(levels - 1)])
    return rights + [in_right], lefts + [in_left]


def settle(own, rights, lefts, kept, horizon):
    lanes = own.shape[0]
    count = len(rights)
    allowed = [(lane, lane) for lane in range(lanes)]
    allowed += [(lanes + t, lanes + t) for t in range(count)]
    allowed += [(lanes + horizon + t, lanes + count + t) for t in range(count)]
    return pick(kept, own, rights + lefts, ((lanes, allowed),))[0]


def route(own, plan, needed, steps, horizon, levels):
    to_right, to_left, kept, origin = plan
    rights, lefts = [], []
    for step in range(steps):
        rights, lefts = step_along(own, rights, lefts, step, to_right, to_left, levels)

    def enough(own, rights, lefts):
        return settle(own, rights, lefts, kept, horizon)

    def more(own, rights, lefts):
        for step in range(steps, horizon):
            rights, lefts = step_along(own, rights, lefts, step, to_right, to_left, levels)
        return settle(own, rights, lefts, kept, horizon)

    def gathered(own, rights, lefts):
        everything = lax.all_gather(own, "z", axis=0, tiled=True)
        return jnp.take(everything, origin, axis=0)

    branch = jnp.where(needed <= steps, 0, jnp.where(needed <= horizon, 1, 2))
    return lax.switch(branch, (enough, more, gathered), own, rights, lefts)


def exchange(pieces, axes):
    return lax.all_to_all(pieces, axes, split_axis=0, concat_axis=0, tiled=True)


def body(state, keys, values, queries, rates, remaining, first_owner, migration):
    levels = lax.axis_size("z")
    lanes = lax.axis_size(LEVEL)
    devices = levels * lanes
    myself = lax.axis_index(GROUP)
    my_level = lax.axis_index("z")
    doc_first = inverse_of(first_owner)
    source_of = inverse_of(migration)
    doc_here = doc_first[myself]
    block_rows, width = keys.shape[2], keys.shape[3]
    part = block_rows // lanes
    weights = (state[0, 0], state[0, 1], state[0, 2])

    steps = (devices // 4 + 1, devices // 8 + 2)
    horizon = steps[0] + EXTRA
    labels = jnp.arange(devices, dtype=jnp.int32)
    targets = jnp.stack([first_owner, first_owner])
    live = jnp.stack([jnp.ones_like(remaining), (remaining >= 2).astype(jnp.int32)])
    to_right, to_left, kept, needed = plan_routes(levels, lanes, horizon, my_level, labels, targets, live)
    origin = lax.dynamic_slice_in_dim(doc_first, my_level * lanes, lanes, 0)

    def deal(blocks):
        split = [block.reshape(lanes, 1, part, width) for block in blocks]
        return exchange(jnp.concatenate(split, axis=1), LEVEL)

    def collect(settled):
        return exchange(settled, LEVEL)

    def bring(section, blocks):
        plan = (to_right[section], to_left[section], kept[section], origin)
        return collect(route(deal(blocks), plan, needed[section], steps[section], horizon, levels))

    def run_round(section, weights_in):
        pair = bring(section, (keys[section, 0], values[section, 0]))
        asked = bring(section, (queries[section, 0],))
        rate_here = lax.dynamic_index_in_dim(rates[section], doc_here, 0, keepdims=False)
        keys_here = pair[:, 0].reshape(block_rows, width)
        values_here = pair[:, 1].reshape(block_rows, width)
        updated = fast_update(weights_in, keys_here, values_here, rate_here)
        return updated, swiglu_apply(updated, asked.reshape(block_rows, width))

    updated, result_one = run_round(0, weights)
    outgoing = result_one.astype(jnp.bfloat16).reshape(devices, block_rows // devices, width)
    dealt_out = exchange(outgoing, GROUP)
    returned = exchange(jnp.take(dealt_out, first_owner, axis=0), GROUP)
    round_one = returned.reshape(1, block_rows, width)

    _, result_two = run_round(1, updated)
    is_live = remaining[doc_here] >= 2
    masked = jnp.where(is_live, result_two, jnp.float32(0.0)).astype(jnp.bfloat16)
    dealt = exchange(masked.reshape(devices, block_rows // devices, width), GROUP)
    regrouped = exchange(jnp.take(dealt, source_of, axis=0), GROUP)
    round_two = regrouped.reshape(1, block_rows, width)
    return (round_one, round_two)


def solution(mesh):
    groups, along, cores = (mesh.shape[name] for name in ("grp", "seq", "doc"))
    wide = max(d for d in range(1, along + 1) if along % d == 0 and d**3 <= along)
    fine = Mesh(mesh.devices.reshape(groups, along // wide, wide, cores), ("grp",) + GROUP)
    everywhere = ("grp",) + GROUP
    return jax.shard_map(
        body,
        mesh=fine,
        in_specs=(
            P(everywhere, None, None, None),
            P(None, everywhere, None, None),
            P(None, everywhere, None, None),
            P(None, everywhere, None, None),
            P(None, "grp", None),
            P("grp"),
            P("grp"),
            P("grp"),
        ),
        out_specs=(P(everywhere, None, None), P(everywhere, None, None)),
        check_vma=False,
    )
```

time: 403 us -> 691 us (1.71); the launches traced: 401 us -> 703 us
  Pallas kernels: 0 us -> 219 us
  starting transfers between devices: 65.8 us -> 262 us
  blocking collectives: 101 us -> 0 us
  waiting for transfers between devices: 131 us -> 89.6 us
  other arithmetic: 12.8 us -> 29.8 us
  between operations: 3.47 us -> 20.3 us
    pallas_call x0 -> x23, Pallas kernels: none -> 219 us  [the longest x22 216 us: pick(): pl.pallas_call(functools.partial(pick_kernel, layout, sizes), out_shape=t...]
    ppermute x0 -> x36, starting transfers between devices: none -> 182 us  [the longest x18 159 us: step_along(): lax.ppermute(out_right, 'z', [(i, i + 1) for i in range(levels - 1)])]
    all_to_all x4 -> x0, blocking collectives: 101 us -> none  [move_rows(): lax.all_to_all(shortened(items), ('seq', 'doc'), split_axis=0, concat_axi...]
    all_to_all x12, waiting for transfers between devices: 131 us -> 72.5 us  [exchange(): return lax.all_to_all(pieces, axes, split_axis=0, concat_axis=0, tiled=True)]
    another operation x0 -> x13, other arithmetic: none -> 18 us  [the longest x9 16.9 us: step_along(): indices = jnp.stack([to_right[step], to_left[step]])]
    ppermute x0 -> x36, waiting for transfers between devices: none -> 17.1 us  [the longest x18 8.56 us: step_along(): lax.ppermute(out_right, 'z', [(i, i + 1) for i in range(levels - 1)])]
    all_to_all x12, starting transfers between devices: 65.8 us -> 79.8 us  [exchange(): return lax.all_to_all(pieces, axes, split_axis=0, concat_axis=0, tiled=True)]
    gather x8 -> x2, local copies, waits for them, and re-layouts: 9.94 us -> 1.2 us  [the longest x1 0.6 us: body(): returned = exchange(jnp.take(dealt_out, first_owner, axis=0), GROUP)]
  transfers between devices with their start and end apart: 12 -> 48, of which waited for: 12 -> 11; matrix products, arithmetic and copies ran while one was open for 22% -> 15% of each run, Pallas kernels for 0% -> 31%
where the time goes in v1:
time: 691 us; the launch traced here: 703 us
  starting transfers between devices  262 us (38%)
  Pallas kernels  219 us (32%)
  waiting for transfers between devices  89.6 us (13%)
  matrix products  59.4 us (9%)
  other arithmetic  29.8 us (4%)
  local copies, waits for them, and re-layouts  22.4 us (3%)
  between operations  20.3 us (3%)
    pallas_call x22, Pallas kernels, pick(): pl.pallas_call(functools.partial(pick_kernel, layout, sizes), out_shape=t...  216 us
    ppermute x18, starting transfers between devices, step_along(): lax.ppermute(out_right, 'z', [(i, i + 1) for i in range(levels - 1)])  159 us
    all_to_all x12, starting transfers between devices, exchange(): return lax.all_to_all(pieces, axes, split_axis=0, concat_axis=0, tiled=True)  79.8 us
    all_to_all x12, waiting for transfers between devices, exchange(): return lax.all_to_all(pieces, axes, split_axis=0, concat_axis=0, tiled=True)  72.5 us
    ppermute x18, starting transfers between devices, step_along(): lax.ppermute(out_left, 'z', [(i + 1, i) for i in range(levels - 1)])  23.1 us
    another operation x9, other arithmetic, step_along(): indices = jnp.stack([to_right[step], to_left[step]])  16.9 us
    dot_general x2, matrix products, swiglu_apply(): return jnp.dot(hidden, weights[2], preferred_element_type=jnp.float32)  13.9 us
  transfers between devices with their start and end apart: 48, of which 11 were waited for; matrix products, arithmetic and copies ran while one was open for 15% of the time, Pallas kernels for 31%

profile of v1, /device:TPU:1, one launch (start us, length us, event | category | flops | bytes accessed | tf_op | source)
XLA Modules:
  0.0 702.7 jit_solution(8837138230269067003)
XLA Ops:
  10.5 4.4 all-to-all-start.8
  20.9 12.9 %all-to-all-done.8.refs_1_ = bf16[4,2,96,1024]{3,2,1,0:T(8,128)(2,1)S(1)} async-done(((bf16[4,2,96,1024]{3,2,1,0:T(8,128)(2,1)}), bf16[4,2,96,1024]{3,2,1,0:T(8,128)(2,1)S(1)}, u32[]{:S(2)}, u32[]{:S(2)}) %all-to-all-start.8) | async-done | bytes 1572896 | tf_op jit(solution)/shard_map/all_to_all | solution.py:211
  33.8 4.7 all-to-all-start.2
  71.1 5.6 all-to-all-start
  80.7 4.3 collective-permute-start.30
  87.9 16.9 %collective-permute-start.52 = (bf16[2,96,1024]{2,1,0:T(8,128)(2,1)}, bf16[2,96,1024]{2,1,0:T(8,128)(2,1)}, u32[]{:S(2)}, u32[]{:S(2)}) collective-permute-start(bf16[2,96,1024]{2,1,0:T(8,128)(2,1)} %get-tuple-element.425), channel_id=1, source_target_pairs={{0,4},{4,8},{8,12},{1,5},{5,9},{9,13},{2,6},{6,10},{10,14},{3,7},{... | collective-permute-start | bytes 1179656 | tf_op jit(solution)/shard_map/ppermute | solution.py:174
  108.4 16.9 %collective-permute-start.32 = (bf16[2,96,1024]{2,1,0:T(8,128)(2,1)}, bf16[2,96,1024]{2,1,0:T(8,128)(2,1)}, u32[]{:S(2)}, u32[]{:S(2)}) collective-permute-start(bf16[2,96,1024]{2,1,0:T(8,128)(2,1)} %get-tuple-element.405), channel_id=1, source_target_pairs={{0,4},{4,8},{8,12},{1,5},{5,9},{9,13},{2,6},{6,10},{10,14},{3,7},{... | collective-permute-start | bytes 1179656 | tf_op jit(solution)/shard_map/ppermute | solution.py:174
  126.6 5.6 all-to-all-start.6
  136.3 5.0 collective-permute-start.54
  148.9 25.9 %collective-permute-start.34 = (bf16[2,96,1024]{2,1,0:T(8,128)(2,1)}, bf16[2,96,1024]{2,1,0:T(8,128)(2,1)}, u32[]{:S(2)}, u32[]{:S(2)}) collective-permute-start(bf16[2,96,1024]{2,1,0:T(8,128)(2,1)} %get-tuple-element.407), channel_id=1, source_target_pairs={{0,4},{4,8},{8,12},{1,5},{5,9},{9,13},{2,6},{6,10},{10,14},{3,7},{... | collective-permute-start | bytes 1179656 | tf_op jit(solution)/shard_map/ppermute | solution.py:174
  176.6 13.8 %conditional.7 = (bf16[4,2,96,1024]{3,2,1,0:T(8,128)(2,1)}) conditional(s32[]{:T(128)} %bitcast.42, (s32[4]{0:T(128)}, bf16[4,2,96,1024]{3,2,1,0:T(8,128)(2,1)S(1)}, bf16[2,96,1024]{2,1,0:T(8,128)(2,1)}, bf16[2,96,1024]{2,1,0:T(8,128)(2,1)}, bf16[2,96,1024]{2,1,0:T(8,128)(2,1)}, /*index=5*/bf16[2,96,1024]{2,1,0:T(8,128)(2,1)}, ...), branch_computations={%region_18.22_spmd, %region_19.23_spmd, %region_20.24_spmd} | conditional | flops 787492 | bytes 36180224 | solution.py:207
  176.6 13.8 %pick_items.49 = bf16[4,2,96,1024]{3,2,1,0:T(8,128)(2,1)} custom-call(s32[4]{0:T(128)} %get-tuple-element.321.refs_0_, bf16[4,2,96,1024]{3,2,1,0:T(8,128)(2,1)S(1)} %get-tuple-element.322.refs_1_, bf16[2,96,1024]{2,1,0:T(8,128)(2,1)} %get-tuple-element.323.refs_2_, bf16[2,96,1024]{2,1,0:T(8,128)(2,1)} %get-tuple-element.324.refs_3_, ...), custom_call_target="tpu_custom_call" | custom-call | tf_op jit(solution)/shard_map/cond/branch_0_fun/pick_items/pallas_call | solution.py:152
  190.4 4.9 all-to-all-start.9
  199.8 38.5 %collective-permute-start.36 = (bf16[2,96,1024]{2,1,0:T(8,128)(2,1)}, bf16[2,96,1024]{2,1,0:T(8,128)(2,1)S(1)}, u32[]{:S(2)}, u32[]{:S(2)}) collective-permute-start(bf16[2,96,1024]{2,1,0:T(8,128)(2,1)} %get-tuple-element.409), channel_id=1, source_target_pairs={{0,4},{4,8},{8,12},{1,5},{5,9},{9,13},{2,6},{6,10},{10,14},{3,7},{... | collective-permute-start | bytes 1179656 | tf_op jit(solution)/shard_map/ppermute | solution.py:174
  241.5 5.6 collective-permute-done.36.refs_5_
  252.4 15.6 %collective-permute-start.38 = (bf16[2,96,1024]{2,1,0:T(8,128)(2,1)}, bf16[2,96,1024]{2,1,0:T(8,128)(2,1)}, u32[]{:S(2)}, u32[]{:S(2)}) collective-permute-start(bf16[2,96,1024]{2,1,0:T(8,128)(2,1)} %get-tuple-element.411), channel_id=1, source_target_pairs={{0,4},{4,8},{8,12},{1,5},{5,9},{9,13},{2,6},{6,10},{10,14},{3,7},{... | collective-permute-start | bytes 1179656 | tf_op jit(solution)/shard_map/ppermute | solution.py:174
  269.3 13.7 %pick_items.54 = (bf16[1,96,1024]{2,1,0:T(8,128)(2,1)}, bf16[1,96,1024]{2,1,0:T(8,128)(2,1)}) custom-call(s32[2]{0:T(128)} %pad_add_fusion.13.refs_0_, bf16[4,1,96,1024]{3,2,1,0:T(8,128)(2,1)} %all-to-all-done.refs_1_), custom_call_target="tpu_custom_call" | custom-call | tf_op jit(solution)/shard_map/pick_items/pallas_call | solution.py:152
  289.4 13.7 %pick_items.64 = (bf16[1,96,1024]{2,1,0:T(8,128)(2,1)}, bf16[1,96,1024]{2,1,0:T(8,128)(2,1)}) custom-call(s32[2]{0:T(128)} %pad_add_fusion.18.refs_0_, bf16[4,1,96,1024]{3,2,1,0:T(8,128)(2,1)} %all-to-all-done.6.refs_1_), custom_call_target="tpu_custom_call" | custom-call | tf_op jit(solution)/shard_map/pick_items/pallas_call | solution.py:152
  308.5 13.7 %pick_items.55 = (bf16[1,96,1024]{2,1,0:T(8,128)(2,1)}, bf16[1,96,1024]{2,1,0:T(8,128)(2,1)}) custom-call(s32[2]{0:T(128)} %pad_add_fusion.14.refs_0_, bf16[4,1,96,1024]{3,2,1,0:T(8,128)(2,1)} %all-to-all-done.refs_1_, bf16[1,96,1024]{2,1,0:T(8,128)(2,1)S(1)} %collective-permute-done.20.refs_2_, ...), custom_call_target="tpu_custom_call" | custom-call | tf_op jit(solution)/shard_map/pick_items/pallas_call | solution.py:152
  324.1 37.6 %conditional.5 = (bf16[4,2,96,1024]{3,2,1,0:T(8,128)(2,1)}) conditional(s32[]{:T(128)} %bitcast.10, (s32[4]{0:T(128)}, bf16[4,2,96,1024]{3,2,1,0:T(8,128)(2,1)S(1)}, bf16[2,96,1024]{2,1,0:T(8,128)(2,1)S(1)}, bf16[2,96,1024]{2,1,0:T(8,128)(2,1)}, bf16[2,96,1024]{2,1,0:T(8,128)(2,1)}, /*index=5*/bf16[2,96,1024]{2,1,0:T(8,128)(2,1)S(1)}, ...), branch_computations={%region_6.8_spmd, %region_7.9_spmd, %region_8.11_spmd} | conditional | flops 787492 | bytes 36180224 | solution.py:207
  324.2 37.5 %pick_items.40 = bf16[4,2,96,1024]{3,2,1,0:T(8,128)(2,1)} custom-call(s32[4]{0:T(128)} %get-tuple-element.259.refs_0_, bf16[4,2,96,1024]{3,2,1,0:T(8,128)(2,1)S(1)} %get-tuple-element.260.refs_1_, bf16[2,96,1024]{2,1,0:T(8,128)(2,1)S(1)} %get-tuple-element.261.refs_2_, bf16[2,96,1024]{2,1,0:T(8,128)(2,1)} %get-tuple-element.262.refs_3_, ...), custom_call_target="tpu_custom_call" | custom-call | tf_op jit(solution)/shard_map/cond/branch_0_fun/pick_items/pallas_call | solution.py:152
  363.0 5.8 all-to-all-start.3
  368.8 13.7 %pick_items.65 = (bf16[1,96,1024]{2,1,0:T(8,128)(2,1)}, bf16[1,96,1024]{2,1,0:T(8,128)(2,1)}) custom-call(s32[2]{0:T(128)} %pad_add_fusion.19.refs_0_, bf16[4,1,96,1024]{3,2,1,0:T(8,128)(2,1)} %all-to-all-done.6.refs_1_, bf16[1,96,1024]{2,1,0:T(8,128)(2,1)S(1)} %collective-permute-done.40.refs_2_, ...), custom_call_target="tpu_custom_call" | custom-call | tf_op jit(solution)/shard_map/pick_items/pallas_call | solution.py:152
  382.5 4.3 collective-permute-start.42
  388.1 13.7 %pick_items.56 = (bf16[1,96,1024]{2,1,0:T(8,128)(2,1)}, bf16[1,96,1024]{2,1,0:T(8,128)(2,1)}) custom-call(s32[2]{0:T(128)} %pad_add_fusion.15.refs_0_, bf16[4,1,96,1024]{3,2,1,0:T(8,128)(2,1)} %all-to-all-done.refs_1_, bf16[1,96,1024]{2,1,0:T(8,128)(2,1)S(1)} %collective-permute-done.20.refs_2_, bf16[1,96,1024]{2,1,0:T(8,128)(2,1)} %collective-permute-done.22.refs_3_, ...), custom_call_target="tpu_custom_call" | custom-call | tf_op jit(solution)/shard_map/pick_items/pallas_call | solution.py:152
  404.5 13.7 %pick_items.66 = (bf16[1,96,1024]{2,1,0:T(8,128)(2,1)}, bf16[1,96,1024]{2,1,0:T(8,128)(2,1)}) custom-call(s32[2]{0:T(128)} %pad_add_fusion.20.refs_0_, bf16[4,1,96,1024]{3,2,1,0:T(8,128)(2,1)} %all-to-all-done.6.refs_1_, bf16[1,96,1024]{2,1,0:T(8,128)(2,1)S(1)} %collective-permute-done.40.refs_2_, bf16[1,96,1024]{2,1,0:T(8,128)(2,1)S(1)} %collective-permute-done.42.refs_3_, ...), custom_call_target="tpu_custom_call" | custom-call | tf_op jit(solution)/shard_map/pick_items/pallas_call | solution.py:152
  420.8 13.7 %pick_items.57 = (bf16[1,96,1024]{2,1,0:T(8,128)(2,1)}, bf16[1,96,1024]{2,1,0:T(8,128)(2,1)}) custom-call(s32[2]{0:T(128)} %pad_add_fusion.16.refs_0_, bf16[4,1,96,1024]{3,2,1,0:T(8,128)(2,1)} %all-to-all-done.refs_1_, bf16[1,96,1024]{2,1,0:T(8,128)(2,1)S(1)} %collective-permute-done.20.refs_2_, bf16[1,96,1024]{2,1,0:T(8,128)(2,1)} %collective-permute-done.22.refs_3_, ...), custom_call_target="tpu_custom_call" | custom-call | tf_op jit(solution)/shard_map/pick_items/pallas_call | solution.py:152
  442.3 13.7 %pick_items.67 = (bf16[1,96,1024]{2,1,0:T(8,128)(2,1)}, bf16[1,96,1024]{2,1,0:T(8,128)(2,1)}) custom-call(s32[2]{0:T(128)} %pad_add_fusion.21.refs_0_, bf16[4,1,96,1024]{3,2,1,0:T(8,128)(2,1)} %all-to-all-done.6.refs_1_, bf16[1,96,1024]{2,1,0:T(8,128)(2,1)S(1)} %collective-permute-done.40.refs_2_, bf16[1,96,1024]{2,1,0:T(8,128)(2,1)S(1)} %collective-permute-done.42.refs_3_, ...), custom_call_target="tpu_custom_call" | custom-call | tf_op jit(solution)/shard_map/pick_items/pallas_call | solution.py:152
  456.0 4.7 collective-permute-start.46
  462.0 13.7 %pick_items.58 = (bf16[1,96,1024]{2,1,0:T(8,128)(2,1)}, bf16[1,96,1024]{2,1,0:T(8,128)(2,1)}) custom-call(s32[2]{0:T(128)} %pad_add_fusion.17.refs_0_, bf16[4,1,96,1024]{3,2,1,0:T(8,128)(2,1)} %all-to-all-done.refs_1_, bf16[1,96,1024]{2,1,0:T(8,128)(2,1)S(1)} %collective-permute-done.20.refs_2_, bf16[1,96,1024]{2,1,0:T(8,128)(2,1)} %collective-permute-done.22.refs_3_, ...), custom_call_target="tpu_custom_call" | custom-call | tf_op jit(solution)/shard_map/pick_items/pallas_call | solution.py:152
  475.7 4.7 collective-permute-start.28
  485.0 19.7 %conditional.6 = (bf16[4,1,96,1024]{3,2,1,0:T(8,128)(2,1)}) conditional(s32[]{:T(128)} %bitcast.42, (s32[4]{0:T(128)}, bf16[4,1,96,1024]{3,2,1,0:T(8,128)(2,1)}, bf16[1,96,1024]{2,1,0:T(8,128)(2,1)S(1)}, bf16[1,96,1024]{2,1,0:T(8,128)(2,1)S(1)}, bf16[1,96,1024]{2,1,0:T(8,128)(2,1)S(1)}, ...), branch_computations={%region_15.19_spmd, %region_16.20_spmd, %region_17.21_spmd} | conditional | flops 394276 | bytes 14946440 | solution.py:207
  485.0 19.7 %pick_items.44 = bf16[4,1,96,1024]{3,2,1,0:T(8,128)(2,1)} custom-call(s32[4]{0:T(128)} %get-tuple-element.291.refs_0_, bf16[4,1,96,1024]{3,2,1,0:T(8,128)(2,1)} %get-tuple-element.292.refs_1_, bf16[1,96,1024]{2,1,0:T(8,128)(2,1)S(1)} %get-tuple-element.293.refs_2_, bf16[1,96,1024]{2,1,0:T(8,128)(2,1)S(1)} %get-tuple-element.294.refs_3_, ...), custom_call_target="tpu_custom_call" | custom-call | tf_op jit(solution)/shard_map/cond/branch_0_fun/pick_items/pallas_call | solution.py:152
  504.8 7.8 %conditional.4 = (bf16[4,1,96,1024]{3,2,1,0:T(8,128)(2,1)}) conditional(s32[]{:T(128)} %bitcast.10, (s32[4]{0:T(128)}, bf16[4,1,96,1024]{3,2,1,0:T(8,128)(2,1)}, bf16[1,96,1024]{2,1,0:T(8,128)(2,1)S(1)}, bf16[1,96,1024]{2,1,0:T(8,128)(2,1)}, bf16[1,96,1024]{2,1,0:T(8,128)(2,1)S(1)}, /*index=5*/bf16[1,96,1024]{2,1,0:T(8,128)(2,1)}, ...), branch_computations={%region_3.4_spmd, %region_4.5_spmd, %region_5.7_spmd} | conditional | flops 394276 | bytes 14946440 | solution.py:207
  504.8 7.8 %pick_items.36 = bf16[4,1,96,1024]{3,2,1,0:T(8,128)(2,1)} custom-call(s32[4]{0:T(128)} %get-tuple-element.211.refs_0_, bf16[4,1,96,1024]{3,2,1,0:T(8,128)(2,1)} %get-tuple-element.212.refs_1_, bf16[1,96,1024]{2,1,0:T(8,128)(2,1)S(1)} %get-tuple-element.213.refs_2_, bf16[1,96,1024]{2,1,0:T(8,128)(2,1)} %get-tuple-element.214.refs_3_, ...), custom_call_target="tpu_custom_call" | custom-call | tf_op jit(solution)/shard_map/cond/branch_0_fun/pick_items/pallas_call | solution.py:152
  516.1 5.1 all-to-all-start.1
  540.9 10.0 %convolution_negate_fusion = f32[384,1024]{1,0:T(8,128)S(1)} fusion(bf16[384,1024]{1,0:T(8,128)(2,1)S(1)} %copy-done.9, bf16[1024,1024]{1,0:T(8,128)(2,1)S(1)} %copy-done.4), kind=kOutput, calls=%fused_computation.97 | convolution fusion | flops 805699584 | bytes 4456448 | tf_op jit(solution)/shard_map/dot_general | solution.py:40
  571.3 5.7 convolution_convert_fusion
  579.7 23.2 %all-to-all-start.4 = ((bf16[16,24,1024]{2,1,0:T(8,128)(2,1)}), bf16[16,24,1024]{2,1,0:T(8,128)(2,1)S(1)}, u32[]{:S(2)}, u32[]{:S(2)}) async-start(bf16[16,24,1024]{2,1,0:T(8,128)(2,1)} %bitcast.137), calls=%async_computation.4 | async-start | bytes 1572864 | tf_op jit(solution)/shard_map/all_to_all | solution.py:211
  602.8 4.6 fusion.8
  607.5 8.2 %select_convert_fusion = bf16[384,1024]{1,0:T(8,128)(2,1)} fusion(f32[1024,1024]{1,0:T(8,128)} %get-tuple-element.516, bf16[1024,1024]{1,0:T(8,128)(2,1)} %get-tuple-element.473, f32[1024]{0:T(1024)S(1)} %rsqrt_multiply_fusion, pred[]{:T(512)} %bitcast.41, f32[384,1024]{1,0:T(8,128)} %fusion.8, bf16[384,1024]{1,0:T(8,128)(2,1)} %bitcast.132, ...), kind=kOutput, calls=%fused_computation.82 | convolution fusion | flops 1623195648 | bytes 15736833 | tf_op jit(solution)/shard_map/dot_general | solution.py:20
  615.7 5.7 all-to-all-done.4
  621.4 5.6 all-to-all-start.10
  628.7 16.9 %all-to-all-done.10 = bf16[16,24,1024]{2,1,0:T(8,128)(2,1)S(1)} async-done(((bf16[16,24,1024]{2,1,0:T(8,128)(2,1)}), bf16[16,24,1024]{2,1,0:T(8,128)(2,1)S(1)}, u32[]{:S(2)}, u32[]{:S(2)}) %all-to-all-start.10) | async-done | bytes 786464 | tf_op jit(solution)/shard_map/all_to_all | solution.py:211
  645.6 5.6 all-to-all-start.5
  653.0 16.8 %all-to-all-done.5 = bf16[16,24,1024]{2,1,0:T(8,128)(2,1)S(1)} async-done(((bf16[16,24,1024]{2,1,0:T(8,128)(2,1)}), bf16[16,24,1024]{2,1,0:T(8,128)(2,1)S(1)}, u32[]{:S(2)}, u32[]{:S(2)}) %all-to-all-start.5) | async-done | bytes 786464 | tf_op jit(solution)/shard_map/all_to_all | solution.py:211
  669.8 5.6 all-to-all-start.11
  675.4 18.6 %all-to-all-done.11 = bf16[16,24,1024]{2,1,0:T(8,128)(2,1)S(1)} async-done(((bf16[16,24,1024]{2,1,0:T(8,128)(2,1)}), bf16[16,24,1024]{2,1,0:T(8,128)(2,1)S(1)}, u32[]{:S(2)}, u32[]{:S(2)}) %all-to-all-start.11) | async-done | bytes 786464 | tf_op jit(solution)/shard_map/all_to_all | solution.py:211
  (205 shorter events, 162.4 us)
Async XLA Ops:
  10.5 23.3 %all-to-all-start.8 = ((bf16[4,2,96,1024]{3,2,1,0:T(8,128)(2,1)}), bf16[4,2,96,1024]{3,2,1,0:T(8,128)(2,1)S(1)}, u32[]{:S(2)}, u32[]{:S(2)}) async-start(bf16[4,2,96,1024]{3,2,1,0:T(8,128)(2,1)} %pad_maximum_fusion.1), calls=%async_computation.8 | async-start | bytes 3145728 | tf_op jit(solution)/shard_map/all_to_all | solution.py:211
  33.8 37.2 %all-to-all-start.2 = ((bf16[4,2,96,1024]{3,2,1,0:T(8,128)(2,1)}), bf16[4,2,96,1024]{3,2,1,0:T(8,128)(2,1)S(1)}, u32[]{:S(2)}, u32[]{:S(2)}) async-start(bf16[4,2,96,1024]{3,2,1,0:T(8,128)(2,1)} %pad_maximum_fusion), calls=%async_computation.2 | async-start | bytes 3145728 | tf_op jit(solution)/shard_map/all_to_all | solution.py:211
  47.7 12.8 %collective-permute-start.48 = (bf16[2,96,1024]{2,1,0:T(8,128)(2,1)}, bf16[2,96,1024]{2,1,0:T(8,128)(2,1)S(1)}, u32[]{:S(2)}, u32[]{:S(2)}) collective-permute-start(bf16[2,96,1024]{2,1,0:T(8,128)(2,1)} %get-tuple-element.421), channel_id=1, source_target_pairs={{0,4},{4,8},{8,12},{1,5},{5,9},{9,13},{2,6},{6,10},{10,14},{3,7},{... | collective-permute-start | bytes 1179656 | tf_op jit(solution)/shard_map/ppermute | solution.py:174
  51.7 12.6 %collective-permute-start.49 = (bf16[2,96,1024]{2,1,0:T(8,128)(2,1)}, bf16[2,96,1024]{2,1,0:T(8,128)(2,1)}, u32[]{:S(2)}, u32[]{:S(2)}) collective-permute-start(bf16[2,96,1024]{2,1,0:T(8,128)(2,1)} %get-tuple-element.422), channel_id=1, source_target_pairs={{4,0},{8,4},{12,8},{5,1},{9,5},{13,9},{6,2},{10,6},{14,10},{7,3},{... | collective-permute-start | bytes 1179656 | tf_op jit(solution)/shard_map/ppermute | solution.py:175
  65.8 20.5 %collective-permute-start.50 = (bf16[2,96,1024]{2,1,0:T(8,128)(2,1)}, bf16[2,96,1024]{2,1,0:T(8,128)(2,1)}, u32[]{:S(2)}, u32[]{:S(2)}) collective-permute-start(bf16[2,96,1024]{2,1,0:T(8,128)(2,1)} %get-tuple-element.423), channel_id=1, source_target_pairs={{0,4},{4,8},{8,12},{1,5},{5,9},{9,13},{2,6},{6,10},{10,14},{3,7},{... | collective-permute-start | bytes 1179656 | tf_op jit(solution)/shard_map/ppermute | solution.py:174
  69.8 16.6 %collective-permute-start.51 = (bf16[2,96,1024]{2,1,0:T(8,128)(2,1)}, bf16[2,96,1024]{2,1,0:T(8,128)(2,1)}, u32[]{:S(2)}, u32[]{:S(2)}) collective-permute-start(bf16[2,96,1024]{2,1,0:T(8,128)(2,1)} %get-tuple-element.424), channel_id=1, source_target_pairs={{4,0},{8,4},{12,8},{5,1},{9,5},{13,9},{6,2},{10,6},{14,10},{7,3},{... | collective-permute-start | bytes 1179656 | tf_op jit(solution)/shard_map/ppermute | solution.py:175
  71.1 55.5 %all-to-all-start = ((bf16[4,1,96,1024]{3,2,1,0:T(8,128)(2,1)}), bf16[4,1,96,1024]{3,2,1,0:T(8,128)(2,1)}, u32[]{:S(2)}, u32[]{:S(2)}) async-start(bf16[4,1,96,1024]{3,2,1,0:T(8,128)(2,1)} %bitcast.126), calls=%async_computation | async-start | bytes 1572864 | tf_op jit(solution)/shard_map/all_to_all | solution.py:211
  80.7 25.9 %collective-permute-start.30 = (bf16[2,96,1024]{2,1,0:T(8,128)(2,1)}, bf16[2,96,1024]{2,1,0:T(8,128)(2,1)S(1)}, u32[]{:S(2)}, u32[]{:S(2)}) collective-permute-start(bf16[2,96,1024]{2,1,0:T(8,128)(2,1)} %get-tuple-element.403), channel_id=1, source_target_pairs={{0,4},{4,8},{8,12},{1,5},{5,9},{9,13},{2,6},{6,10},{10,14},{3,7},{... | collective-permute-start | bytes 1179656 | tf_op jit(solution)/shard_map/ppermute | solution.py:174
  85.0 21.6 %collective-permute-start.31 = (bf16[2,96,1024]{2,1,0:T(8,128)(2,1)}, bf16[2,96,1024]{2,1,0:T(8,128)(2,1)}, u32[]{:S(2)}, u32[]{:S(2)}) collective-permute-start(bf16[2,96,1024]{2,1,0:T(8,128)(2,1)} %get-tuple-element.404), channel_id=1, source_target_pairs={{4,0},{8,4},{12,8},{5,1},{9,5},{13,9},{6,2},{10,6},{14,10},{7,3},{... | collective-permute-start | bytes 1179656 | tf_op jit(solution)/shard_map/ppermute | solution.py:175
  87.9 46.8 %collective-permute-start.52 = (bf16[2,96,1024]{2,1,0:T(8,128)(2,1)}, bf16[2,96,1024]{2,1,0:T(8,128)(2,1)}, u32[]{:S(2)}, u32[]{:S(2)}) collective-permute-start(bf16[2,96,1024]{2,1,0:T(8,128)(2,1)} %get-tuple-element.425), channel_id=1, source_target_pairs={{0,4},{4,8},{8,12},{1,5},{5,9},{9,13},{2,6},{6,10},{10,14},{3,7},{... | collective-permute-start | bytes 1179656 | tf_op jit(solution)/shard_map/ppermute | solution.py:174
  104.8 29.9 %collective-permute-start.53 = (bf16[2,96,1024]{2,1,0:T(8,128)(2,1)}, bf16[2,96,1024]{2,1,0:T(8,128)(2,1)}, u32[]{:S(2)}, u32[]{:S(2)}) collective-permute-start(bf16[2,96,1024]{2,1,0:T(8,128)(2,1)} %get-tuple-element.426), channel_id=1, source_target_pairs={{4,0},{8,4},{12,8},{5,1},{9,5},{13,9},{6,2},{10,6},{14,10},{7,3},{... | collective-permute-start | bytes 1179656 | tf_op jit(solution)/shard_map/ppermute | solution.py:175
  108.4 38.9 %collective-permute-start.32 = (bf16[2,96,1024]{2,1,0:T(8,128)(2,1)}, bf16[2,96,1024]{2,1,0:T(8,128)(2,1)}, u32[]{:S(2)}, u32[]{:S(2)}) collective-permute-start(bf16[2,96,1024]{2,1,0:T(8,128)(2,1)} %get-tuple-element.405), channel_id=1, source_target_pairs={{0,4},{4,8},{8,12},{1,5},{5,9},{9,13},{2,6},{6,10},{10,14},{3,7},{... | collective-permute-start | bytes 1179656 | tf_op jit(solution)/shard_map/ppermute | solution.py:174
  125.3 22.1 %collective-permute-start.33 = (bf16[2,96,1024]{2,1,0:T(8,128)(2,1)}, bf16[2,96,1024]{2,1,0:T(8,128)(2,1)}, u32[]{:S(2)}, u32[]{:S(2)}) collective-permute-start(bf16[2,96,1024]{2,1,0:T(8,128)(2,1)} %get-tuple-element.406), channel_id=1, source_target_pairs={{4,0},{8,4},{12,8},{5,1},{9,5},{13,9},{6,2},{10,6},{14,10},{7,3},{... | collective-permute-start | bytes 1179656 | tf_op jit(solution)/shard_map/ppermute | solution.py:175
  126.6 63.9 %all-to-all-start.6 = ((bf16[4,1,96,1024]{3,2,1,0:T(8,128)(2,1)}), bf16[4,1,96,1024]{3,2,1,0:T(8,128)(2,1)}, u32[]{:S(2)}, u32[]{:S(2)}) async-start(bf16[4,1,96,1024]{3,2,1,0:T(8,128)(2,1)} %bitcast.125), calls=%async_computation.6 | async-start | bytes 1572864 | tf_op jit(solution)/shard_map/all_to_all | solution.py:211
  136.3 40.3 %collective-permute-start.54 = (bf16[2,96,1024]{2,1,0:T(8,128)(2,1)}, bf16[2,96,1024]{2,1,0:T(8,128)(2,1)}, u32[]{:S(2)}, u32[]{:S(2)}) collective-permute-start(bf16[2,96,1024]{2,1,0:T(8,128)(2,1)} %get-tuple-element.427), channel_id=1, source_target_pairs={{0,4},{4,8},{8,12},{1,5},{5,9},{9,13},{2,6},{6,10},{10,14},{3,7},{... | collective-permute-start | bytes 1179656 | tf_op jit(solution)/shard_map/ppermute | solution.py:174
  141.3 35.3 %collective-permute-start.55 = (bf16[2,96,1024]{2,1,0:T(8,128)(2,1)}, bf16[2,96,1024]{2,1,0:T(8,128)(2,1)}, u32[]{:S(2)}, u32[]{:S(2)}) collective-permute-start(bf16[2,96,1024]{2,1,0:T(8,128)(2,1)} %get-tuple-element.428), channel_id=1, source_target_pairs={{4,0},{8,4},{12,8},{5,1},{9,5},{13,9},{6,2},{10,6},{14,10},{7,3},{... | collective-permute-start | bytes 1179656 | tf_op jit(solution)/shard_map/ppermute | solution.py:175
  148.9 48.3 %collective-permute-start.34 = (bf16[2,96,1024]{2,1,0:T(8,128)(2,1)}, bf16[2,96,1024]{2,1,0:T(8,128)(2,1)}, u32[]{:S(2)}, u32[]{:S(2)}) collective-permute-start(bf16[2,96,1024]{2,1,0:T(8,128)(2,1)} %get-tuple-element.407), channel_id=1, source_target_pairs={{0,4},{4,8},{8,12},{1,5},{5,9},{9,13},{2,6},{6,10},{10,14},{3,7},{... | collective-permute-start | bytes 1179656 | tf_op jit(solution)/shard_map/ppermute | solution.py:174
  174.8 23.4 %collective-permute-start.35 = (bf16[2,96,1024]{2,1,0:T(8,128)(2,1)}, bf16[2,96,1024]{2,1,0:T(8,128)(2,1)}, u32[]{:S(2)}, u32[]{:S(2)}) collective-permute-start(bf16[2,96,1024]{2,1,0:T(8,128)(2,1)} %get-tuple-element.408), channel_id=1, source_target_pairs={{4,0},{8,4},{12,8},{5,1},{9,5},{13,9},{6,2},{10,6},{14,10},{7,3},{... | collective-permute-start | bytes 1179656 | tf_op jit(solution)/shard_map/ppermute | solution.py:175
  190.4 172.6 %all-to-all-start.9 = ((bf16[4,2,96,1024]{3,2,1,0:T(8,128)(2,1)}), bf16[4,2,96,1024]{3,2,1,0:T(8,128)(2,1)}, u32[]{:S(2)}, u32[]{:S(2)}) async-start(bf16[4,2,96,1024]{3,2,1,0:T(8,128)(2,1)} %get-tuple-element.531), calls=%async_computation.9 | async-start | bytes 3145728 | tf_op jit(solution)/shard_map/all_to_all | solution.py:211
  199.8 47.3 %collective-permute-start.36 = (bf16[2,96,1024]{2,1,0:T(8,128)(2,1)}, bf16[2,96,1024]{2,1,0:T(8,128)(2,1)S(1)}, u32[]{:S(2)}, u32[]{:S(2)}) collective-permute-start(bf16[2,96,1024]{2,1,0:T(8,128)(2,1)} %get-tuple-element.409), channel_id=1, source_target_pairs={{0,4},{4,8},{8,12},{1,5},{5,9},{9,13},{2,6},{6,10},{10,14},{3,7},{... | collective-permute-start | bytes 1179656 | tf_op jit(solution)/shard_map/ppermute | solution.py:174
  238.3 12.5 %collective-permute-start.37 = (bf16[2,96,1024]{2,1,0:T(8,128)(2,1)}, bf16[2,96,1024]{2,1,0:T(8,128)(2,1)S(1)}, u32[]{:S(2)}, u32[]{:S(2)}) collective-permute-start(bf16[2,96,1024]{2,1,0:T(8,128)(2,1)} %get-tuple-element.410), channel_id=1, source_target_pairs={{4,0},{8,4},{12,8},{5,1},{9,5},{13,9},{6,2},{10,6},{14,10},{7,3},{... | collective-permute-start | bytes 1179656 | tf_op jit(solution)/shard_map/ppermute | solution.py:175
  252.4 71.8 %collective-permute-start.38 = (bf16[2,96,1024]{2,1,0:T(8,128)(2,1)}, bf16[2,96,1024]{2,1,0:T(8,128)(2,1)}, u32[]{:S(2)}, u32[]{:S(2)}) collective-permute-start(bf16[2,96,1024]{2,1,0:T(8,128)(2,1)} %get-tuple-element.411), channel_id=1, source_target_pairs={{0,4},{4,8},{8,12},{1,5},{5,9},{9,13},{2,6},{6,10},{10,14},{3,7},{... | collective-permute-start | bytes 1179656 | tf_op jit(solution)/shard_map/ppermute | solution.py:174
  268.0 56.2 %collective-permute-start.39 = (bf16[2,96,1024]{2,1,0:T(8,128)(2,1)}, bf16[2,96,1024]{2,1,0:T(8,128)(2,1)}, u32[]{:S(2)}, u32[]{:S(2)}) collective-permute-start(bf16[2,96,1024]{2,1,0:T(8,128)(2,1)} %get-tuple-element.412), channel_id=1, source_target_pairs={{4,0},{8,4},{12,8},{5,1},{9,5},{13,9},{6,2},{10,6},{14,10},{7,3},{... | collective-permute-start | bytes 1179656 | tf_op jit(solution)/shard_map/ppermute | solution.py:175
  283.0 24.2 %collective-permute-start.20 = (bf16[1,96,1024]{2,1,0:T(8,128)(2,1)}, bf16[1,96,1024]{2,1,0:T(8,128)(2,1)S(1)}, u32[]{:S(2)}, u32[]{:S(2)}) collective-permute-start(bf16[1,96,1024]{2,1,0:T(8,128)(2,1)} %get-tuple-element.393), channel_id=1, source_target_pairs={{0,4},{4,8},{8,12},{1,5},{5,9},{9,13},{2,6},{6,10},{10,14},{3,7},{... | collective-permute-start | bytes 589832 | tf_op jit(solution)/shard_map/ppermute | solution.py:174
  287.0 21.5 %collective-permute-start.21 = (bf16[1,96,1024]{2,1,0:T(8,128)(2,1)}, bf16[1,96,1024]{2,1,0:T(8,128)(2,1)S(1)}, u32[]{:S(2)}, u32[]{:S(2)}) collective-permute-start(bf16[1,96,1024]{2,1,0:T(8,128)(2,1)} %get-tuple-element.394), channel_id=1, source_target_pairs={{4,0},{8,4},{12,8},{5,1},{9,5},{13,9},{6,2},{10,6},{14,10},{7,3},{... | collective-permute-start | bytes 589832 | tf_op jit(solution)/shard_map/ppermute | solution.py:175
  303.1 65.7 %collective-permute-start.40 = (bf16[1,96,1024]{2,1,0:T(8,128)(2,1)}, bf16[1,96,1024]{2,1,0:T(8,128)(2,1)S(1)}, u32[]{:S(2)}, u32[]{:S(2)}) collective-permute-start(bf16[1,96,1024]{2,1,0:T(8,128)(2,1)} %get-tuple-element.413), channel_id=1, source_target_pairs={{0,4},{4,8},{8,12},{1,5},{5,9},{9,13},{2,6},{6,10},{10,14},{3,7},{... | collective-permute-start | bytes 589832 | tf_op jit(solution)/shard_map/ppermute | solution.py:174
  307.1 61.7 %collective-permute-start.41 = (bf16[1,96,1024]{2,1,0:T(8,128)(2,1)}, bf16[1,96,1024]{2,1,0:T(8,128)(2,1)S(1)}, u32[]{:S(2)}, u32[]{:S(2)}) collective-permute-start(bf16[1,96,1024]{2,1,0:T(8,128)(2,1)} %get-tuple-element.414), channel_id=1, source_target_pairs={{4,0},{8,4},{12,8},{5,1},{9,5},{13,9},{6,2},{10,6},{14,10},{7,3},{... | collective-permute-start | bytes 589832 | tf_op jit(solution)/shard_map/ppermute | solution.py:175
  322.2 65.9 %collective-permute-start.22 = (bf16[1,96,1024]{2,1,0:T(8,128)(2,1)}, bf16[1,96,1024]{2,1,0:T(8,128)(2,1)}, u32[]{:S(2)}, u32[]{:S(2)}) collective-permute-start(bf16[1,96,1024]{2,1,0:T(8,128)(2,1)} %get-tuple-element.395), channel_id=1, source_target_pairs={{0,4},{4,8},{8,12},{1,5},{5,9},{9,13},{2,6},{6,10},{10,14},{3,7},{... | collective-permute-start | bytes 589832 | tf_op jit(solution)/shard_map/ppermute | solution.py:174
  361.7 26.4 %collective-permute-start.23 = (bf16[1,96,1024]{2,1,0:T(8,128)(2,1)}, bf16[1,96,1024]{2,1,0:T(8,128)(2,1)S(1)}, u32[]{:S(2)}, u32[]{:S(2)}) collective-permute-start(bf16[1,96,1024]{2,1,0:T(8,128)(2,1)} %get-tuple-element.396), channel_id=1, source_target_pairs={{4,0},{8,4},{12,8},{5,1},{9,5},{13,9},{6,2},{10,6},{14,10},{7,3},{... | collective-permute-start | bytes 589832 | tf_op jit(solution)/shard_map/ppermute | solution.py:175
  363.0 153.1 %all-to-all-start.3 = ((bf16[4,2,96,1024]{3,2,1,0:T(8,128)(2,1)}), bf16[4,2,96,1024]{3,2,1,0:T(8,128)(2,1)S(1)}, u32[]{:S(2)}, u32[]{:S(2)}) async-start(bf16[4,2,96,1024]{3,2,1,0:T(8,128)(2,1)} %get-tuple-element.529), calls=%async_computation.3 | async-start | bytes 3145728 | tf_op jit(solution)/shard_map/all_to_all | solution.py:211
  382.5 21.9 %collective-permute-start.42 = (bf16[1,96,1024]{2,1,0:T(8,128)(2,1)}, bf16[1,96,1024]{2,1,0:T(8,128)(2,1)S(1)}, u32[]{:S(2)}, u32[]{:S(2)}) collective-permute-start(bf16[1,96,1024]{2,1,0:T(8,128)(2,1)} %get-tuple-element.415), channel_id=1, source_target_pairs={{0,4},{4,8},{8,12},{1,5},{5,9},{9,13},{2,6},{6,10},{10,14},{3,7},{... | collective-permute-start | bytes 589832 | tf_op jit(solution)/shard_map/ppermute | solution.py:174
  386.8 17.7 %collective-permute-start.43 = (bf16[1,96,1024]{2,1,0:T(8,128)(2,1)}, bf16[1,96,1024]{2,1,0:T(8,128)(2,1)S(1)}, u32[]{:S(2)}, u32[]{:S(2)}) collective-permute-start(bf16[1,96,1024]{2,1,0:T(8,128)(2,1)} %get-tuple-element.416), channel_id=1, source_target_pairs={{4,0},{8,4},{12,8},{5,1},{9,5},{13,9},{6,2},{10,6},{14,10},{7,3},{... | collective-permute-start | bytes 589832 | tf_op jit(solution)/shard_map/ppermute | solution.py:175
  401.8 19.0 %collective-permute-start.24 = (bf16[1,96,1024]{2,1,0:T(8,128)(2,1)}, bf16[1,96,1024]{2,1,0:T(8,128)(2,1)S(1)}, u32[]{:S(2)}, u32[]{:S(2)}) collective-permute-start(bf16[1,96,1024]{2,1,0:T(8,128)(2,1)} %get-tuple-element.397), channel_id=1, source_target_pairs={{0,4},{4,8},{8,12},{1,5},{5,9},{9,13},{2,6},{6,10},{10,14},{3,7},{... | collective-permute-start | bytes 589832 | tf_op jit(solution)/shard_map/ppermute | solution.py:174
  403.2 17.6 %collective-permute-start.25 = (bf16[1,96,1024]{2,1,0:T(8,128)(2,1)}, bf16[1,96,1024]{2,1,0:T(8,128)(2,1)S(1)}, u32[]{:S(2)}, u32[]{:S(2)}) collective-permute-start(bf16[1,96,1024]{2,1,0:T(8,128)(2,1)} %get-tuple-element.398), channel_id=1, source_target_pairs={{4,0},{8,4},{12,8},{5,1},{9,5},{13,9},{6,2},{10,6},{14,10},{7,3},{... | collective-permute-start | bytes 589832 | tf_op jit(solution)/shard_map/ppermute | solution.py:175
  418.2 24.1 %collective-permute-start.44 = (bf16[1,96,1024]{2,1,0:T(8,128)(2,1)}, bf16[1,96,1024]{2,1,0:T(8,128)(2,1)S(1)}, u32[]{:S(2)}, u32[]{:S(2)}) collective-permute-start(bf16[1,96,1024]{2,1,0:T(8,128)(2,1)} %get-tuple-element.417), channel_id=1, source_target_pairs={{0,4},{4,8},{8,12},{1,5},{5,9},{9,13},{2,6},{6,10},{10,14},{3,7},{... | collective-permute-start | bytes 589832 | tf_op jit(solution)/shard_map/ppermute | solution.py:174
  419.5 22.8 %collective-permute-start.45 = (bf16[1,96,1024]{2,1,0:T(8,128)(2,1)}, bf16[1,96,1024]{2,1,0:T(8,128)(2,1)}, u32[]{:S(2)}, u32[]{:S(2)}) collective-permute-start(bf16[1,96,1024]{2,1,0:T(8,128)(2,1)} %get-tuple-element.418), channel_id=1, source_target_pairs={{4,0},{8,4},{12,8},{5,1},{9,5},{13,9},{6,2},{10,6},{14,10},{7,3},{... | collective-permute-start | bytes 589832 | tf_op jit(solution)/shard_map/ppermute | solution.py:175
  434.5 27.5 %collective-permute-start.26 = (bf16[1,96,1024]{2,1,0:T(8,128)(2,1)}, bf16[1,96,1024]{2,1,0:T(8,128)(2,1)}, u32[]{:S(2)}, u32[]{:S(2)}) collective-permute-start(bf16[1,96,1024]{2,1,0:T(8,128)(2,1)} %get-tuple-element.399), channel_id=1, source_target_pairs={{0,4},{4,8},{8,12},{1,5},{5,9},{9,13},{2,6},{6,10},{10,14},{3,7},{... | collective-permute-start | bytes 589832 | tf_op jit(solution)/shard_map/ppermute | solution.py:174
  436.5 25.5 %collective-permute-start.27 = (bf16[1,96,1024]{2,1,0:T(8,128)(2,1)}, bf16[1,96,1024]{2,1,0:T(8,128)(2,1)}, u32[]{:S(2)}, u32[]{:S(2)}) collective-permute-start(bf16[1,96,1024]{2,1,0:T(8,128)(2,1)} %get-tuple-element.400), channel_id=1, source_target_pairs={{4,0},{8,4},{12,8},{5,1},{9,5},{13,9},{6,2},{10,6},{14,10},{7,3},{... | collective-permute-start | bytes 589832 | tf_op jit(solution)/shard_map/ppermute | solution.py:175
  456.0 29.1 %collective-permute-start.46 = (bf16[1,96,1024]{2,1,0:T(8,128)(2,1)}, bf16[1,96,1024]{2,1,0:T(8,128)(2,1)}, u32[]{:S(2)}, u32[]{:S(2)}) collective-permute-start(bf16[1,96,1024]{2,1,0:T(8,128)(2,1)} %get-tuple-element.419), channel_id=1, source_target_pairs={{0,4},{4,8},{8,12},{1,5},{5,9},{9,13},{2,6},{6,10},{10,14},{3,7},{... | collective-permute-start | bytes 589832 | tf_op jit(solution)/shard_map/ppermute | solution.py:174
  460.7 24.4 %collective-permute-start.47 = (bf16[1,96,1024]{2,1,0:T(8,128)(2,1)}, bf16[1,96,1024]{2,1,0:T(8,128)(2,1)}, u32[]{:S(2)}, u32[]{:S(2)}) collective-permute-start(bf16[1,96,1024]{2,1,0:T(8,128)(2,1)} %get-tuple-element.420), channel_id=1, source_target_pairs={{4,0},{8,4},{12,8},{5,1},{9,5},{13,9},{6,2},{10,6},{14,10},{7,3},{... | collective-permute-start | bytes 589832 | tf_op jit(solution)/shard_map/ppermute | solution.py:175
  475.7 29.0 %collective-permute-start.28 = (bf16[1,96,1024]{2,1,0:T(8,128)(2,1)}, bf16[1,96,1024]{2,1,0:T(8,128)(2,1)}, u32[]{:S(2)}, u32[]{:S(2)}) collective-permute-start(bf16[1,96,1024]{2,1,0:T(8,128)(2,1)} %get-tuple-element.401), channel_id=1, source_target_pairs={{0,4},{4,8},{8,12},{1,5},{5,9},{9,13},{2,6},{6,10},{10,14},{3,7},{... | collective-permute-start | bytes 589832 | tf_op jit(solution)/shard_map/ppermute | solution.py:174
  480.4 24.4 %collective-permute-start.29 = (bf16[1,96,1024]{2,1,0:T(8,128)(2,1)}, bf16[1,96,1024]{2,1,0:T(8,128)(2,1)}, u32[]{:S(2)}, u32[]{:S(2)}) collective-permute-start(bf16[1,96,1024]{2,1,0:T(8,128)(2,1)} %get-tuple-element.402), channel_id=1, source_target_pairs={{4,0},{8,4},{12,8},{5,1},{9,5},{13,9},{6,2},{10,6},{14,10},{7,3},{... | collective-permute-start | bytes 589832 | tf_op jit(solution)/shard_map/ppermute | solution.py:175
  516.1 47.5 %all-to-all-start.1 = ((bf16[4,1,96,1024]{3,2,1,0:T(8,128)(2,1)}), bf16[4,1,96,1024]{3,2,1,0:T(8,128)(2,1)S(1)}, u32[]{:S(2)}, u32[]{:S(2)}) async-start(bf16[4,1,96,1024]{3,2,1,0:T(8,128)(2,1)} %get-tuple-element.528), calls=%async_computation.1 | async-start | bytes 1572864 | tf_op jit(solution)/shard_map/all_to_all | solution.py:211
  564.5 14.3 %all-to-all-start.7 = ((bf16[4,1,96,1024]{3,2,1,0:T(8,128)(2,1)}), bf16[4,1,96,1024]{3,2,1,0:T(8,128)(2,1)S(1)}, u32[]{:S(2)}, u32[]{:S(2)}) async-start(bf16[4,1,96,1024]{3,2,1,0:T(8,128)(2,1)} %get-tuple-element.530), calls=%async_computation.7 | async-start | bytes 1572864 | tf_op jit(solution)/shard_map/all_to_all | solution.py:211
  579.7 41.7 %all-to-all-start.4 = ((bf16[16,24,1024]{2,1,0:T(8,128)(2,1)}), bf16[16,24,1024]{2,1,0:T(8,128)(2,1)S(1)}, u32[]{:S(2)}, u32[]{:S(2)}) async-start(bf16[16,24,1024]{2,1,0:T(8,128)(2,1)} %bitcast.137), calls=%async_computation.4 | async-start | bytes 1572864 | tf_op jit(solution)/shard_map/all_to_all | solution.py:211
  621.4 24.2 %all-to-all-start.10 = ((bf16[16,24,1024]{2,1,0:T(8,128)(2,1)}), bf16[16,24,1024]{2,1,0:T(8,128)(2,1)S(1)}, u32[]{:S(2)}, u32[]{:S(2)}) async-start(bf16[16,24,1024]{2,1,0:T(8,128)(2,1)} %bitcast.60), calls=%async_computation.10 | async-start | bytes 1572864 | tf_op jit(solution)/shard_map/all_to_all | solution.py:211
  645.6 24.2 %all-to-all-start.5 = ((bf16[16,24,1024]{2,1,0:T(8,128)(2,1)}), bf16[16,24,1024]{2,1,0:T(8,128)(2,1)S(1)}, u32[]{:S(2)}, u32[]{:S(2)}) async-start(bf16[16,24,1024]{2,1,0:T(8,128)(2,1)} %broadcast_select_fusion.3), calls=%async_computation.5 | async-start | bytes 1572864 | tf_op jit(solution)/shard_map/all_to_all | solution.py:211
  669.8 24.2 %all-to-all-start.11 = ((bf16[16,24,1024]{2,1,0:T(8,128)(2,1)}), bf16[16,24,1024]{2,1,0:T(8,128)(2,1)S(1)}, u32[]{:S(2)}, u32[]{:S(2)}) async-start(bf16[16,24,1024]{2,1,0:T(8,128)(2,1)} %broadcast_select_fusion.2), calls=%async_computation.11 | async-start | bytes 1572864 | tf_op jit(solution)/shard_map/all_to_all | solution.py:211
  (23 other events, 272.9 us)

commit v2 on v1

v2 whole, which is shorter than its diff:
```python
import functools
import math

import jax
import jax.numpy as jnp
from jax import lax
from jax.experimental import pallas as pl
from jax.experimental.pallas import tpu as pltpu
from jax.sharding import Mesh, PartitionSpec as P

EPSILON = 1e-06
LEVEL = ("x", "core")
GROUP = ("z", "x", "core")
EXTRA = 2
LAG = 2
LONGEST = 16


def dot(left, right, left_dim, right_dim):
    return lax.dot_general(left, right, (((left_dim,), (right_dim,)), ((), ())), preferred_element_type=jnp.float32)


def round_kernel(tiles, live_ref, blocks_ref, rates_ref, first_ref, third_ref, second_ref, *refs):
    result_ref, fresh_ref, stepped_ref, held_ref, turned_ref, values_ref, old_ref, new_ref = refs
    new_first, new_third, new_second = (fresh_ref.at[0, member] for member in range(3))
    lanes, _, part, width = blocks_ref.shape
    rows = lanes * part
    tile = first_ref.shape[-1]
    mean = 1.0 / width
    number = pl.program_id(0)

    def columns_of(index):
        start = index * tile
        return pl.ds(start if isinstance(index, int) else pl.multiple_of(start, tile), tile)

    def block(index):
        return blocks_ref[:, index].reshape(rows, width)

    @pl.when(number == 0)
    def _():
        turned_ref[...] = block(0).T
        values_ref[...] = (rates_ref[...] * block(1).astype(jnp.float32)).astype(jnp.bfloat16)
        old_ref[...] = jnp.zeros_like(old_ref)
        new_ref[...] = jnp.zeros_like(new_ref)

    def renorm(before, gradient):
        before = before.astype(jnp.float32)
        stepped = before - gradient
        old = jnp.sqrt(jnp.sum(before * before, axis=0, keepdims=True) * mean + EPSILON)
        new = jnp.sqrt(jnp.sum(stepped * stepped, axis=0, keepdims=True) * mean + EPSILON)
        return (stepped * (old / new)).astype(jnp.bfloat16)

    columns = columns_of(number)
    first, third, second = first_ref[0, 0], third_ref[0, 0], second_ref[0, 0]
    keys, values = block(0), values_ref[...]
    gate = dot(keys, first, 1, 0)
    upward = dot(keys, third, 1, 0)
    sigmoid = jax.nn.sigmoid(gate)
    active = gate * sigmoid
    hidden = (active * upward).astype(jnp.bfloat16)
    slope = sigmoid * (1.0 + gate * (1.0 - sigmoid))
    grad_hidden = -dot(values, second, 1, 1)
    grad_gate = (grad_hidden * upward * slope).astype(jnp.bfloat16)
    grad_up = (grad_hidden * active).astype(jnp.bfloat16)
    new_first[:, columns] = renorm(first, dot(turned_ref[...], grad_gate, 1, 0))
    new_third[:, columns] = renorm(third, dot(turned_ref[...], grad_up, 1, 0))
    before = second.astype(jnp.float32)
    stepped = before + dot(hidden, values, 0, 0)
    stepped_ref[columns, :] = stepped
    old_ref[...] += jnp.sum(before * before, axis=0, keepdims=True)
    new_ref[...] += jnp.sum(stepped * stepped, axis=0, keepdims=True)

    @pl.when(number == tiles - 1)
    def _():
        factor = jnp.sqrt(old_ref[...] * mean + EPSILON) / jnp.sqrt(new_ref[...] * mean + EPSILON)
        for index in range(tiles):
            columns = columns_of(index)
            new_second[columns, :] = (stepped_ref[columns, :] * factor).astype(jnp.bfloat16)
            gate = dot(block(2), new_first[:, columns], 1, 0)
            upward = dot(block(2), new_third[:, columns], 1, 0)
            held_ref[:, columns] = (gate * jax.nn.sigmoid(gate) * upward).astype(jnp.bfloat16)
        live = live_ref[0] > 0
        for index in range(width // tile):
            columns = columns_of(index)
            out = dot(held_ref[...], new_second[:, columns], 1, 0)
            result_ref[:, columns] = jnp.where(live, out, 0.0).astype(jnp.bfloat16)


def run_document(live, blocks, rates, weights, keep):
    lanes, _, part, width = blocks.shape
    rows = lanes * part
    hidden_width = weights.shape[-1]
    tile = math.gcd(256, hidden_width)
    tiles = hidden_width // tile
    whole = pl.BlockSpec(memory_space=pltpu.VMEM)
    result = jax.ShapeDtypeStruct((rows, width), jnp.bfloat16)
    fresh = (1, 3, hidden_width, width)
    spots = [
        pl.BlockSpec((1, 1, width, tile), lambda i: (0, 0, 0, i)),
        pl.BlockSpec((1, 1, width, tile), lambda i: (0, 1, 0, i)),
        pl.BlockSpec((1, 1, tile, width), lambda i: (0, 2, i, 0)),
    ]
    scratch = [
        pltpu.VMEM((hidden_width, width), jnp.float32),
        pltpu.VMEM((rows, hidden_width), jnp.bfloat16),
        pltpu.VMEM((width, rows), jnp.bfloat16),
        pltpu.VMEM((rows, width), jnp.bfloat16),
        pltpu.VMEM((1, width), jnp.float32),
        pltpu.VMEM((1, width), jnp.float32),
    ]
    if not keep:
        scratch = [pltpu.VMEM(fresh, jnp.bfloat16)] + scratch
    return pl.pallas_call(
        functools.partial(round_kernel, tiles),
        grid=(tiles,),
        in_specs=[pl.BlockSpec(memory_space=pltpu.SMEM), whole, whole] + spots,
        out_specs=(whole,) + ((pl.BlockSpec(fresh, lambda i: (0, 0, 0, 0)),) if keep else ()),
        out_shape=(result,) + ((jax.ShapeDtypeStruct(fresh, jnp.bfloat16),) if keep else ()),
        scratch_shapes=scratch,
        compiler_params=pltpu.CompilerParams(vmem_limit_bytes=36 << 20),
        cost_estimate=pl.CostEstimate(
            flops=18 * rows * width * hidden_width,
            transcendentals=2 * rows * hidden_width,
            bytes_accessed=12 * width * hidden_width + 8 * rows * width,
        ),
        name="run_document",
    )(live.reshape(1), blocks, rates.reshape(rows, 1), weights, weights, weights)


def inverse_of(permuted):
    count = permuted.shape[0]
    labels = jnp.arange(count, dtype=jnp.int32)
    return jnp.sum(jnp.where(permuted[None, :] == labels[:, None], labels[None, :], 0), axis=1)


def schedule_kernel(levels, lanes, horizon, level_ref, items_ref, table_ref):
    problems, _, count = items_ref.shape
    rows = 2 * levels
    shape = (rows, count)
    row = lax.broadcasted_iota(jnp.int32, shape, 0)
    item = lax.broadcasted_iota(jnp.int32, shape, 1)
    right = row < levels
    level = jnp.where(right, row, row - levels)
    heading = jnp.where(right, 1, -1)
    mine = level_ref[0]
    column = lax.broadcasted_iota(jnp.int32, (1, table_ref.shape[2]), 1)
    last = 2 * horizon + lanes
    for problem in range(problems):
        source = jnp.broadcast_to(items_ref[problem, 0:1, :], shape)
        target = jnp.broadcast_to(items_ref[problem, 1:2, :], shape)
        lane = jnp.broadcast_to(items_ref[problem, 2:3, :], shape)
        live = jnp.broadcast_to(items_ref[problem, 4:5, :], shape)
        present = jnp.where(level == source, live, 0) * jnp.where((target - source) * heading > 0, 1, 0)
        index = lane
        following = jnp.where(right, level + 1, level - 1)
        urgency = jnp.abs(target - level) * count + item + 1
        final = items_ref[problem, 2:3, :]
        table = jnp.zeros(column.shape, jnp.int32)
        needed = jnp.zeros((1, 1), jnp.int32)
        for step in range(horizon):
            key = jnp.where(present > 0, urgency, 0)
            best = jnp.max(key, axis=1, keepdims=True)
            chosen = jnp.where((key == best) & (present > 0), 1, 0)
            own_row = jnp.where(row == mine, chosen * index, 0)
            sent_right = jnp.max(jnp.max(own_row, axis=1, keepdims=True), axis=0, keepdims=True)
            own_row = jnp.where(row == levels + mine, chosen * index, 0)
            sent_left = jnp.max(jnp.max(own_row, axis=1, keepdims=True), axis=0, keepdims=True)
            table = jnp.where(column == step, sent_right, table)
            table = jnp.where(column == horizon + step, sent_left, table)
            busy = jnp.max(best, axis=0, keepdims=True)
            needed = jnp.where(busy > 0, step + 1, needed)
            arrived = jnp.where(target == following, chosen, 0)
            mark = jnp.where(right, lanes + step, lanes + horizon + step)
            landed = jnp.max(arrived * mark, axis=0, keepdims=True)
            final = jnp.where(landed > 0, landed, final)
            moving = chosen - arrived
            moved = pltpu.roll(jnp.where(right, moving, 0), 1, 0)
            moved += pltpu.roll(jnp.where(right, 0, moving), rows - 1, 0)
            present = present - chosen + moved
            index = jnp.where(moved > 0, lanes + step, index)
        left = jnp.max(jnp.max(present, axis=1, keepdims=True), axis=0, keepdims=True)
        needed = jnp.where(left > 0, horizon + 1, needed)
        table = jnp.where(column == last, needed, table)
        for lane_here in range(lanes):
            kept = (items_ref[problem, 1:2, :] == mine) & (items_ref[problem, 3:4, :] == lane_here)
            value = jnp.max(jnp.where(kept, final, 0), axis=1, keepdims=True)
            table = jnp.where(column == 2 * horizon + lane_here, value, table)
        table_ref[problem] = table


def plan_routes(levels, lanes, horizon, my_level, targets, live):
    problems, count = targets.shape
    sources = jnp.broadcast_to(jnp.arange(count, dtype=jnp.int32), targets.shape)
    items = jnp.stack([sources // lanes, targets // lanes, sources % lanes, targets % lanes, live], axis=1)
    columns = -(-(2 * horizon + lanes + 1) // 128) * 128
    return pl.pallas_call(
        functools.partial(schedule_kernel, levels, lanes, horizon),
        out_shape=jax.ShapeDtypeStruct((problems, 1, columns), jnp.int32),
        in_specs=[pl.BlockSpec(memory_space=pltpu.SMEM), pl.BlockSpec(memory_space=pltpu.VMEM)],
        name="plan_routes",
    )(my_level.reshape(1), items).reshape(problems, columns)


def pick_kernel(layout, sizes, problem, *refs):
    index_ref = refs[0]
    ins = refs[1 : 1 + len(sizes)]
    outs = refs[1 + len(sizes) : -1]
    sems = refs[-1]
    candidates = []
    for ref, size in zip(ins, sizes):
        candidates.extend([ref] if size is None else [ref.at[lane] for lane in range(size)])
    slots = []
    for number, (slot_count, first, allowed) in enumerate(layout):
        for slot in range(max(slot_count, 1)):
            place = outs[number] if slot_count == 0 else outs[number].at[slot]
            slots.append((place, first + slot, allowed))
    for slot, (place, entry, allowed) in enumerate(slots):
        wanted = index_ref[problem, entry]
        for value, position in allowed:

            @pl.when(wanted == value)
            def _():
                pltpu.make_async_copy(candidates[position], place, sems.at[slot]).start()

    for slot, (place, _, allowed) in enumerate(slots):
        pltpu.make_async_copy(candidates[allowed[0][1]], place, sems.at[slot]).wait()


def pick(table, problem, own, arrays, layout):
    item = own.shape[1:]
    sizes = [own.shape[0]] + [None] * len(arrays)
    total = sum(max(slot_count, 1) for slot_count, _, _ in layout)
    item_bytes = math.prod(item) * own.dtype.itemsize
    return pl.pallas_call(
        functools.partial(pick_kernel, layout, sizes, problem),
        out_shape=tuple(
            jax.ShapeDtypeStruct(((slot_count,) if slot_count else ()) + item, own.dtype) for slot_count, _, _ in layout
        ),
        in_specs=[pl.BlockSpec(memory_space=pltpu.SMEM)] + [pl.BlockSpec(memory_space=pl.ANY)] * (1 + len(arrays)),
        out_specs=tuple(pl.BlockSpec(memory_space=pltpu.VMEM) for _ in layout),
        scratch_shapes=[pltpu.SemaphoreType.DMA((total,))],
        compiler_params=pltpu.CompilerParams(vmem_limit_bytes=16 << 20),
        cost_estimate=pl.CostEstimate(flops=0, transcendentals=0, bytes_accessed=4 * total * item_bytes),
        name="pick_items",
    )(table, own, *arrays)


class Order:
    def __init__(self):
        self.last = ()

    def add(self, *values):
        self.last = values

    def follow(self, value):
        return after(value, *self.last) if self.last else value


def exchange(pieces, axes):
    return lax.all_to_all(pieces, axes, split_axis=0, concat_axis=0, tiled=True)


def spread(own, doc_of, levels):
    lanes, blocks, part, width = own.shape
    pieces = jnp.moveaxis(own.reshape(lanes, blocks, levels, part // levels, width), 2, 0)
    dealt = exchange(pieces, "z").reshape(levels * lanes, blocks, part // levels, width)
    placed = jnp.take(dealt, doc_of, axis=0).reshape(pieces.shape)
    return jnp.moveaxis(exchange(placed, "z"), 0, 2).reshape(own.shape)


class Route:
    def __init__(self, own, table, problem, doc_of, steps, horizon, levels):
        self.own, self.table, self.problem, self.doc_of = own, table, problem, doc_of
        self.steps, self.horizon, self.levels = steps, horizon, levels
        self.rights, self.lefts = [], []

    def step(self, order):
        self.rights, self.lefts = self.stepped(self.rights, self.lefts, self.own, self.table, order)

    def stepped(self, rights, lefts, own, table, order=None):
        ways = (0, [(i, i + 1) for i in range(self.levels - 1)]), (self.horizon, [(i + 1, i) for i in range(self.levels - 1)])
        came = []
        for arrivals, (first, pairs) in zip((rights, lefts), ways):
            lanes, count = own.shape[0], len(arrivals)
            allowed = [(index, index) for index in range(lanes + count)]
            entries = order.follow(table) if order else table
            (outgoing,) = pick(entries, self.problem, own, arrivals, ((0, first + count, allowed),))
            if order:
                order.add(outgoing)
            came.append(arrivals + [lax.ppermute(outgoing, "z", pairs)])
        return came

    def settle(self, rights, lefts, own, table):
        lanes, count = own.shape[0], len(rights)
        allowed = [(lane, lane) for lane in range(lanes)]
        allowed += [(lanes + t, lanes + t) for t in range(count)]
        allowed += [(lanes + self.horizon + t, lanes + count + t) for t in range(count)]
        return pick(table, self.problem, own, rights + lefts, ((lanes, 2 * self.horizon, allowed),))[0]

    def finish(self, rights, lefts, own, table):
        lanes = own.shape[0]

        def more(rights, lefts, own, table):
            if len(rights) == self.horizon:
                return spread(own, self.doc_of, self.levels)
            rights, lefts = self.stepped(rights, lefts, own, table)
            return self.finish(rights, lefts, own, table)

        needed = table[self.problem, 2 * self.horizon + lanes]
        return lax.cond(needed > len(rights), more, self.settle, rights, lefts, own, table)

    def result(self, *earlier):
        table = after(self.table, *earlier) if earlier else self.table
        return self.finish(self.rights, self.lefts, self.own, table)


def pack_kernel(*refs):
    out_ref = refs[-1]
    for number, ref in enumerate(refs[:-1]):
        out_ref[0, number] = ref[0, 0]


def pack(section, lanes, blocks):
    block_rows, width = blocks[0].shape[2:]
    part = block_rows // lanes
    shape = (lanes, len(blocks), part, width)
    return pl.pallas_call(
        pack_kernel,
        grid=(lanes,),
        in_specs=[pl.BlockSpec((1, 1, part, width), lambda lane: (section, 0, lane, 0)) for _ in blocks],
        out_specs=pl.BlockSpec((1,) + shape[1:], lambda lane: (lane, 0, 0, 0)),
        out_shape=jax.ShapeDtypeStruct(shape, blocks[0].dtype),
        cost_estimate=pl.CostEstimate(flops=0, transcendentals=0, bytes_accessed=4 * math.prod(shape)),
        name="pack_blocks",
    )(*blocks)


def after(value, *others):
    return lax.optimization_barrier((value,) + others)[0]


def body(state, keys, values, queries, rates, remaining, first_owner, migration):
    levels = lax.axis_size("z")
    lanes = lax.axis_size(LEVEL)
    devices = levels * lanes
    myself = lax.axis_index(GROUP)
    my_level = lax.axis_index("z")
    block_rows, width = keys.shape[2], keys.shape[3]
    piece_rows = block_rows // devices
    packed_first = pack(0, lanes, (keys, values, queries))
    own_first = exchange(packed_first, LEVEL)

    doc_first = inverse_of(first_owner)
    doc_here = doc_first[myself]
    steps = (devices // 4 + 1, devices // 8 + 1)
    horizon = steps[0] + EXTRA
    has_second = (remaining >= 2).astype(jnp.int32)
    rates_here = lax.dynamic_index_in_dim(rates, doc_here, 1, keepdims=False)
    source_of = inverse_of(migration)
    blocks = (keys, values, queries)

    if horizon > LONGEST:
        own_second = exchange(pack(1, lanes, blocks), LEVEL)
        blocks_first = exchange(spread(own_first, doc_first, levels), LEVEL)
        blocks_second = exchange(spread(own_second, doc_first, levels), LEVEL)
    else:
        targets = jnp.stack([first_owner, first_owner])
        live = jnp.stack([jnp.ones_like(has_second), has_second])
        table = plan_routes(levels, lanes, horizon, my_level, targets, live)
        first = Route(own_first, table, 0, doc_first, steps[0], horizon, levels)
        order = Order()
        first.step(order)
        own_second = exchange(order.follow(after(pack(1, lanes, blocks), table)), LEVEL)
        second = Route(own_second, table, 1, doc_first, steps[1], horizon, levels)
        for step in range(1, max(steps[0], steps[1] + LAG)):
            if step >= LAG and step - LAG < steps[1]:
                second.step(order)
            if step < steps[0]:
                first.step(order)
        blocks_first = exchange(first.result(second.rights[-1], second.lefts[-1]), LEVEL)
        blocks_second = exchange(second.result(), LEVEL)

    always = jnp.ones((), jnp.int32)
    result_one, updated = run_document(always, blocks_first, rates_here[0], state, True)
    dealt_one = exchange(result_one.reshape(devices, piece_rows, width), GROUP)
    (result_two,) = run_document(has_second[doc_here], blocks_second, rates_here[1], updated, False)
    both = jnp.stack([jnp.take(dealt_one, first_owner, axis=0), result_two.reshape(devices, piece_rows, width)], axis=1)
    both = exchange(both, GROUP)
    round_one, dealt_two = both[:, 0], both[:, 1]
    round_two = exchange(jnp.take(dealt_two, source_of, axis=0), GROUP)
    return round_one.reshape(1, block_rows, width), round_two.reshape(1, block_rows, width)


def solution(mesh):
    groups, along, cores = (mesh.shape[name] for name in ("grp", "seq", "doc"))
    wide = max(d for d in range(1, along + 1) if along % d == 0 and d**3 <= along)
    fine = Mesh(mesh.devices.reshape(groups, along // wide, wide, cores), ("grp",) + GROUP)
    everywhere = ("grp",) + GROUP
    return jax.shard_map(
        body,
        mesh=fine,
        in_specs=(
            P(everywhere, None, None, None),
            P(None, everywhere, None, None),
            P(None, everywhere, None, None),
            P(None, everywhere, None, None),
            P(None, "grp", None),
            P("grp"),
            P("grp"),
            P("grp"),
        ),
        out_specs=(P(everywhere, None, None), P(everywhere, None, None)),
        check_vma=False,
    )
```

time: 691 us -> 333 us (0.48); the launches traced: 703 us -> 331 us
  starting transfers between devices: 262 us -> 69.6 us
  Pallas kernels: 219 us -> 63.6 us
  blocking collectives: 0 us -> 63.2 us
  matrix products: 59.4 us -> 0 us
  other arithmetic: 29.8 us -> 2.4 us
  waiting for transfers between devices: 89.6 us -> 109 us
  between operations: 20.3 us -> 4.37 us
    pallas_call x22, Pallas kernels: 216 us -> 61.6 us  [the longest x2 27 us: run_document(): pl.pallas_call(functools.partial(round_kernel, tiles), grid=(tiles,), in_...]
    ppermute x36 -> x16, starting transfers between devices: 182 us -> 44.8 us  [stepped(): came.append(arrivals + [lax.ppermute(outgoing, 'z', pairs)])]
    all_to_all x0 -> x2, blocking collectives: none -> 63.2 us  [exchange(): return lax.all_to_all(pieces, axes, split_axis=0, concat_axis=0, tiled=True)]
    dot_general x16 -> x0, matrix products: 59.4 us -> none  [the longest x2 13.9 us: swiglu_apply(): return jnp.dot(hidden, weights[2], preferred_element_type=jnp.float32)]
    all_to_all x12 -> x5, starting transfers between devices: 79.8 us -> 24.8 us  [exchange(): return lax.all_to_all(pieces, axes, split_axis=0, concat_axis=0, tiled=True)]
    ppermute x36 -> x16, waiting for transfers between devices: 17.1 us -> 50 us  [stepped(): came.append(arrivals + [lax.ppermute(outgoing, 'z', pairs)])]
    another operation x13 -> x3, other arithmetic: 18 us -> 1.95 us  [the longest x2 1.43 us: body(): jnp.stack([jnp.take(dealt_one, first_owner, axis=0), result_two.reshape(d...]
    all_to_all x12 -> x5, waiting for transfers between devices: 72.5 us -> 59.1 us  [exchange(): return lax.all_to_all(pieces, axes, split_axis=0, concat_axis=0, tiled=True)]
  transfers between devices with their start and end apart: 48 -> 21, of which waited for: 11 -> 16; matrix products, arithmetic and copies ran while one was open for 15% -> 1% of each run, Pallas kernels for 31% -> 15%
where the time goes in v2:
time: 333 us; the launch traced here: 331 us
  waiting for transfers between devices  109 us (33%)
  starting transfers between devices  69.6 us (21%)
  Pallas kernels  63.6 us (19%)
  blocking collectives  63.2 us (19%)
  local copies, waits for them, and re-layouts  18.7 us (6%)
  between operations  4.37 us (1%)
    all_to_all x2, blocking collectives, exchange(): return lax.all_to_all(pieces, axes, split_axis=0, concat_axis=0, tiled=True)  63.2 us
    all_to_all x5, waiting for transfers between devices, exchange(): return lax.all_to_all(pieces, axes, split_axis=0, concat_axis=0, tiled=True)  59.1 us
    ppermute x16, waiting for transfers between devices, stepped(): came.append(arrivals + [lax.ppermute(outgoing, 'z', pairs)])  50 us
    ppermute x16, starting transfers between devices, stepped(): came.append(arrivals + [lax.ppermute(outgoing, 'z', pairs)])  44.8 us
    pallas_call x2, Pallas kernels, run_document(): pl.pallas_call(functools.partial(round_kernel, tiles), grid=(tiles,), in_...  27 us
    pallas_call x18, Pallas kernels, pick(): pl.pallas_call(functools.partial(pick_kernel, layout, sizes, problem), ou...  26.6 us
    all_to_all x5, starting transfers between devices, exchange(): return lax.all_to_all(pieces, axes, split_axis=0, concat_axis=0, tiled=True)  24.8 us
    unnamed x45, local copies, waits for them, and re-layouts  11.2 us
  transfers between devices with their start and end apart: 21, of which 16 were waited for; matrix products, arithmetic and copies ran while one was open for 1% of the time, Pallas kernels for 15%

profile of v2, /device:TPU:1, one launch (start us, length us, event | category | flops | bytes accessed | tf_op | source)
XLA Modules:
  0.0 331.2 jit_solution(11959862039931167379)
XLA Ops:
  0.6 4.0 %pack_blocks.2 = bf16[4,3,96,1024]{3,2,1,0:T(8,128)(2,1)} custom-call(bf16[2,1,384,1024]{3,2,1,0:T(8,128)(2,1)} %refs_0_.3, bf16[2,1,384,1024]{3,2,1,0:T(8,128)(2,1)} %refs_1_.3, bf16[2,1,384,1024]{3,2,1,0:T(8,128)(2,1)} %refs_2_.3), custom_call_target="tpu_custom_call" | custom-call | bytes 4718592 | tf_op jit(solution)/shard_map/pack_blocks/pallas_call | solution.py:327
  4.6 4.5 %all-to-all-start.4 = ((bf16[4,3,96,1024]{3,2,1,0:T(8,128)(2,1)}), bf16[4,3,96,1024]{3,2,1,0:T(8,128)(2,1)}, u32[]{:S(2)}, u32[]{:S(2)}) async-start(bf16[4,3,96,1024]{3,2,1,0:T(8,128)(2,1)} %pack_blocks.2), calls=%async_computation.4 | async-start | bytes 4718592 | tf_op jit(solution)/shard_map/all_to_all | solution.py:260
  9.2 4.0 %pack_blocks.3 = bf16[4,3,96,1024]{3,2,1,0:T(8,128)(2,1)} custom-call(bf16[2,1,384,1024]{3,2,1,0:T(8,128)(2,1)} %refs_0_.3, bf16[2,1,384,1024]{3,2,1,0:T(8,128)(2,1)} %refs_1_.3, bf16[2,1,384,1024]{3,2,1,0:T(8,128)(2,1)} %refs_2_.3), custom_call_target="tpu_custom_call" | custom-call | bytes 4718592 | tf_op jit(solution)/shard_map/pack_blocks/pallas_call | solution.py:327
  14.9 2.0 plan_routes.1
  17.0 20.1 %all-to-all-done.4.refs_1_ = bf16[4,3,96,1024]{3,2,1,0:T(8,128)(2,1)} async-done(((bf16[4,3,96,1024]{3,2,1,0:T(8,128)(2,1)}), bf16[4,3,96,1024]{3,2,1,0:T(8,128)(2,1)}, u32[]{:S(2)}, u32[]{:S(2)}) %all-to-all-start.4) | async-done | bytes 2359328 | tf_op jit(solution)/shard_map/all_to_all | solution.py:260
  37.1 1.6 pick_items.56
  38.7 1.6 pick_items.57
  40.4 4.9 %all-to-all-start.5 = ((bf16[4,3,96,1024]{3,2,1,0:T(8,128)(2,1)}), bf16[4,3,96,1024]{3,2,1,0:T(8,128)(2,1)S(1)}, u32[]{:S(2)}, u32[]{:S(2)}) async-start(bf16[4,3,96,1024]{3,2,1,0:T(8,128)(2,1)} %pack_blocks.3), calls=%async_computation.5 | async-start | bytes 4718592 | tf_op jit(solution)/shard_map/all_to_all | solution.py:260
  45.2 4.1 %collective-permute-start.12 = (bf16[3,96,1024]{2,1,0:T(8,128)(2,1)S(1)}, bf16[3,96,1024]{2,1,0:T(8,128)(2,1)S(1)}, u32[]{:S(2)}, u32[]{:S(2)}) collective-permute-start(bf16[3,96,1024]{2,1,0:T(8,128)(2,1)S(1)} %pick_items.56), channel_id=1, source_target_pairs={{0,4},{4,8},{8,12},{1,5},{5,9},{9,13},{2,6},{6,10},{10,14},{3,7},{... | collective-permute-start | bytes 1769480 | tf_op jit(solution)/shard_map/ppermute | solution.py:290
  50.6 11.3 %collective-permute-done.12.refs_2_ = bf16[3,96,1024]{2,1,0:T(8,128)(2,1)S(1)} collective-permute-done((bf16[3,96,1024]{2,1,0:T(8,128)(2,1)S(1)}, bf16[3,96,1024]{2,1,0:T(8,128)(2,1)S(1)}, u32[]{:S(2)}, u32[]{:S(2)}) %collective-permute-start.12) | collective-permute-done | bytes 589856 | tf_op jit(solution)/shard_map/ppermute | solution.py:290
  63.6 5.0 %collective-permute-start.14 = (bf16[3,96,1024]{2,1,0:T(8,128)(2,1)S(1)}, bf16[3,96,1024]{2,1,0:T(8,128)(2,1)}, u32[]{:S(2)}, u32[]{:S(2)}) collective-permute-start(bf16[3,96,1024]{2,1,0:T(8,128)(2,1)S(1)} %pick_items.58), channel_id=1, source_target_pairs={{0,4},{4,8},{8,12},{1,5},{5,9},{9,13},{2,6},{6,10},{10,14},{3,7},{... | collective-permute-start | bytes 1769480 | tf_op jit(solution)/shard_map/ppermute | solution.py:290
  68.6 1.6 pick_items.59
  73.6 4.2 %collective-permute-start.16 = (bf16[3,96,1024]{2,1,0:T(8,128)(2,1)S(1)}, bf16[3,96,1024]{2,1,0:T(8,128)(2,1)S(1)}, u32[]{:S(2)}, u32[]{:S(2)}) collective-permute-start(bf16[3,96,1024]{2,1,0:T(8,128)(2,1)S(1)} %pick_items.60), channel_id=1, source_target_pairs={{0,4},{4,8},{8,12},{1,5},{5,9},{9,13},{2,6},{6,10},{10,14},{3,7},{... | collective-permute-start | bytes 1769480 | tf_op jit(solution)/shard_map/ppermute | solution.py:290
  80.0 1.6 pick_items.62
  81.6 4.0 %collective-permute-start.18 = (bf16[3,96,1024]{2,1,0:T(8,128)(2,1)S(1)}, bf16[3,96,1024]{2,1,0:T(8,128)(2,1)S(1)}, u32[]{:S(2)}, u32[]{:S(2)}) collective-permute-start(bf16[3,96,1024]{2,1,0:T(8,128)(2,1)S(1)} %pick_items.62), channel_id=1, source_target_pairs={{0,4},{4,8},{8,12},{1,5},{5,9},{9,13},{2,6},{6,10},{10,14},{3,7},{... | collective-permute-start | bytes 1769480 | tf_op jit(solution)/shard_map/ppermute | solution.py:290
  85.9 1.6 pick_items.63
  88.9 3.3 collective-permute-done.16.refs_2_
  92.9 4.1 %collective-permute-start.20 = (bf16[3,96,1024]{2,1,0:T(8,128)(2,1)S(1)}, bf16[3,96,1024]{2,1,0:T(8,128)(2,1)S(1)}, u32[]{:S(2)}, u32[]{:S(2)}) collective-permute-start(bf16[3,96,1024]{2,1,0:T(8,128)(2,1)S(1)} %pick_items.64), channel_id=1, source_target_pairs={{0,4},{4,8},{8,12},{1,5},{5,9},{9,13},{2,6},{6,10},{10,14},{3,7},{... | collective-permute-start | bytes 1769480 | tf_op jit(solution)/shard_map/ppermute | solution.py:290
  100.5 4.3 %collective-permute-done.18.refs_4_ = bf16[3,96,1024]{2,1,0:T(8,128)(2,1)S(1)} collective-permute-done((bf16[3,96,1024]{2,1,0:T(8,128)(2,1)S(1)}, bf16[3,96,1024]{2,1,0:T(8,128)(2,1)S(1)}, u32[]{:S(2)}, u32[]{:S(2)}) %collective-permute-start.18) | collective-permute-done | bytes 589856 | tf_op jit(solution)/shard_map/ppermute | solution.py:290
  106.4 4.1 %collective-permute-start.24 = (bf16[3,96,1024]{2,1,0:T(8,128)(2,1)S(1)}, bf16[3,96,1024]{2,1,0:T(8,128)(2,1)S(1)}, u32[]{:S(2)}, u32[]{:S(2)}) collective-permute-start(bf16[3,96,1024]{2,1,0:T(8,128)(2,1)S(1)} %pick_items.66), channel_id=1, source_target_pairs={{0,4},{4,8},{8,12},{1,5},{5,9},{9,13},{2,6},{6,10},{10,14},{3,7},{... | collective-permute-start | bytes 1769480 | tf_op jit(solution)/shard_map/ppermute | solution.py:290
  111.1 1.6 pick_items.67
  114.0 3.4 %collective-permute-done.20.refs_3_ = bf16[3,96,1024]{2,1,0:T(8,128)(2,1)S(1)} collective-permute-done((bf16[3,96,1024]{2,1,0:T(8,128)(2,1)S(1)}, bf16[3,96,1024]{2,1,0:T(8,128)(2,1)S(1)}, u32[]{:S(2)}, u32[]{:S(2)}) %collective-permute-start.20) | collective-permute-done | bytes 589856 | tf_op jit(solution)/shard_map/ppermute | solution.py:290
  118.2 5.6 %collective-permute-done.22.refs_3_ = bf16[3,96,1024]{2,1,0:T(8,128)(2,1)S(1)} collective-permute-done((bf16[3,96,1024]{2,1,0:T(8,128)(2,1)S(1)}, bf16[3,96,1024]{2,1,0:T(8,128)(2,1)S(1)}, u32[]{:S(2)}, u32[]{:S(2)}) %collective-permute-start.22) | collective-permute-done | bytes 589856 | tf_op jit(solution)/shard_map/ppermute | solution.py:290
  125.8 4.8 %collective-permute-start.21 = (bf16[3,96,1024]{2,1,0:T(8,128)(2,1)S(1)}, bf16[3,96,1024]{2,1,0:T(8,128)(2,1)}, u32[]{:S(2)}, u32[]{:S(2)}) collective-permute-start(bf16[3,96,1024]{2,1,0:T(8,128)(2,1)S(1)} %pick_items.68), channel_id=1, source_target_pairs={{0,4},{4,8},{8,12},{1,5},{5,9},{9,13},{2,6},{6,10},{10,14},{3,7},{... | collective-permute-start | bytes 1769480 | tf_op jit(solution)/shard_map/ppermute | solution.py:290
  130.6 1.6 pick_items.70
  132.2 4.2 %collective-permute-done.26.refs_5_ = bf16[3,96,1024]{2,1,0:T(8,128)(2,1)S(1)} collective-permute-done((bf16[3,96,1024]{2,1,0:T(8,128)(2,1)S(1)}, bf16[3,96,1024]{2,1,0:T(8,128)(2,1)S(1)}, u32[]{:S(2)}, u32[]{:S(2)}) %collective-permute-start.26) | collective-permute-done | bytes 589856 | tf_op jit(solution)/shard_map/ppermute | solution.py:290
  139.3 4.0 %collective-permute-start.25 = (bf16[3,96,1024]{2,1,0:T(8,128)(2,1)S(1)}, bf16[3,96,1024]{2,1,0:T(8,128)(2,1)S(1)}, u32[]{:S(2)}, u32[]{:S(2)}) collective-permute-start(bf16[3,96,1024]{2,1,0:T(8,128)(2,1)S(1)} %pick_items.70), channel_id=1, source_target_pairs={{0,4},{4,8},{8,12},{1,5},{5,9},{9,13},{2,6},{6,10},{10,14},{3,7},{... | collective-permute-start | bytes 1769480 | tf_op jit(solution)/shard_map/ppermute | solution.py:290
  144.7 4.4 %collective-permute-done.23 = bf16[3,96,1024]{2,1,0:T(8,128)(2,1)} collective-permute-done((bf16[3,96,1024]{2,1,0:T(8,128)(2,1)S(1)}, bf16[3,96,1024]{2,1,0:T(8,128)(2,1)}, u32[]{:S(2)}, u32[]{:S(2)}) %collective-permute-start.23) | collective-permute-done | bytes 589856 | tf_op jit(solution)/shard_map/ppermute | solution.py:290
  150.4 11.3 %collective-permute-done.27 = bf16[3,96,1024]{2,1,0:T(8,128)(2,1)S(1)} collective-permute-done((bf16[3,96,1024]{2,1,0:T(8,128)(2,1)S(1)}, bf16[3,96,1024]{2,1,0:T(8,128)(2,1)S(1)}, u32[]{:S(2)}, u32[]{:S(2)}) %collective-permute-start.27) | collective-permute-done | bytes 589856 | tf_op jit(solution)/shard_map/ppermute | solution.py:290
  161.7 3.5 %conditional.8 = (bf16[4,3,96,1024]{3,2,1,0:T(8,128)(2,1)}) conditional(s32[]{:T(128)} %bitcast.26, (s32[2,128]{1,0:T(2,128)S(1)}, bf16[4,3,96,1024]{3,2,1,0:T(8,128)(2,1)}, bf16[3,96,1024]{2,1,0:T(8,128)(2,1)S(1)}, bf16[3,96,1024]{2,1,0:T(8,128)(2,1)}, bf16[3,96,1024]{2,1,0:T(8,128)(2,1)S(1)}, /*index=5*/bf16[3,96,1024]{2,1,0:T(8,128)(2,1)S(1)}, ...), branch_computations={%region_1.2_spmd, %region_2.8_spmd} | conditional | flops 1180820 | bytes 49550568 | solution.py:310
  161.7 3.5 %pick_items.36 = bf16[4,3,96,1024]{3,2,1,0:T(8,128)(2,1)} custom-call(s32[2,128]{1,0:T(2,128)S(1)} %get-tuple-element.290.refs_0_, bf16[4,3,96,1024]{3,2,1,0:T(8,128)(2,1)} %get-tuple-element.291.refs_1_, bf16[3,96,1024]{2,1,0:T(8,128)(2,1)S(1)} %get-tuple-element.292.refs_2_, bf16[3,96,1024]{2,1,0:T(8,128)(2,1)} %get-tuple-element.293.refs_3_, ...), custom_call_target="tpu_custom_call" | custom-call | bytes 9437184 | tf_op jit(solution)/shard_map/cond/branch_0_fun/pick_items/pallas_call | solution.py:234
  165.2 2.9 conditional.9
  165.2 2.7 pick_items.43
  168.1 34.0 %all_to_all.53.blocks_ref = bf16[4,3,96,1024]{3,2,1,0:T(8,128)(2,1)} all-to-all(bf16[4,3,96,1024]{3,2,1,0:T(8,128)(2,1)} %get-tuple-element.638), channel_id=1, replica_groups=mesh['grp'=2,'z'=4,'x'=2,'core'=2] {'x','core'}, dimensions={0} | all-to-all | bytes 4718592 | tf_op jit(solution)/shard_map/all_to_all | solution.py:260
  202.1 4.8 %all-to-all-start.8 = ((bf16[4,3,96,1024]{3,2,1,0:T(8,128)(2,1)}), bf16[4,3,96,1024]{3,2,1,0:T(8,128)(2,1)S(1)}, u32[]{:S(2)}, u32[]{:S(2)}) async-start(bf16[4,3,96,1024]{3,2,1,0:T(8,128)(2,1)} %get-tuple-element.639), calls=%async_computation.8 | async-start | bytes 4718592 | tf_op jit(solution)/shard_map/all_to_all | solution.py:260
  210.3 1.7 copy-done
  212.0 2.8 copy-done.1
  214.7 13.7 %run_document.2 = (bf16[384,1024]{1,0:T(8,128)(2,1)}, bf16[1,3,1024,1024]{3,2,1,0:T(8,128)(2,1)S(1)}) custom-call(s32[1]{0:T(128)} %constant.99.clone.1.live_ref, bf16[4,3,96,1024]{3,2,1,0:T(8,128)(2,1)S(1)} %copy-done, f32[384,1]{1,0:T(8,128)S(1)} %copy.34.rates_ref, bf16[1,3,1024,1024]{3,2,1,0:T(8,128)(2,1)S(1)} %copy-done.1, ...), custom_call_target="tpu_custom_call" | custom-call | flops 7247757312 | bytes 15728640 | tf_op jit(solution)/shard_map/run_document/pallas_call | solution.py:113
  228.4 2.6 copy-done.2
  231.0 3.5 %all-to-all-done.8.blocks_ref = bf16[4,3,96,1024]{3,2,1,0:T(8,128)(2,1)S(1)} async-done(((bf16[4,3,96,1024]{3,2,1,0:T(8,128)(2,1)}), bf16[4,3,96,1024]{3,2,1,0:T(8,128)(2,1)S(1)}, u32[]{:S(2)}, u32[]{:S(2)}) %all-to-all-start.8) | async-done | bytes 2359328 | tf_op jit(solution)/shard_map/all_to_all | solution.py:260
  234.5 4.9 %all-to-all-start.7 = ((bf16[16,24,1024]{2,1,0:T(8,128)(2,1)}), bf16[16,24,1024]{2,1,0:T(8,128)(2,1)}, u32[]{:S(2)}, u32[]{:S(2)}) async-start(bf16[16,24,1024]{2,1,0:T(8,128)(2,1)} %bitcast.29), calls=%async_computation.7 | async-start | bytes 1572864 | tf_op jit(solution)/shard_map/all_to_all | solution.py:260
  240.2 2.8 copy-done.3
  243.0 13.4 %run_document.3 = bf16[384,1024]{1,0:T(8,128)(2,1)S(1)} custom-call(s32[1]{0:T(128)} %dynamic_slice.12.live_ref, bf16[4,3,96,1024]{3,2,1,0:T(8,128)(2,1)S(1)} %all-to-all-done.8.blocks_ref, f32[384,1]{1,0:T(8,128)S(1)} %copy.35.rates_ref, bf16[1,3,1024,1024]{3,2,1,0:T(8,128)(2,1)S(1)} %copy-done.3, bf16[1,3,1024,1024]{3,2,1,0:T(8,128)(2,1)S(1)} %copy-done.3, ...), custom_call_target="tpu_custom_call" | custom-call | flops 7247757312 | bytes 15728640 | tf_op jit(solution)/shard_map/run_document/pallas_call | solution.py:113
  256.3 1.8 all-to-all-done.7
  258.1 1.7 gather_fusion.2
  261.3 5.7 %all-to-all-start.9 = ((bf16[16,2,24,1024]{3,2,1,0:T(8,128)(2,1)}), bf16[16,2,24,1024]{3,2,1,0:T(8,128)(2,1)S(1)}, u32[]{:S(2)}, u32[]{:S(2)}) async-start(bf16[16,2,24,1024]{3,2,1,0:T(8,128)(2,1)} %pad_maximum_fusion), calls=%async_computation.9 | async-start | bytes 3145728 | tf_op jit(solution)/shard_map/all_to_all | solution.py:260
  267.1 32.3 %all-to-all-done.9 = bf16[16,2,24,1024]{3,2,1,0:T(8,128)(2,1)S(1)} async-done(((bf16[16,2,24,1024]{3,2,1,0:T(8,128)(2,1)}), bf16[16,2,24,1024]{3,2,1,0:T(8,128)(2,1)S(1)}, u32[]{:S(2)}, u32[]{:S(2)}) %all-to-all-start.9) | async-done | bytes 1572896 | tf_op jit(solution)/shard_map/all_to_all | solution.py:260
  301.1 29.2 %all_to_all.54 = bf16[16,24,1024]{2,1,0:T(8,128)(2,1)S(1)} all-to-all(bf16[16,24,1024]{2,1,0:T(8,128)(2,1)S(1)} %broadcast_select_fusion.2), channel_id=1, replica_groups=mesh['grp'=2,'z'=4,'x'=2,'core'=2] {'z','x','core'}, dimensions={0} | all-to-all | bytes 1572864 | tf_op jit(solution)/shard_map/all_to_all | solution.py:260
  (97 shorter events, 32.7 us)
Async XLA Ops:
  4.6 32.5 %all-to-all-start.4 = ((bf16[4,3,96,1024]{3,2,1,0:T(8,128)(2,1)}), bf16[4,3,96,1024]{3,2,1,0:T(8,128)(2,1)}, u32[]{:S(2)}, u32[]{:S(2)}) async-start(bf16[4,3,96,1024]{3,2,1,0:T(8,128)(2,1)} %pack_blocks.2), calls=%async_computation.4 | async-start | bytes 4718592 | tf_op jit(solution)/shard_map/all_to_all | solution.py:260
  9.1 4.0 %copy-start.17 = (s32[16]{0:T(128)S(1)}, s32[16]{0:T(128)}, u32[]{:S(2)}) copy-start(s32[16]{0:T(128)} %param.33) | copy-start | bytes 196
  9.1 4.5 %copy-start.16 = (s32[16]{0:T(128)S(1)}, s32[16]{0:T(128)}, u32[]{:S(2)}) copy-start(s32[16]{0:T(128)} %param.34) | copy-start | bytes 196
  9.2 4.6 %copy-start.18 = (s32[16]{0:T(128)S(1)}, s32[16]{0:T(128)}, u32[]{:S(2)}) copy-start(s32[16]{0:T(128)} %param.35) | copy-start | bytes 196
  13.8 0.5 copy-start.19
  40.4 32.5 %all-to-all-start.5 = ((bf16[4,3,96,1024]{3,2,1,0:T(8,128)(2,1)}), bf16[4,3,96,1024]{3,2,1,0:T(8,128)(2,1)S(1)}, u32[]{:S(2)}, u32[]{:S(2)}) async-start(bf16[4,3,96,1024]{3,2,1,0:T(8,128)(2,1)} %pack_blocks.3), calls=%async_computation.5 | async-start | bytes 4718592 | tf_op jit(solution)/shard_map/all_to_all | solution.py:260
  45.2 16.7 %collective-permute-start.12 = (bf16[3,96,1024]{2,1,0:T(8,128)(2,1)S(1)}, bf16[3,96,1024]{2,1,0:T(8,128)(2,1)S(1)}, u32[]{:S(2)}, u32[]{:S(2)}) collective-permute-start(bf16[3,96,1024]{2,1,0:T(8,128)(2,1)S(1)} %pick_items.56), channel_id=1, source_target_pairs={{0,4},{4,8},{8,12},{1,5},{5,9},{9,13},{2,6},{6,10},{10,14},{3,7},{... | collective-permute-start | bytes 1769480 | tf_op jit(solution)/shard_map/ppermute | solution.py:290
  49.3 19.2 %collective-permute-start.13 = (bf16[3,96,1024]{2,1,0:T(8,128)(2,1)S(1)}, bf16[3,96,1024]{2,1,0:T(8,128)(2,1)S(1)}, u32[]{:S(2)}, u32[]{:S(2)}) collective-permute-start(bf16[3,96,1024]{2,1,0:T(8,128)(2,1)S(1)} %pick_items.57), channel_id=1, source_target_pairs={{4,0},{8,4},{12,8},{5,1},{9,5},{13,9},{6,2},{10,6},{14,10},{7,3},{... | collective-permute-start | bytes 1769480 | tf_op jit(solution)/shard_map/ppermute | solution.py:290
  62.0 8.2 %copy-start.12 = (bf16[3,96,1024]{2,1,0:T(8,128)(2,1)}, bf16[3,96,1024]{2,1,0:T(8,128)(2,1)S(1)}, u32[]{:S(2)}) copy-start(bf16[3,96,1024]{2,1,0:T(8,128)(2,1)S(1)} %collective-permute-done.12.refs_2_) | copy-start | bytes 1769476
  63.6 16.3 %collective-permute-start.14 = (bf16[3,96,1024]{2,1,0:T(8,128)(2,1)S(1)}, bf16[3,96,1024]{2,1,0:T(8,128)(2,1)}, u32[]{:S(2)}, u32[]{:S(2)}) collective-permute-start(bf16[3,96,1024]{2,1,0:T(8,128)(2,1)S(1)} %pick_items.58), channel_id=1, source_target_pairs={{0,4},{4,8},{8,12},{1,5},{5,9},{9,13},{2,6},{6,10},{10,14},{3,7},{... | collective-permute-start | bytes 1769480 | tf_op jit(solution)/shard_map/ppermute | solution.py:290
  68.6 1.6 copy-start.14
  70.2 15.7 %collective-permute-start.15 = (bf16[3,96,1024]{2,1,0:T(8,128)(2,1)S(1)}, bf16[3,96,1024]{2,1,0:T(8,128)(2,1)}, u32[]{:S(2)}, u32[]{:S(2)}) collective-permute-start(bf16[3,96,1024]{2,1,0:T(8,128)(2,1)S(1)} %pick_items.59), channel_id=1, source_target_pairs={{4,0},{8,4},{12,8},{5,1},{9,5},{13,9},{6,2},{10,6},{14,10},{7,3},{... | collective-permute-start | bytes 1769480 | tf_op jit(solution)/shard_map/ppermute | solution.py:290
  72.9 7.1 %copy-start.13 = (bf16[3,96,1024]{2,1,0:T(8,128)(2,1)S(1)}, bf16[3,96,1024]{2,1,0:T(8,128)(2,1)}, u32[]{:S(2)}) copy-start(bf16[3,96,1024]{2,1,0:T(8,128)(2,1)} %copy-done.12) | copy-start | bytes 1769476
  73.6 18.6 %collective-permute-start.16 = (bf16[3,96,1024]{2,1,0:T(8,128)(2,1)S(1)}, bf16[3,96,1024]{2,1,0:T(8,128)(2,1)S(1)}, u32[]{:S(2)}, u32[]{:S(2)}) collective-permute-start(bf16[3,96,1024]{2,1,0:T(8,128)(2,1)S(1)} %pick_items.60), channel_id=1, source_target_pairs={{0,4},{4,8},{8,12},{1,5},{5,9},{9,13},{2,6},{6,10},{10,14},{3,7},{... | collective-permute-start | bytes 1769480 | tf_op jit(solution)/shard_map/ppermute | solution.py:290
  78.5 7.4 %copy-start.15 = (bf16[3,96,1024]{2,1,0:T(8,128)(2,1)S(1)}, bf16[3,96,1024]{2,1,0:T(8,128)(2,1)}, u32[]{:S(2)}) copy-start(bf16[3,96,1024]{2,1,0:T(8,128)(2,1)} %copy-done.14) | copy-start | bytes 1769476
  78.5 19.9 %collective-permute-start.17 = (bf16[3,96,1024]{2,1,0:T(8,128)(2,1)S(1)}, bf16[3,96,1024]{2,1,0:T(8,128)(2,1)S(1)}, u32[]{:S(2)}, u32[]{:S(2)}) collective-permute-start(bf16[3,96,1024]{2,1,0:T(8,128)(2,1)S(1)} %pick_items.61), channel_id=1, source_target_pairs={{4,0},{8,4},{12,8},{5,1},{9,5},{13,9},{6,2},{10,6},{14,10},{7,3},{... | collective-permute-start | bytes 1769480 | tf_op jit(solution)/shard_map/ppermute | solution.py:290
  81.6 23.2 %collective-permute-start.18 = (bf16[3,96,1024]{2,1,0:T(8,128)(2,1)S(1)}, bf16[3,96,1024]{2,1,0:T(8,128)(2,1)S(1)}, u32[]{:S(2)}, u32[]{:S(2)}) collective-permute-start(bf16[3,96,1024]{2,1,0:T(8,128)(2,1)S(1)} %pick_items.62), channel_id=1, source_target_pairs={{0,4},{4,8},{8,12},{1,5},{5,9},{9,13},{2,6},{6,10},{10,14},{3,7},{... | collective-permute-start | bytes 1769480 | tf_op jit(solution)/shard_map/ppermute | solution.py:290
  87.6 23.5 %collective-permute-start.19 = (bf16[3,96,1024]{2,1,0:T(8,128)(2,1)S(1)}, bf16[3,96,1024]{2,1,0:T(8,128)(2,1)S(1)}, u32[]{:S(2)}, u32[]{:S(2)}) collective-permute-start(bf16[3,96,1024]{2,1,0:T(8,128)(2,1)S(1)} %pick_items.63), channel_id=1, source_target_pairs={{4,0},{8,4},{12,8},{5,1},{9,5},{13,9},{6,2},{10,6},{14,10},{7,3},{... | collective-permute-start | bytes 1769480 | tf_op jit(solution)/shard_map/ppermute | solution.py:290
  92.2 25.3 %copy-start.4 = (bf16[3,96,1024]{2,1,0:T(8,128)(2,1)}, bf16[3,96,1024]{2,1,0:T(8,128)(2,1)S(1)}, u32[]{:S(2)}) copy-start(bf16[3,96,1024]{2,1,0:T(8,128)(2,1)S(1)} %collective-permute-done.16.refs_2_) | copy-start | bytes 1769476
  92.9 24.6 %collective-permute-start.20 = (bf16[3,96,1024]{2,1,0:T(8,128)(2,1)S(1)}, bf16[3,96,1024]{2,1,0:T(8,128)(2,1)S(1)}, u32[]{:S(2)}, u32[]{:S(2)}) collective-permute-start(bf16[3,96,1024]{2,1,0:T(8,128)(2,1)S(1)} %pick_items.64), channel_id=1, source_target_pairs={{0,4},{4,8},{8,12},{1,5},{5,9},{9,13},{2,6},{6,10},{10,14},{3,7},{... | collective-permute-start | bytes 1769480 | tf_op jit(solution)/shard_map/ppermute | solution.py:290
  98.5 25.3 %copy-start.6 = (bf16[3,96,1024]{2,1,0:T(8,128)(2,1)}, bf16[3,96,1024]{2,1,0:T(8,128)(2,1)S(1)}, u32[]{:S(2)}) copy-start(bf16[3,96,1024]{2,1,0:T(8,128)(2,1)S(1)} %collective-permute-done.17.refs_2_) | copy-start | bytes 1769476
  99.2 24.6 %collective-permute-start.22 = (bf16[3,96,1024]{2,1,0:T(8,128)(2,1)S(1)}, bf16[3,96,1024]{2,1,0:T(8,128)(2,1)S(1)}, u32[]{:S(2)}, u32[]{:S(2)}) collective-permute-start(bf16[3,96,1024]{2,1,0:T(8,128)(2,1)S(1)} %pick_items.65), channel_id=1, source_target_pairs={{4,0},{8,4},{12,8},{5,1},{9,5},{13,9},{6,2},{10,6},{14,10},{7,3},{... | collective-permute-start | bytes 1769480 | tf_op jit(solution)/shard_map/ppermute | solution.py:290
  106.4 24.2 %collective-permute-start.24 = (bf16[3,96,1024]{2,1,0:T(8,128)(2,1)S(1)}, bf16[3,96,1024]{2,1,0:T(8,128)(2,1)S(1)}, u32[]{:S(2)}, u32[]{:S(2)}) collective-permute-start(bf16[3,96,1024]{2,1,0:T(8,128)(2,1)S(1)} %pick_items.66), channel_id=1, source_target_pairs={{0,4},{4,8},{8,12},{1,5},{5,9},{9,13},{2,6},{6,10},{10,14},{3,7},{... | collective-permute-start | bytes 1769480 | tf_op jit(solution)/shard_map/ppermute | solution.py:290
  112.7 23.6 %collective-permute-start.26 = (bf16[3,96,1024]{2,1,0:T(8,128)(2,1)S(1)}, bf16[3,96,1024]{2,1,0:T(8,128)(2,1)S(1)}, u32[]{:S(2)}, u32[]{:S(2)}) collective-permute-start(bf16[3,96,1024]{2,1,0:T(8,128)(2,1)S(1)} %pick_items.67), channel_id=1, source_target_pairs={{4,0},{8,4},{12,8},{5,1},{9,5},{13,9},{6,2},{10,6},{14,10},{7,3},{... | collective-permute-start | bytes 1769480 | tf_op jit(solution)/shard_map/ppermute | solution.py:290
  117.4 20.6 %copy-start.8 = (bf16[3,96,1024]{2,1,0:T(8,128)(2,1)}, bf16[3,96,1024]{2,1,0:T(8,128)(2,1)S(1)}, u32[]{:S(2)}) copy-start(bf16[3,96,1024]{2,1,0:T(8,128)(2,1)S(1)} %collective-permute-done.20.refs_3_) | copy-start | bytes 1769476
  123.7 14.3 %copy-start.10 = (bf16[3,96,1024]{2,1,0:T(8,128)(2,1)}, bf16[3,96,1024]{2,1,0:T(8,128)(2,1)S(1)}, u32[]{:S(2)}) copy-start(bf16[3,96,1024]{2,1,0:T(8,128)(2,1)S(1)} %collective-permute-done.22.refs_3_) | copy-start | bytes 1769476
  124.5 24.7 %collective-permute-start.23 = (bf16[3,96,1024]{2,1,0:T(8,128)(2,1)S(1)}, bf16[3,96,1024]{2,1,0:T(8,128)(2,1)}, u32[]{:S(2)}, u32[]{:S(2)}) collective-permute-start(bf16[3,96,1024]{2,1,0:T(8,128)(2,1)S(1)} %pick_items.69), channel_id=1, source_target_pairs={{4,0},{8,4},{12,8},{5,1},{9,5},{13,9},{6,2},{10,6},{14,10},{7,3},{... | collective-permute-start | bytes 1769480 | tf_op jit(solution)/shard_map/ppermute | solution.py:290
  125.8 23.4 %collective-permute-start.21 = (bf16[3,96,1024]{2,1,0:T(8,128)(2,1)S(1)}, bf16[3,96,1024]{2,1,0:T(8,128)(2,1)}, u32[]{:S(2)}, u32[]{:S(2)}) collective-permute-start(bf16[3,96,1024]{2,1,0:T(8,128)(2,1)S(1)} %pick_items.68), channel_id=1, source_target_pairs={{0,4},{4,8},{8,12},{1,5},{5,9},{9,13},{2,6},{6,10},{10,14},{3,7},{... | collective-permute-start | bytes 1769480 | tf_op jit(solution)/shard_map/ppermute | solution.py:290
  138.0 23.6 %collective-permute-start.27 = (bf16[3,96,1024]{2,1,0:T(8,128)(2,1)S(1)}, bf16[3,96,1024]{2,1,0:T(8,128)(2,1)S(1)}, u32[]{:S(2)}, u32[]{:S(2)}) collective-permute-start(bf16[3,96,1024]{2,1,0:T(8,128)(2,1)S(1)} %pick_items.71), channel_id=1, source_target_pairs={{4,0},{8,4},{12,8},{5,1},{9,5},{13,9},{6,2},{10,6},{14,10},{7,3},{... | collective-permute-start | bytes 1769480 | tf_op jit(solution)/shard_map/ppermute | solution.py:290
  139.3 22.3 %collective-permute-start.25 = (bf16[3,96,1024]{2,1,0:T(8,128)(2,1)S(1)}, bf16[3,96,1024]{2,1,0:T(8,128)(2,1)S(1)}, u32[]{:S(2)}, u32[]{:S(2)}) collective-permute-start(bf16[3,96,1024]{2,1,0:T(8,128)(2,1)S(1)} %pick_items.70), channel_id=1, source_target_pairs={{0,4},{4,8},{8,12},{1,5},{5,9},{9,13},{2,6},{6,10},{10,14},{3,7},{... | collective-permute-start | bytes 1769480 | tf_op jit(solution)/shard_map/ppermute | solution.py:290
  144.7 16.9 %copy-start.22 = (s32[16]{0:T(128)}, s32[16]{0:T(128)S(1)}, u32[]{:S(2)}) copy-start(s32[16]{0:T(128)S(1)} %select_reduce_fusion.1) | copy-start | bytes 196
  161.7 3.5 %copy-start.5 = (bf16[3,96,1024]{2,1,0:T(8,128)(2,1)S(1)}, bf16[3,96,1024]{2,1,0:T(8,128)(2,1)}, u32[]{:S(2)}) copy-start(bf16[3,96,1024]{2,1,0:T(8,128)(2,1)} %copy-done.4) | copy-start | bytes 1769476
  161.7 3.5 %copy-start.7 = (bf16[3,96,1024]{2,1,0:T(8,128)(2,1)S(1)}, bf16[3,96,1024]{2,1,0:T(8,128)(2,1)}, u32[]{:S(2)}) copy-start(bf16[3,96,1024]{2,1,0:T(8,128)(2,1)} %copy-done.6) | copy-start | bytes 1769476
  202.1 4.8 %copy-start.23 = (s32[16]{0:T(128)S(1)}, s32[16]{0:T(128)}, u32[]{:S(2)}) copy-start(s32[16]{0:T(128)} %copy-done.22) | copy-start | bytes 196
  202.1 32.4 %all-to-all-start.8 = ((bf16[4,3,96,1024]{3,2,1,0:T(8,128)(2,1)}), bf16[4,3,96,1024]{3,2,1,0:T(8,128)(2,1)S(1)}, u32[]{:S(2)}, u32[]{:S(2)}) async-start(bf16[4,3,96,1024]{3,2,1,0:T(8,128)(2,1)} %get-tuple-element.639), calls=%async_computation.8 | async-start | bytes 4718592 | tf_op jit(solution)/shard_map/all_to_all | solution.py:260
  210.3 1.7 copy-start
  211.9 2.8 copy-start.1
  214.7 24.8 %copy-start.21 = (s32[16]{0:T(128)S(1)}, s32[16]{0:T(128)}, u32[]{:S(2)}) copy-start(s32[16]{0:T(128)} %get-tuple-element.621) | copy-start | bytes 196
  228.4 2.6 copy-start.2
  234.5 23.6 %all-to-all-start.7 = ((bf16[16,24,1024]{2,1,0:T(8,128)(2,1)}), bf16[16,24,1024]{2,1,0:T(8,128)(2,1)}, u32[]{:S(2)}, u32[]{:S(2)}) async-start(bf16[16,24,1024]{2,1,0:T(8,128)(2,1)} %bitcast.29), calls=%async_computation.7 | async-start | bytes 1572864 | tf_op jit(solution)/shard_map/all_to_all | solution.py:260
  240.2 2.8 copy-start.3
  261.3 5.7 %copy-start.20 = (s32[16]{0:T(128)S(1)}, s32[16]{0:T(128)}, u32[]{:S(2)}) copy-start(s32[16]{0:T(128)} %copy-done.19) | copy-start | bytes 196
  261.3 38.1 %all-to-all-start.9 = ((bf16[16,2,24,1024]{3,2,1,0:T(8,128)(2,1)}), bf16[16,2,24,1024]{3,2,1,0:T(8,128)(2,1)S(1)}, u32[]{:S(2)}, u32[]{:S(2)}) async-start(bf16[16,2,24,1024]{3,2,1,0:T(8,128)(2,1)} %pad_maximum_fusion), calls=%async_computation.9 | async-start | bytes 3145728 | tf_op jit(solution)/shard_map/all_to_all | solution.py:260

commit v3 on v2

--- a/solution.py
+++ b/solution.py
@@ -269,8 +269,8 @@
 
 
 class Route:
-    def __init__(self, own, table, problem, doc_of, steps, horizon, levels):
-        self.own, self.table, self.problem, self.doc_of = own, table, problem, doc_of
+    def __init__(self, own, table, problem, origin, steps, horizon, levels):
+        self.own, self.table, self.problem, self.origin = own, table, problem, origin
         self.steps, self.horizon, self.levels = steps, horizon, levels
         self.rights, self.lefts = [], []
 
@@ -302,7 +302,8 @@
 
         def more(rights, lefts, own, table):
             if len(rights) == self.horizon:
-                return spread(own, self.doc_of, self.levels)
+                everything = lax.all_gather(own, "z", axis=0, tiled=True)
+                return jnp.take(everything, self.origin, axis=0)
             rights, lefts = self.stepped(rights, lefts, own, table)
             return self.finish(rights, lefts, own, table)
 
@@ -364,14 +365,15 @@
         blocks_first = exchange(spread(own_first, doc_first, levels), LEVEL)
         blocks_second = exchange(spread(own_second, doc_first, levels), LEVEL)
     else:
+        origin = lax.dynamic_slice_in_dim(doc_first, my_level * lanes, lanes, 0)
         targets = jnp.stack([first_owner, first_owner])
         live = jnp.stack([jnp.ones_like(has_second), has_second])
         table = plan_routes(levels, lanes, horizon, my_level, targets, live)
-        first = Route(own_first, table, 0, doc_first, steps[0], horizon, levels)
+        first = Route(own_first, table, 0, origin, steps[0], horizon, levels)
         order = Order()
         first.step(order)
         own_second = exchange(order.follow(after(pack(1, lanes, blocks), table)), LEVEL)
-        second = Route(own_second, table, 1, doc_first, steps[1], horizon, levels)
+        second = Route(own_second, table, 1, origin, steps[1], horizon, levels)
         for step in range(1, max(steps[0], steps[1] + LAG)):
             if step >= LAG and step - LAG < steps[1]:
                 second.step(order)

time: 333 us -> 345 us (1.036)
  blocking collectives: 63.2 us -> 29.2 us
  waiting for transfers between devices: 109 us -> 128 us
  between operations: 4.37 us -> 17.8 us
  Pallas kernels: 63.6 us -> 71.4 us
  starting transfers between devices: 69.6 us -> 75.7 us
    all_to_all x2 -> x1, blocking collectives: 63.2 us -> 29.2 us  [exchange(): return lax.all_to_all(pieces, axes, split_axis=0, concat_axis=0, tiled=True)]
    all_to_all x5 -> x6, waiting for transfers between devices: 59.1 us -> 83.6 us  [exchange(): return lax.all_to_all(pieces, axes, split_axis=0, concat_axis=0, tiled=True)]
    all_to_all x5 -> x6, starting transfers between devices: 24.8 us -> 31.9 us  [exchange(): return lax.all_to_all(pieces, axes, split_axis=0, concat_axis=0, tiled=True)]
    pallas_call x18, Pallas kernels: 26.6 us -> 33 us  [pick(): pl.pallas_call(functools.partial(pick_kernel, layout, sizes, problem), ou...]
    ppermute x16, waiting for transfers between devices: 50 us -> 44.6 us  [stepped(): came.append(arrivals + [lax.ppermute(outgoing, 'z', pairs)])]
  transfers between devices with their start and end apart: 21 -> 22, of which waited for: 16 -> 16; matrix products, arithmetic and copies ran while one was open for 1% -> 2% of each run, Pallas kernels for 15% -> 18%
where the time goes in v3:
time: 345 us; the launch traced here: 342 us
  waiting for transfers between devices  128 us (37%)
  starting transfers between devices  75.7 us (22%)
  Pallas kernels  71.4 us (21%)
  blocking collectives  29.2 us (8%)
  between operations  17.8 us (5%)
  local copies, waits for them, and re-layouts  17.1 us (5%)
    all_to_all x6, waiting for transfers between devices, exchange(): return lax.all_to_all(pieces, axes, split_axis=0, concat_axis=0, tiled=True)  83.6 us
    ppermute x16, waiting for transfers between devices, stepped(): came.append(arrivals + [lax.ppermute(outgoing, 'z', pairs)])  44.6 us
    ppermute x16, starting transfers between devices, stepped(): came.append(arrivals + [lax.ppermute(outgoing, 'z', pairs)])  43.8 us
    pallas_call x18, Pallas kernels, pick(): pl.pallas_call(functools.partial(pick_kernel, layout, sizes, problem), ou...  33 us
    all_to_all x6, starting transfers between devices, exchange(): return lax.all_to_all(pieces, axes, split_axis=0, concat_axis=0, tiled=True)  31.9 us
    all_to_all x1, blocking collectives, exchange(): return lax.all_to_all(pieces, axes, split_axis=0, concat_axis=0, tiled=True)  29.2 us
    pallas_call x2, Pallas kernels, run_document(): pl.pallas_call(functools.partial(round_kernel, tiles), grid=(tiles,), in_...  28.5 us
    unnamed x45, local copies, waits for them, and re-layouts  9.12 us
  transfers between devices with their start and end apart: 22, of which 16 were waited for; matrix products, arithmetic and copies ran while one was open for 2% of the time, Pallas kernels for 18%

profile of v3, /device:TPU:1, one launch (start us, length us, event | category | flops | bytes accessed | tf_op | source)
XLA Modules:
  0.0 342.1 jit_solution(16055104392192450424)
XLA Ops:
  7.2 3.9 %pack_blocks.2 = bf16[4,3,96,1024]{3,2,1,0:T(8,128)(2,1)} custom-call(bf16[2,1,384,1024]{3,2,1,0:T(8,128)(2,1)} %refs_0_.3, bf16[2,1,384,1024]{3,2,1,0:T(8,128)(2,1)} %refs_1_.3, bf16[2,1,384,1024]{3,2,1,0:T(8,128)(2,1)} %refs_2_.3), custom_call_target="tpu_custom_call" | custom-call | bytes 4718592 | tf_op jit(solution)/shard_map/pack_blocks/pallas_call | solution.py:328
  11.1 4.5 %all-to-all-start = ((bf16[4,3,96,1024]{3,2,1,0:T(8,128)(2,1)}), bf16[4,3,96,1024]{3,2,1,0:T(8,128)(2,1)}, u32[]{:S(2)}, u32[]{:S(2)}) async-start(bf16[4,3,96,1024]{3,2,1,0:T(8,128)(2,1)} %pack_blocks.2), calls=%async_computation | async-start | bytes 4718592 | tf_op jit(solution)/shard_map/all_to_all | solution.py:260
  15.6 4.0 %pack_blocks.3 = bf16[4,3,96,1024]{3,2,1,0:T(8,128)(2,1)} custom-call(bf16[2,1,384,1024]{3,2,1,0:T(8,128)(2,1)} %refs_0_.3, bf16[2,1,384,1024]{3,2,1,0:T(8,128)(2,1)} %refs_1_.3, bf16[2,1,384,1024]{3,2,1,0:T(8,128)(2,1)} %refs_2_.3), custom_call_target="tpu_custom_call" | custom-call | bytes 4718592 | tf_op jit(solution)/shard_map/pack_blocks/pallas_call | solution.py:328
  21.0 2.0 plan_routes.1
  23.1 20.6 %all-to-all-done.refs_1_ = bf16[4,3,96,1024]{3,2,1,0:T(8,128)(2,1)} async-done(((bf16[4,3,96,1024]{3,2,1,0:T(8,128)(2,1)}), bf16[4,3,96,1024]{3,2,1,0:T(8,128)(2,1)}, u32[]{:S(2)}, u32[]{:S(2)}) %all-to-all-start) | async-done | bytes 2359328 | tf_op jit(solution)/shard_map/all_to_all | solution.py:260
  43.6 1.6 pick_items.56
  45.3 1.6 pick_items.57
  46.9 5.7 %all-to-all-start.1 = ((bf16[4,3,96,1024]{3,2,1,0:T(8,128)(2,1)}), bf16[4,3,96,1024]{3,2,1,0:T(8,128)(2,1)}, u32[]{:S(2)}, u32[]{:S(2)}) async-start(bf16[4,3,96,1024]{3,2,1,0:T(8,128)(2,1)} %pack_blocks.3), calls=%async_computation.1 | async-start | bytes 4718592 | tf_op jit(solution)/shard_map/all_to_all | solution.py:260
  52.6 4.0 %collective-permute-start.12 = (bf16[3,96,1024]{2,1,0:T(8,128)(2,1)S(1)}, bf16[3,96,1024]{2,1,0:T(8,128)(2,1)S(1)}, u32[]{:S(2)}, u32[]{:S(2)}) collective-permute-start(bf16[3,96,1024]{2,1,0:T(8,128)(2,1)S(1)} %pick_items.56), channel_id=1, source_target_pairs={{0,4},{4,8},{8,12},{1,5},{5,9},{9,13},{2,6},{6,10},{10,14},{3,7},{... | collective-permute-start | bytes 1769480 | tf_op jit(solution)/shard_map/ppermute | solution.py:290
  58.0 11.3 %collective-permute-done.12.refs_2_ = bf16[3,96,1024]{2,1,0:T(8,128)(2,1)S(1)} collective-permute-done((bf16[3,96,1024]{2,1,0:T(8,128)(2,1)S(1)}, bf16[3,96,1024]{2,1,0:T(8,128)(2,1)S(1)}, u32[]{:S(2)}, u32[]{:S(2)}) %collective-permute-start.12) | collective-permute-done | bytes 589856 | tf_op jit(solution)/shard_map/ppermute | solution.py:290
  70.9 4.1 %collective-permute-start.14 = (bf16[3,96,1024]{2,1,0:T(8,128)(2,1)S(1)}, bf16[3,96,1024]{2,1,0:T(8,128)(2,1)}, u32[]{:S(2)}, u32[]{:S(2)}) collective-permute-start(bf16[3,96,1024]{2,1,0:T(8,128)(2,1)S(1)} %pick_items.58), channel_id=1, source_target_pairs={{0,4},{4,8},{8,12},{1,5},{5,9},{9,13},{2,6},{6,10},{10,14},{3,7},{... | collective-permute-start | bytes 1769480 | tf_op jit(solution)/shard_map/ppermute | solution.py:290
  75.0 1.6 pick_items.59
  78.0 2.4 all-to-all-done.1.refs_1_
  82.0 4.1 %collective-permute-start.16 = (bf16[3,96,1024]{2,1,0:T(8,128)(2,1)S(1)}, bf16[3,96,1024]{2,1,0:T(8,128)(2,1)S(1)}, u32[]{:S(2)}, u32[]{:S(2)}) collective-permute-start(bf16[3,96,1024]{2,1,0:T(8,128)(2,1)S(1)} %pick_items.60), channel_id=1, source_target_pairs={{0,4},{4,8},{8,12},{1,5},{5,9},{9,13},{2,6},{6,10},{10,14},{3,7},{... | collective-permute-start | bytes 1769480 | tf_op jit(solution)/shard_map/ppermute | solution.py:290
  86.1 1.6 pick_items.61
  89.2 1.6 pick_items.62
  90.8 4.0 %collective-permute-start.18 = (bf16[3,96,1024]{2,1,0:T(8,128)(2,1)S(1)}, bf16[3,96,1024]{2,1,0:T(8,128)(2,1)S(1)}, u32[]{:S(2)}, u32[]{:S(2)}) collective-permute-start(bf16[3,96,1024]{2,1,0:T(8,128)(2,1)S(1)} %pick_items.62), channel_id=1, source_target_pairs={{0,4},{4,8},{8,12},{1,5},{5,9},{9,13},{2,6},{6,10},{10,14},{3,7},{... | collective-permute-start | bytes 1769480 | tf_op jit(solution)/shard_map/ppermute | solution.py:290
  94.9 1.6 pick_items.63
  100.9 3.3 collective-permute-start.20
  108.1 3.8 %collective-permute-done.18.refs_4_ = bf16[3,96,1024]{2,1,0:T(8,128)(2,1)S(1)} collective-permute-done((bf16[3,96,1024]{2,1,0:T(8,128)(2,1)S(1)}, bf16[3,96,1024]{2,1,0:T(8,128)(2,1)S(1)}, u32[]{:S(2)}, u32[]{:S(2)}) %collective-permute-start.18) | collective-permute-done | bytes 589856 | tf_op jit(solution)/shard_map/ppermute | solution.py:290
  113.5 4.1 %collective-permute-start.24 = (bf16[3,96,1024]{2,1,0:T(8,128)(2,1)S(1)}, bf16[3,96,1024]{2,1,0:T(8,128)(2,1)S(1)}, u32[]{:S(2)}, u32[]{:S(2)}) collective-permute-start(bf16[3,96,1024]{2,1,0:T(8,128)(2,1)S(1)} %pick_items.66), channel_id=1, source_target_pairs={{0,4},{4,8},{8,12},{1,5},{5,9},{9,13},{2,6},{6,10},{10,14},{3,7},{... | collective-permute-start | bytes 1769480 | tf_op jit(solution)/shard_map/ppermute | solution.py:290
  120.7 3.8 %collective-permute-done.20.refs_3_ = bf16[3,96,1024]{2,1,0:T(8,128)(2,1)S(1)} collective-permute-done((bf16[3,96,1024]{2,1,0:T(8,128)(2,1)S(1)}, bf16[3,96,1024]{2,1,0:T(8,128)(2,1)S(1)}, u32[]{:S(2)}, u32[]{:S(2)}) %collective-permute-start.20) | collective-permute-done | bytes 589856 | tf_op jit(solution)/shard_map/ppermute | solution.py:290
  126.1 4.3 %collective-permute-done.22.refs_3_ = bf16[3,96,1024]{2,1,0:T(8,128)(2,1)S(1)} collective-permute-done((bf16[3,96,1024]{2,1,0:T(8,128)(2,1)S(1)}, bf16[3,96,1024]{2,1,0:T(8,128)(2,1)S(1)}, u32[]{:S(2)}, u32[]{:S(2)}) %collective-permute-start.22) | collective-permute-done | bytes 589856 | tf_op jit(solution)/shard_map/ppermute | solution.py:290
  133.4 4.8 %collective-permute-start.21 = (bf16[3,96,1024]{2,1,0:T(8,128)(2,1)S(1)}, bf16[3,96,1024]{2,1,0:T(8,128)(2,1)}, u32[]{:S(2)}, u32[]{:S(2)}) collective-permute-start(bf16[3,96,1024]{2,1,0:T(8,128)(2,1)S(1)} %pick_items.68), channel_id=1, source_target_pairs={{0,4},{4,8},{8,12},{1,5},{5,9},{9,13},{2,6},{6,10},{10,14},{3,7},{... | collective-permute-start | bytes 1769480 | tf_op jit(solution)/shard_map/ppermute | solution.py:290
  138.2 1.6 pick_items.70
  139.8 3.2 collective-permute-done.26.refs_5_
  143.1 1.6 pick_items.71
  146.0 4.8 %collective-permute-start.25 = (bf16[3,96,1024]{2,1,0:T(8,128)(2,1)S(1)}, bf16[3,96,1024]{2,1,0:T(8,128)(2,1)}, u32[]{:S(2)}, u32[]{:S(2)}) collective-permute-start(bf16[3,96,1024]{2,1,0:T(8,128)(2,1)S(1)} %pick_items.70), channel_id=1, source_target_pairs={{0,4},{4,8},{8,12},{1,5},{5,9},{9,13},{2,6},{6,10},{10,14},{3,7},{... | collective-permute-start | bytes 1769480 | tf_op jit(solution)/shard_map/ppermute | solution.py:290
  151.6 4.2 %collective-permute-done.23 = bf16[3,96,1024]{2,1,0:T(8,128)(2,1)} collective-permute-done((bf16[3,96,1024]{2,1,0:T(8,128)(2,1)S(1)}, bf16[3,96,1024]{2,1,0:T(8,128)(2,1)}, u32[]{:S(2)}, u32[]{:S(2)}) %collective-permute-start.23) | collective-permute-done | bytes 589856 | tf_op jit(solution)/shard_map/ppermute | solution.py:290
  157.0 11.4 %collective-permute-done.27 = bf16[3,96,1024]{2,1,0:T(8,128)(2,1)} collective-permute-done((bf16[3,96,1024]{2,1,0:T(8,128)(2,1)S(1)}, bf16[3,96,1024]{2,1,0:T(8,128)(2,1)}, u32[]{:S(2)}, u32[]{:S(2)}) %collective-permute-start.27) | collective-permute-done | bytes 589856 | tf_op jit(solution)/shard_map/ppermute | solution.py:290
  168.5 3.6 %conditional.8 = (bf16[4,3,96,1024]{3,2,1,0:T(8,128)(2,1)}) conditional(s32[]{:T(128)} %bitcast.12, (s32[2,128]{1,0:T(2,128)S(1)}, bf16[4,3,96,1024]{3,2,1,0:T(8,128)(2,1)}, bf16[3,96,1024]{2,1,0:T(8,128)(2,1)}, bf16[3,96,1024]{2,1,0:T(8,128)(2,1)}, bf16[3,96,1024]{2,1,0:T(8,128)(2,1)}, /*index=5*/bf16[3,96,1024]{2,1,0:T(8,128)(2,1)}, ...), branch_computations={%region_1.2_spmd, %region_2.8_spmd} | conditional | flops 1180712 | bytes 77861928 | solution.py:311
  168.5 3.6 %pick_items.36 = bf16[4,3,96,1024]{3,2,1,0:T(8,128)(2,1)} custom-call(s32[2,128]{1,0:T(2,128)S(1)} %get-tuple-element.290.refs_0_, bf16[4,3,96,1024]{3,2,1,0:T(8,128)(2,1)} %get-tuple-element.291.refs_1_, bf16[3,96,1024]{2,1,0:T(8,128)(2,1)} %get-tuple-element.292.refs_2_, bf16[3,96,1024]{2,1,0:T(8,128)(2,1)} %get-tuple-element.293.refs_3_, ...), custom_call_target="tpu_custom_call" | custom-call | bytes 9437184 | tf_op jit(solution)/shard_map/cond/branch_0_fun/pick_items/pallas_call | solution.py:234
  172.1 5.4 %all-to-all-start.2 = ((bf16[4,3,96,1024]{3,2,1,0:T(8,128)(2,1)}), bf16[4,3,96,1024]{3,2,1,0:T(8,128)(2,1)S(1)}, u32[]{:S(2)}, u32[]{:S(2)}) async-start(bf16[4,3,96,1024]{3,2,1,0:T(8,128)(2,1)} %get-tuple-element.638), calls=%async_computation.2 | async-start | bytes 4718592 | tf_op jit(solution)/shard_map/all_to_all | solution.py:260
  178.8 3.6 %conditional.9 = (bf16[4,3,96,1024]{3,2,1,0:T(8,128)(2,1)}) conditional(s32[]{:T(128)} %bitcast.17, (s32[2,128]{1,0:T(2,128)S(1)}, bf16[4,3,96,1024]{3,2,1,0:T(8,128)(2,1)}, bf16[3,96,1024]{2,1,0:T(8,128)(2,1)S(1)}, bf16[3,96,1024]{2,1,0:T(8,128)(2,1)}, bf16[3,96,1024]{2,1,0:T(8,128)(2,1)}, /*index=5*/bf16[3,96,1024]{2,1,0:T(8,128)(2,1)S(1)}, ...), branch_computations={%region_7.10_spmd, %region_8.19_spmd} | conditional | flops 1180716 | bytes 87299400 | solution.py:311
  178.8 3.4 %pick_items.43 = bf16[4,3,96,1024]{3,2,1,0:T(8,128)(2,1)} custom-call(s32[2,128]{1,0:T(2,128)S(1)} %get-tuple-element.462.refs_0_, bf16[4,3,96,1024]{3,2,1,0:T(8,128)(2,1)} %get-tuple-element.463.refs_1_, bf16[3,96,1024]{2,1,0:T(8,128)(2,1)S(1)} %get-tuple-element.464.refs_2_, bf16[3,96,1024]{2,1,0:T(8,128)(2,1)} %get-tuple-element.465.refs_3_, ...), custom_call_target="tpu_custom_call" | custom-call | bytes 9437184 | tf_op jit(solution)/shard_map/cond/branch_0_fun/pick_items/pallas_call | solution.py:234
  182.4 22.7 %all-to-all-done.2.blocks_ref = bf16[4,3,96,1024]{3,2,1,0:T(8,128)(2,1)S(1)} async-done(((bf16[4,3,96,1024]{3,2,1,0:T(8,128)(2,1)}), bf16[4,3,96,1024]{3,2,1,0:T(8,128)(2,1)S(1)}, u32[]{:S(2)}, u32[]{:S(2)}) %all-to-all-start.2) | async-done | bytes 2359328 | tf_op jit(solution)/shard_map/all_to_all | solution.py:260
  205.1 5.4 %all-to-all-start.4 = ((bf16[4,3,96,1024]{3,2,1,0:T(8,128)(2,1)}), bf16[4,3,96,1024]{3,2,1,0:T(8,128)(2,1)}, u32[]{:S(2)}, u32[]{:S(2)}) async-start(bf16[4,3,96,1024]{3,2,1,0:T(8,128)(2,1)} %get-tuple-element.639), calls=%async_computation.4 | async-start | bytes 4718592 | tf_op jit(solution)/shard_map/all_to_all | solution.py:260
  213.9 2.8 copy-done
  216.7 13.6 %run_document.2 = (bf16[384,1024]{1,0:T(8,128)(2,1)}, bf16[1,3,1024,1024]{3,2,1,0:T(8,128)(2,1)S(1)}) custom-call(s32[1]{0:T(128)} %constant.99.clone.1.live_ref, bf16[4,3,96,1024]{3,2,1,0:T(8,128)(2,1)S(1)} %all-to-all-done.2.blocks_ref, f32[384,1]{1,0:T(8,128)S(1)} %copy.19.rates_ref, bf16[1,3,1024,1024]{3,2,1,0:T(8,128)(2,1)S(1)} %copy-done, ...), custom_call_target="tpu_custom_call" | custom-call | flops 7247757312 | bytes 15728640 | tf_op jit(solution)/shard_map/run_document/pallas_call | solution.py:113
  230.3 2.6 copy-done.1
  232.9 5.3 %all-to-all-done.4.blocks_ref = bf16[4,3,96,1024]{3,2,1,0:T(8,128)(2,1)} async-done(((bf16[4,3,96,1024]{3,2,1,0:T(8,128)(2,1)}), bf16[4,3,96,1024]{3,2,1,0:T(8,128)(2,1)}, u32[]{:S(2)}, u32[]{:S(2)}) %all-to-all-start.4) | async-done | bytes 2359328 | tf_op jit(solution)/shard_map/all_to_all | solution.py:260
  238.3 4.9 %all-to-all-start.3 = ((bf16[16,24,1024]{2,1,0:T(8,128)(2,1)}), bf16[16,24,1024]{2,1,0:T(8,128)(2,1)}, u32[]{:S(2)}, u32[]{:S(2)}) async-start(bf16[16,24,1024]{2,1,0:T(8,128)(2,1)} %bitcast.15), calls=%async_computation.3 | async-start | bytes 1572864 | tf_op jit(solution)/shard_map/all_to_all | solution.py:260
  243.9 2.8 copy-done.2
  246.7 14.9 %run_document.3 = bf16[384,1024]{1,0:T(8,128)(2,1)S(1)} custom-call(s32[1]{0:T(128)} %dynamic_slice.16.live_ref, bf16[4,3,96,1024]{3,2,1,0:T(8,128)(2,1)} %all-to-all-done.4.blocks_ref, f32[384,1]{1,0:T(8,128)S(1)} %copy.20.rates_ref, bf16[1,3,1024,1024]{3,2,1,0:T(8,128)(2,1)S(1)} %copy-done.2, bf16[1,3,1024,1024]{3,2,1,0:T(8,128)(2,1)S(1)} %copy-done.2, ...), custom_call_target="tpu_custom_call" | custom-call | flops 7247757312 | bytes 15728640 | tf_op jit(solution)/shard_map/run_document/pallas_call | solution.py:113
  261.9 1.7 gather_fusion.2
  265.1 6.0 %all-to-all-start.5 = ((bf16[16,2,24,1024]{3,2,1,0:T(8,128)(2,1)}), bf16[16,2,24,1024]{3,2,1,0:T(8,128)(2,1)S(1)}, u32[]{:S(2)}, u32[]{:S(2)}) async-start(bf16[16,2,24,1024]{3,2,1,0:T(8,128)(2,1)} %pad_maximum_fusion), calls=%async_computation.5 | async-start | bytes 3145728 | tf_op jit(solution)/shard_map/all_to_all | solution.py:260
  271.1 32.3 %all-to-all-done.5 = bf16[16,2,24,1024]{3,2,1,0:T(8,128)(2,1)S(1)} async-done(((bf16[16,2,24,1024]{3,2,1,0:T(8,128)(2,1)}), bf16[16,2,24,1024]{3,2,1,0:T(8,128)(2,1)S(1)}, u32[]{:S(2)}, u32[]{:S(2)}) %all-to-all-start.5) | async-done | bytes 1572896 | tf_op jit(solution)/shard_map/all_to_all | solution.py:260
  305.2 29.2 %all_to_all.35 = bf16[16,24,1024]{2,1,0:T(8,128)(2,1)S(1)} all-to-all(bf16[16,24,1024]{2,1,0:T(8,128)(2,1)S(1)} %broadcast_select_fusion.2), channel_id=1, replica_groups=mesh['grp'=2,'z'=4,'x'=2,'core'=2] {'z','x','core'}, dimensions={0} | all-to-all | bytes 1572864 | tf_op jit(solution)/shard_map/all_to_all | solution.py:260
  (99 shorter events, 36.0 us)
Async XLA Ops:
  11.1 32.5 %all-to-all-start = ((bf16[4,3,96,1024]{3,2,1,0:T(8,128)(2,1)}), bf16[4,3,96,1024]{3,2,1,0:T(8,128)(2,1)}, u32[]{:S(2)}, u32[]{:S(2)}) async-start(bf16[4,3,96,1024]{3,2,1,0:T(8,128)(2,1)} %pack_blocks.2), calls=%async_computation | async-start | bytes 4718592 | tf_op jit(solution)/shard_map/all_to_all | solution.py:260
  15.6 4.0 %copy-start.22 = (s32[16]{0:T(128)S(1)}, s32[16]{0:T(128)}, u32[]{:S(2)}) copy-start(s32[16]{0:T(128)} %param.33) | copy-start | bytes 196
  15.6 4.6 %copy-start.21 = (s32[16]{0:T(128)S(1)}, s32[16]{0:T(128)}, u32[]{:S(2)}) copy-start(s32[16]{0:T(128)} %param.34) | copy-start | bytes 196
  15.6 4.6 %copy-start.23 = (s32[16]{0:T(128)S(1)}, s32[16]{0:T(128)}, u32[]{:S(2)}) copy-start(s32[16]{0:T(128)} %param.35) | copy-start | bytes 196
  20.4 23.3 %copy-start.24 = (s32[16]{0:T(128)}, s32[16]{0:T(128)S(1)}, u32[]{:S(2)}) copy-start(s32[16]{0:T(128)S(1)} %select_reduce_fusion) | copy-start | bytes 196
  46.9 33.5 %all-to-all-start.1 = ((bf16[4,3,96,1024]{3,2,1,0:T(8,128)(2,1)}), bf16[4,3,96,1024]{3,2,1,0:T(8,128)(2,1)}, u32[]{:S(2)}, u32[]{:S(2)}) async-start(bf16[4,3,96,1024]{3,2,1,0:T(8,128)(2,1)} %pack_blocks.3), calls=%async_computation.1 | async-start | bytes 4718592 | tf_op jit(solution)/shard_map/all_to_all | solution.py:260
  52.6 16.7 %collective-permute-start.12 = (bf16[3,96,1024]{2,1,0:T(8,128)(2,1)S(1)}, bf16[3,96,1024]{2,1,0:T(8,128)(2,1)S(1)}, u32[]{:S(2)}, u32[]{:S(2)}) collective-permute-start(bf16[3,96,1024]{2,1,0:T(8,128)(2,1)S(1)} %pick_items.56), channel_id=1, source_target_pairs={{0,4},{4,8},{8,12},{1,5},{5,9},{9,13},{2,6},{6,10},{10,14},{3,7},{... | collective-permute-start | bytes 1769480 | tf_op jit(solution)/shard_map/ppermute | solution.py:290
  56.7 18.4 %collective-permute-start.13 = (bf16[3,96,1024]{2,1,0:T(8,128)(2,1)S(1)}, bf16[3,96,1024]{2,1,0:T(8,128)(2,1)S(1)}, u32[]{:S(2)}, u32[]{:S(2)}) collective-permute-start(bf16[3,96,1024]{2,1,0:T(8,128)(2,1)S(1)} %pick_items.57), channel_id=1, source_target_pairs={{4,0},{8,4},{12,8},{5,1},{9,5},{13,9},{6,2},{10,6},{14,10},{7,3},{... | collective-permute-start | bytes 1769480 | tf_op jit(solution)/shard_map/ppermute | solution.py:290
  69.3 19.8 %copy-start.7 = (bf16[3,96,1024]{2,1,0:T(8,128)(2,1)}, bf16[3,96,1024]{2,1,0:T(8,128)(2,1)S(1)}, u32[]{:S(2)}) copy-start(bf16[3,96,1024]{2,1,0:T(8,128)(2,1)S(1)} %collective-permute-done.12.refs_2_) | copy-start | bytes 1769476
  70.9 18.2 %collective-permute-start.14 = (bf16[3,96,1024]{2,1,0:T(8,128)(2,1)S(1)}, bf16[3,96,1024]{2,1,0:T(8,128)(2,1)}, u32[]{:S(2)}, u32[]{:S(2)}) collective-permute-start(bf16[3,96,1024]{2,1,0:T(8,128)(2,1)S(1)} %pick_items.58), channel_id=1, source_target_pairs={{0,4},{4,8},{8,12},{1,5},{5,9},{9,13},{2,6},{6,10},{10,14},{3,7},{... | collective-permute-start | bytes 1769480 | tf_op jit(solution)/shard_map/ppermute | solution.py:290
  75.0 7.0 %copy-start.10 = (bf16[3,96,1024]{2,1,0:T(8,128)(2,1)}, bf16[3,96,1024]{2,1,0:T(8,128)(2,1)S(1)}, u32[]{:S(2)}) copy-start(bf16[3,96,1024]{2,1,0:T(8,128)(2,1)S(1)} %collective-permute-done.13.refs_2_) | copy-start | bytes 1769476
  76.7 18.2 %collective-permute-start.15 = (bf16[3,96,1024]{2,1,0:T(8,128)(2,1)S(1)}, bf16[3,96,1024]{2,1,0:T(8,128)(2,1)}, u32[]{:S(2)}, u32[]{:S(2)}) collective-permute-start(bf16[3,96,1024]{2,1,0:T(8,128)(2,1)S(1)} %pick_items.59), channel_id=1, source_target_pairs={{4,0},{8,4},{12,8},{5,1},{9,5},{13,9},{6,2},{10,6},{14,10},{7,3},{... | collective-permute-start | bytes 1769480 | tf_op jit(solution)/shard_map/ppermute | solution.py:290
  82.0 17.2 %collective-permute-start.16 = (bf16[3,96,1024]{2,1,0:T(8,128)(2,1)S(1)}, bf16[3,96,1024]{2,1,0:T(8,128)(2,1)S(1)}, u32[]{:S(2)}, u32[]{:S(2)}) collective-permute-start(bf16[3,96,1024]{2,1,0:T(8,128)(2,1)S(1)} %pick_items.60), channel_id=1, source_target_pairs={{0,4},{4,8},{8,12},{1,5},{5,9},{9,13},{2,6},{6,10},{10,14},{3,7},{... | collective-permute-start | bytes 1769480 | tf_op jit(solution)/shard_map/ppermute | solution.py:290
  87.7 7.1 %copy-start.11 = (bf16[3,96,1024]{2,1,0:T(8,128)(2,1)S(1)}, bf16[3,96,1024]{2,1,0:T(8,128)(2,1)}, u32[]{:S(2)}) copy-start(bf16[3,96,1024]{2,1,0:T(8,128)(2,1)} %copy-done.10) | copy-start | bytes 1769476
  87.7 17.4 %collective-permute-start.17 = (bf16[3,96,1024]{2,1,0:T(8,128)(2,1)S(1)}, bf16[3,96,1024]{2,1,0:T(8,128)(2,1)S(1)}, u32[]{:S(2)}, u32[]{:S(2)}) collective-permute-start(bf16[3,96,1024]{2,1,0:T(8,128)(2,1)S(1)} %pick_items.61), channel_id=1, source_target_pairs={{4,0},{8,4},{12,8},{5,1},{9,5},{13,9},{6,2},{10,6},{14,10},{7,3},{... | collective-permute-start | bytes 1769480 | tf_op jit(solution)/shard_map/ppermute | solution.py:290
  90.8 21.1 %collective-permute-start.18 = (bf16[3,96,1024]{2,1,0:T(8,128)(2,1)S(1)}, bf16[3,96,1024]{2,1,0:T(8,128)(2,1)S(1)}, u32[]{:S(2)}, u32[]{:S(2)}) collective-permute-start(bf16[3,96,1024]{2,1,0:T(8,128)(2,1)S(1)} %pick_items.62), channel_id=1, source_target_pairs={{0,4},{4,8},{8,12},{1,5},{5,9},{9,13},{2,6},{6,10},{10,14},{3,7},{... | collective-permute-start | bytes 1769480 | tf_op jit(solution)/shard_map/ppermute | solution.py:290
  96.5 21.3 %collective-permute-start.19 = (bf16[3,96,1024]{2,1,0:T(8,128)(2,1)S(1)}, bf16[3,96,1024]{2,1,0:T(8,128)(2,1)S(1)}, u32[]{:S(2)}, u32[]{:S(2)}) collective-permute-start(bf16[3,96,1024]{2,1,0:T(8,128)(2,1)S(1)} %pick_items.63), channel_id=1, source_target_pairs={{4,0},{8,4},{12,8},{5,1},{9,5},{13,9},{6,2},{10,6},{14,10},{7,3},{... | collective-permute-start | bytes 1769480 | tf_op jit(solution)/shard_map/ppermute | solution.py:290
  100.9 11.0 %copy-start.8 = (bf16[3,96,1024]{2,1,0:T(8,128)(2,1)S(1)}, bf16[3,96,1024]{2,1,0:T(8,128)(2,1)}, u32[]{:S(2)}) copy-start(bf16[3,96,1024]{2,1,0:T(8,128)(2,1)} %copy-done.7) | copy-start | bytes 1769476
  100.9 23.6 %collective-permute-start.20 = (bf16[3,96,1024]{2,1,0:T(8,128)(2,1)S(1)}, bf16[3,96,1024]{2,1,0:T(8,128)(2,1)S(1)}, u32[]{:S(2)}, u32[]{:S(2)}) collective-permute-start(bf16[3,96,1024]{2,1,0:T(8,128)(2,1)S(1)} %pick_items.64), channel_id=1, source_target_pairs={{0,4},{4,8},{8,12},{1,5},{5,9},{9,13},{2,6},{6,10},{10,14},{3,7},{... | collective-permute-start | bytes 1769480 | tf_op jit(solution)/shard_map/ppermute | solution.py:290
  106.8 23.6 %collective-permute-start.22 = (bf16[3,96,1024]{2,1,0:T(8,128)(2,1)S(1)}, bf16[3,96,1024]{2,1,0:T(8,128)(2,1)S(1)}, u32[]{:S(2)}, u32[]{:S(2)}) collective-permute-start(bf16[3,96,1024]{2,1,0:T(8,128)(2,1)S(1)} %pick_items.65), channel_id=1, source_target_pairs={{4,0},{8,4},{12,8},{5,1},{9,5},{13,9},{6,2},{10,6},{14,10},{7,3},{... | collective-permute-start | bytes 1769480 | tf_op jit(solution)/shard_map/ppermute | solution.py:290
  111.9 26.3 %copy-start.13 = (bf16[3,96,1024]{2,1,0:T(8,128)(2,1)}, bf16[3,96,1024]{2,1,0:T(8,128)(2,1)S(1)}, u32[]{:S(2)}) copy-start(bf16[3,96,1024]{2,1,0:T(8,128)(2,1)S(1)} %collective-permute-done.18.refs_4_) | copy-start | bytes 1769476
  113.5 24.7 %collective-permute-start.24 = (bf16[3,96,1024]{2,1,0:T(8,128)(2,1)S(1)}, bf16[3,96,1024]{2,1,0:T(8,128)(2,1)S(1)}, u32[]{:S(2)}, u32[]{:S(2)}) collective-permute-start(bf16[3,96,1024]{2,1,0:T(8,128)(2,1)S(1)} %pick_items.66), channel_id=1, source_target_pairs={{0,4},{4,8},{8,12},{1,5},{5,9},{9,13},{2,6},{6,10},{10,14},{3,7},{... | collective-permute-start | bytes 1769480 | tf_op jit(solution)/shard_map/ppermute | solution.py:290
  117.8 25.3 %copy-start.15 = (bf16[3,96,1024]{2,1,0:T(8,128)(2,1)}, bf16[3,96,1024]{2,1,0:T(8,128)(2,1)S(1)}, u32[]{:S(2)}) copy-start(bf16[3,96,1024]{2,1,0:T(8,128)(2,1)S(1)} %collective-permute-done.19.refs_4_) | copy-start | bytes 1769476
  119.4 23.6 %collective-permute-start.26 = (bf16[3,96,1024]{2,1,0:T(8,128)(2,1)S(1)}, bf16[3,96,1024]{2,1,0:T(8,128)(2,1)S(1)}, u32[]{:S(2)}, u32[]{:S(2)}) collective-permute-start(bf16[3,96,1024]{2,1,0:T(8,128)(2,1)S(1)} %pick_items.67), channel_id=1, source_target_pairs={{4,0},{8,4},{12,8},{5,1},{9,5},{13,9},{6,2},{10,6},{14,10},{7,3},{... | collective-permute-start | bytes 1769480 | tf_op jit(solution)/shard_map/ppermute | solution.py:290
  124.5 7.6 %copy-start.3 = (bf16[3,96,1024]{2,1,0:T(8,128)(2,1)}, bf16[3,96,1024]{2,1,0:T(8,128)(2,1)S(1)}, u32[]{:S(2)}) copy-start(bf16[3,96,1024]{2,1,0:T(8,128)(2,1)S(1)} %collective-permute-done.20.refs_3_) | copy-start | bytes 1769476
  130.4 14.3 %copy-start.5 = (bf16[3,96,1024]{2,1,0:T(8,128)(2,1)}, bf16[3,96,1024]{2,1,0:T(8,128)(2,1)S(1)}, u32[]{:S(2)}) copy-start(bf16[3,96,1024]{2,1,0:T(8,128)(2,1)S(1)} %collective-permute-done.22.refs_3_) | copy-start | bytes 1769476
  132.1 23.7 %collective-permute-start.23 = (bf16[3,96,1024]{2,1,0:T(8,128)(2,1)S(1)}, bf16[3,96,1024]{2,1,0:T(8,128)(2,1)}, u32[]{:S(2)}, u32[]{:S(2)}) collective-permute-start(bf16[3,96,1024]{2,1,0:T(8,128)(2,1)S(1)} %pick_items.69), channel_id=1, source_target_pairs={{4,0},{8,4},{12,8},{5,1},{9,5},{13,9},{6,2},{10,6},{14,10},{7,3},{... | collective-permute-start | bytes 1769480 | tf_op jit(solution)/shard_map/ppermute | solution.py:290
  133.4 22.4 %collective-permute-start.21 = (bf16[3,96,1024]{2,1,0:T(8,128)(2,1)S(1)}, bf16[3,96,1024]{2,1,0:T(8,128)(2,1)}, u32[]{:S(2)}, u32[]{:S(2)}) collective-permute-start(bf16[3,96,1024]{2,1,0:T(8,128)(2,1)S(1)} %pick_items.68), channel_id=1, source_target_pairs={{0,4},{4,8},{8,12},{1,5},{5,9},{9,13},{2,6},{6,10},{10,14},{3,7},{... | collective-permute-start | bytes 1769480 | tf_op jit(solution)/shard_map/ppermute | solution.py:290
  138.2 1.6 copy-start.17
  143.1 1.6 copy-start.19
  144.7 23.7 %collective-permute-start.27 = (bf16[3,96,1024]{2,1,0:T(8,128)(2,1)S(1)}, bf16[3,96,1024]{2,1,0:T(8,128)(2,1)}, u32[]{:S(2)}, u32[]{:S(2)}) collective-permute-start(bf16[3,96,1024]{2,1,0:T(8,128)(2,1)S(1)} %pick_items.71), channel_id=1, source_target_pairs={{4,0},{8,4},{12,8},{5,1},{9,5},{13,9},{6,2},{10,6},{14,10},{7,3},{... | collective-permute-start | bytes 1769480 | tf_op jit(solution)/shard_map/ppermute | solution.py:290
  146.0 22.4 %collective-permute-start.25 = (bf16[3,96,1024]{2,1,0:T(8,128)(2,1)S(1)}, bf16[3,96,1024]{2,1,0:T(8,128)(2,1)}, u32[]{:S(2)}, u32[]{:S(2)}) collective-permute-start(bf16[3,96,1024]{2,1,0:T(8,128)(2,1)S(1)} %pick_items.70), channel_id=1, source_target_pairs={{0,4},{4,8},{8,12},{1,5},{5,9},{9,13},{2,6},{6,10},{10,14},{3,7},{... | collective-permute-start | bytes 1769480 | tf_op jit(solution)/shard_map/ppermute | solution.py:290
  151.0 17.5 %copy-start.27 = (s32[16]{0:T(128)}, s32[16]{0:T(128)S(1)}, u32[]{:S(2)}) copy-start(s32[16]{0:T(128)S(1)} %select_reduce_fusion.1) | copy-start | bytes 196
  172.1 6.7 %copy-start.29 = (s32[4]{0:T(128)S(1)}, s32[4]{0:T(128)}, u32[]{:S(2)}) copy-start(s32[4]{0:T(128)} %dynamic_slice.13) | copy-start | bytes 52
  172.1 33.0 %all-to-all-start.2 = ((bf16[4,3,96,1024]{3,2,1,0:T(8,128)(2,1)}), bf16[4,3,96,1024]{3,2,1,0:T(8,128)(2,1)S(1)}, u32[]{:S(2)}, u32[]{:S(2)}) async-start(bf16[4,3,96,1024]{3,2,1,0:T(8,128)(2,1)} %get-tuple-element.638), calls=%async_computation.2 | async-start | bytes 4718592 | tf_op jit(solution)/shard_map/all_to_all | solution.py:260
  182.4 28.1 %copy-start.28 = (s32[16]{0:T(128)S(1)}, s32[16]{0:T(128)}, u32[]{:S(2)}) copy-start(s32[16]{0:T(128)} %copy-done.27) | copy-start | bytes 196
  205.1 33.1 %all-to-all-start.4 = ((bf16[4,3,96,1024]{3,2,1,0:T(8,128)(2,1)}), bf16[4,3,96,1024]{3,2,1,0:T(8,128)(2,1)}, u32[]{:S(2)}, u32[]{:S(2)}) async-start(bf16[4,3,96,1024]{3,2,1,0:T(8,128)(2,1)} %get-tuple-element.639), calls=%async_computation.4 | async-start | bytes 4718592 | tf_op jit(solution)/shard_map/all_to_all | solution.py:260
  213.9 2.8 copy-start
  216.7 26.6 %copy-start.26 = (s32[16]{0:T(128)S(1)}, s32[16]{0:T(128)}, u32[]{:S(2)}) copy-start(s32[16]{0:T(128)} %get-tuple-element.621) | copy-start | bytes 196
  230.3 2.6 copy-start.1
  238.3 23.6 %all-to-all-start.3 = ((bf16[16,24,1024]{2,1,0:T(8,128)(2,1)}), bf16[16,24,1024]{2,1,0:T(8,128)(2,1)}, u32[]{:S(2)}, u32[]{:S(2)}) async-start(bf16[16,24,1024]{2,1,0:T(8,128)(2,1)} %bitcast.15), calls=%async_computation.3 | async-start | bytes 1572864 | tf_op jit(solution)/shard_map/all_to_all | solution.py:260
  243.9 2.8 copy-start.2
  265.1 6.0 %copy-start.25 = (s32[16]{0:T(128)S(1)}, s32[16]{0:T(128)}, u32[]{:S(2)}) copy-start(s32[16]{0:T(128)} %copy-done.24) | copy-start | bytes 196
  265.1 38.3 %all-to-all-start.5 = ((bf16[16,2,24,1024]{3,2,1,0:T(8,128)(2,1)}), bf16[16,2,24,1024]{3,2,1,0:T(8,128)(2,1)S(1)}, u32[]{:S(2)}, u32[]{:S(2)}) async-start(bf16[16,2,24,1024]{3,2,1,0:T(8,128)(2,1)} %pad_maximum_fusion), calls=%async_computation.5 | async-start | bytes 3145728 | tf_op jit(solution)/shard_map/all_to_all | solution.py:260

commit v4 on v3

--- a/solution.py
+++ b/solution.py
@@ -318,18 +318,19 @@
 def pack_kernel(*refs):
     out_ref = refs[-1]
     for number, ref in enumerate(refs[:-1]):
-        out_ref[0, number] = ref[0, 0]
+        out_ref[:, number] = ref[0, 0].reshape(out_ref.shape[0], *out_ref.shape[2:])
 
 
 def pack(section, lanes, blocks):
     block_rows, width = blocks[0].shape[2:]
     part = block_rows // lanes
     shape = (lanes, len(blocks), part, width)
+    each = math.gcd(2, lanes)
     return pl.pallas_call(
         pack_kernel,
-        grid=(lanes,),
-        in_specs=[pl.BlockSpec((1, 1, part, width), lambda lane: (section, 0, lane, 0)) for _ in blocks],
-        out_specs=pl.BlockSpec((1,) + shape[1:], lambda lane: (lane, 0, 0, 0)),
+        grid=(lanes // each,),
+        in_specs=[pl.BlockSpec((1, 1, each * part, width), lambda lane: (section, 0, lane, 0)) for _ in blocks],
+        out_specs=pl.BlockSpec((each,) + shape[1:], lambda lane: (lane, 0, 0, 0)),
         out_shape=jax.ShapeDtypeStruct(shape, blocks[0].dtype),
         cost_estimate=pl.CostEstimate(flops=0, transcendentals=0, bytes_accessed=4 * math.prod(shape)),
         name="pack_blocks",

time: 345 us -> 343 us (level)
  transfers between devices with their start and end apart: 22 -> 22, of which waited for: 16 -> 16; matrix products, arithmetic and copies ran while one was open for 2% -> 2% of each run, Pallas kernels for 18% -> 17%
where the time goes in v4:
time: 343 us; the launch traced here: 342 us
  waiting for transfers between devices  129 us (38%)
  starting transfers between devices  76.8 us (22%)
  Pallas kernels  69.2 us (20%)
  blocking collectives  29.2 us (9%)
  between operations  17.8 us (5%)
  local copies, waits for them, and re-layouts  17.1 us (5%)
    all_to_all x6, waiting for transfers between devices, exchange(): return lax.all_to_all(pieces, axes, split_axis=0, concat_axis=0, tiled=True)  83.7 us
    ppermute x16, waiting for transfers between devices, stepped(): came.append(arrivals + [lax.ppermute(outgoing, 'z', pairs)])  45.4 us
    ppermute x16, starting transfers between devices, stepped(): came.append(arrivals + [lax.ppermute(outgoing, 'z', pairs)])  44.7 us
    pallas_call x18, Pallas kernels, pick(): pl.pallas_call(functools.partial(pick_kernel, layout, sizes, problem), ou...  33.2 us
    all_to_all x6, starting transfers between devices, exchange(): return lax.all_to_all(pieces, axes, split_axis=0, concat_axis=0, tiled=True)  32 us
    all_to_all x1, blocking collectives, exchange(): return lax.all_to_all(pieces, axes, split_axis=0, concat_axis=0, tiled=True)  29.2 us
    pallas_call x2, Pallas kernels, run_document(): pl.pallas_call(functools.partial(round_kernel, tiles), grid=(tiles,), in_...  28.5 us
    unnamed x45, local copies, waits for them, and re-layouts  9.12 us
  transfers between devices with their start and end apart: 22, of which 16 were waited for; matrix products, arithmetic and copies ran while one was open for 2% of the time, Pallas kernels for 17%

profile of v4, /device:TPU:1, one launch (start us, length us, event | category | flops | bytes accessed | tf_op | source)
XLA Modules:
  0.0 341.8 jit_solution(15770692573745945868)
XLA Ops:
  7.2 2.7 pack_blocks.2
  9.9 4.5 %all-to-all-start = ((bf16[4,3,96,1024]{3,2,1,0:T(8,128)(2,1)}), bf16[4,3,96,1024]{3,2,1,0:T(8,128)(2,1)}, u32[]{:S(2)}, u32[]{:S(2)}) async-start(bf16[4,3,96,1024]{3,2,1,0:T(8,128)(2,1)} %pack_blocks.2), calls=%async_computation | async-start | bytes 4718592 | tf_op jit(solution)/shard_map/all_to_all | solution.py:260
  14.4 2.7 pack_blocks.3
  18.6 2.0 plan_routes.1
  20.6 21.8 %all-to-all-done.refs_1_ = bf16[4,3,96,1024]{3,2,1,0:T(8,128)(2,1)} async-done(((bf16[4,3,96,1024]{3,2,1,0:T(8,128)(2,1)}), bf16[4,3,96,1024]{3,2,1,0:T(8,128)(2,1)}, u32[]{:S(2)}, u32[]{:S(2)}) %all-to-all-start) | async-done | bytes 2359328 | tf_op jit(solution)/shard_map/all_to_all | solution.py:260
  42.4 1.6 pick_items.56
  44.1 1.6 pick_items.57
  45.7 5.7 %all-to-all-start.1 = ((bf16[4,3,96,1024]{3,2,1,0:T(8,128)(2,1)}), bf16[4,3,96,1024]{3,2,1,0:T(8,128)(2,1)}, u32[]{:S(2)}, u32[]{:S(2)}) async-start(bf16[4,3,96,1024]{3,2,1,0:T(8,128)(2,1)} %pack_blocks.3), calls=%async_computation.1 | async-start | bytes 4718592 | tf_op jit(solution)/shard_map/all_to_all | solution.py:260
  51.4 4.0 %collective-permute-start.12 = (bf16[3,96,1024]{2,1,0:T(8,128)(2,1)S(1)}, bf16[3,96,1024]{2,1,0:T(8,128)(2,1)S(1)}, u32[]{:S(2)}, u32[]{:S(2)}) collective-permute-start(bf16[3,96,1024]{2,1,0:T(8,128)(2,1)S(1)} %pick_items.56), channel_id=1, source_target_pairs={{0,4},{4,8},{8,12},{1,5},{5,9},{9,13},{2,6},{6,10},{10,14},{3,7},{... | collective-permute-start | bytes 1769480 | tf_op jit(solution)/shard_map/ppermute | solution.py:290
  56.8 11.3 %collective-permute-done.12.refs_2_ = bf16[3,96,1024]{2,1,0:T(8,128)(2,1)S(1)} collective-permute-done((bf16[3,96,1024]{2,1,0:T(8,128)(2,1)S(1)}, bf16[3,96,1024]{2,1,0:T(8,128)(2,1)S(1)}, u32[]{:S(2)}, u32[]{:S(2)}) %collective-permute-start.12) | collective-permute-done | bytes 589856 | tf_op jit(solution)/shard_map/ppermute | solution.py:290
  69.7 5.0 %collective-permute-start.14 = (bf16[3,96,1024]{2,1,0:T(8,128)(2,1)S(1)}, bf16[3,96,1024]{2,1,0:T(8,128)(2,1)}, u32[]{:S(2)}, u32[]{:S(2)}) collective-permute-start(bf16[3,96,1024]{2,1,0:T(8,128)(2,1)S(1)} %pick_items.58), channel_id=1, source_target_pairs={{0,4},{4,8},{8,12},{1,5},{5,9},{9,13},{2,6},{6,10},{10,14},{3,7},{... | collective-permute-start | bytes 1769480 | tf_op jit(solution)/shard_map/ppermute | solution.py:290
  74.8 1.6 pick_items.59
  79.2 1.6 pick_items.60
  80.8 4.1 %collective-permute-start.16 = (bf16[3,96,1024]{2,1,0:T(8,128)(2,1)S(1)}, bf16[3,96,1024]{2,1,0:T(8,128)(2,1)S(1)}, u32[]{:S(2)}, u32[]{:S(2)}) collective-permute-start(bf16[3,96,1024]{2,1,0:T(8,128)(2,1)S(1)} %pick_items.60), channel_id=1, source_target_pairs={{0,4},{4,8},{8,12},{1,5},{5,9},{9,13},{2,6},{6,10},{10,14},{3,7},{... | collective-permute-start | bytes 1769480 | tf_op jit(solution)/shard_map/ppermute | solution.py:290
  84.9 1.6 pick_items.61
  88.0 1.6 pick_items.62
  89.6 4.0 %collective-permute-start.18 = (bf16[3,96,1024]{2,1,0:T(8,128)(2,1)S(1)}, bf16[3,96,1024]{2,1,0:T(8,128)(2,1)S(1)}, u32[]{:S(2)}, u32[]{:S(2)}) collective-permute-start(bf16[3,96,1024]{2,1,0:T(8,128)(2,1)S(1)} %pick_items.62), channel_id=1, source_target_pairs={{0,4},{4,8},{8,12},{1,5},{5,9},{9,13},{2,6},{6,10},{10,14},{3,7},{... | collective-permute-start | bytes 1769480 | tf_op jit(solution)/shard_map/ppermute | solution.py:290
  93.7 1.6 pick_items.63
  96.6 1.9 collective-permute-done.16.refs_2_
  100.1 3.3 collective-permute-start.20
  107.7 3.5 %collective-permute-done.18.refs_4_ = bf16[3,96,1024]{2,1,0:T(8,128)(2,1)S(1)} collective-permute-done((bf16[3,96,1024]{2,1,0:T(8,128)(2,1)S(1)}, bf16[3,96,1024]{2,1,0:T(8,128)(2,1)S(1)}, u32[]{:S(2)}, u32[]{:S(2)}) %collective-permute-start.18) | collective-permute-done | bytes 589856 | tf_op jit(solution)/shard_map/ppermute | solution.py:290
  112.8 4.2 %collective-permute-start.24 = (bf16[3,96,1024]{2,1,0:T(8,128)(2,1)S(1)}, bf16[3,96,1024]{2,1,0:T(8,128)(2,1)S(1)}, u32[]{:S(2)}, u32[]{:S(2)}) collective-permute-start(bf16[3,96,1024]{2,1,0:T(8,128)(2,1)S(1)} %pick_items.66), channel_id=1, source_target_pairs={{0,4},{4,8},{8,12},{1,5},{5,9},{9,13},{2,6},{6,10},{10,14},{3,7},{... | collective-permute-start | bytes 1769480 | tf_op jit(solution)/shard_map/ppermute | solution.py:290
  120.3 3.5 %collective-permute-done.20.refs_3_ = bf16[3,96,1024]{2,1,0:T(8,128)(2,1)S(1)} collective-permute-done((bf16[3,96,1024]{2,1,0:T(8,128)(2,1)S(1)}, bf16[3,96,1024]{2,1,0:T(8,128)(2,1)S(1)}, u32[]{:S(2)}, u32[]{:S(2)}) %collective-permute-start.20) | collective-permute-done | bytes 589856 | tf_op jit(solution)/shard_map/ppermute | solution.py:290
  125.4 4.6 %collective-permute-done.22.refs_3_ = bf16[3,96,1024]{2,1,0:T(8,128)(2,1)S(1)} collective-permute-done((bf16[3,96,1024]{2,1,0:T(8,128)(2,1)S(1)}, bf16[3,96,1024]{2,1,0:T(8,128)(2,1)S(1)}, u32[]{:S(2)}, u32[]{:S(2)}) %collective-permute-start.22) | collective-permute-done | bytes 589856 | tf_op jit(solution)/shard_map/ppermute | solution.py:290
  133.0 4.8 %collective-permute-start.21 = (bf16[3,96,1024]{2,1,0:T(8,128)(2,1)S(1)}, bf16[3,96,1024]{2,1,0:T(8,128)(2,1)}, u32[]{:S(2)}, u32[]{:S(2)}) collective-permute-start(bf16[3,96,1024]{2,1,0:T(8,128)(2,1)S(1)} %pick_items.68), channel_id=1, source_target_pairs={{0,4},{4,8},{8,12},{1,5},{5,9},{9,13},{2,6},{6,10},{10,14},{3,7},{... | collective-permute-start | bytes 1769480 | tf_op jit(solution)/shard_map/ppermute | solution.py:290
  137.8 1.6 pick_items.70
  139.4 3.2 collective-permute-done.26.refs_5_
  145.6 4.8 %collective-permute-start.25 = (bf16[3,96,1024]{2,1,0:T(8,128)(2,1)S(1)}, bf16[3,96,1024]{2,1,0:T(8,128)(2,1)}, u32[]{:S(2)}, u32[]{:S(2)}) collective-permute-start(bf16[3,96,1024]{2,1,0:T(8,128)(2,1)S(1)} %pick_items.70), channel_id=1, source_target_pairs={{0,4},{4,8},{8,12},{1,5},{5,9},{9,13},{2,6},{6,10},{10,14},{3,7},{... | collective-permute-start | bytes 1769480 | tf_op jit(solution)/shard_map/ppermute | solution.py:290
  151.2 4.2 %collective-permute-done.23 = bf16[3,96,1024]{2,1,0:T(8,128)(2,1)} collective-permute-done((bf16[3,96,1024]{2,1,0:T(8,128)(2,1)S(1)}, bf16[3,96,1024]{2,1,0:T(8,128)(2,1)}, u32[]{:S(2)}, u32[]{:S(2)}) %collective-permute-start.23) | collective-permute-done | bytes 589856 | tf_op jit(solution)/shard_map/ppermute | solution.py:290
  156.6 11.4 %collective-permute-done.27 = bf16[3,96,1024]{2,1,0:T(8,128)(2,1)} collective-permute-done((bf16[3,96,1024]{2,1,0:T(8,128)(2,1)S(1)}, bf16[3,96,1024]{2,1,0:T(8,128)(2,1)}, u32[]{:S(2)}, u32[]{:S(2)}) %collective-permute-start.27) | collective-permute-done | bytes 589856 | tf_op jit(solution)/shard_map/ppermute | solution.py:290
  168.0 3.6 %conditional.8 = (bf16[4,3,96,1024]{3,2,1,0:T(8,128)(2,1)}) conditional(s32[]{:T(128)} %bitcast.12, (s32[2,128]{1,0:T(2,128)S(1)}, bf16[4,3,96,1024]{3,2,1,0:T(8,128)(2,1)}, bf16[3,96,1024]{2,1,0:T(8,128)(2,1)}, bf16[3,96,1024]{2,1,0:T(8,128)(2,1)}, bf16[3,96,1024]{2,1,0:T(8,128)(2,1)}, /*index=5*/bf16[3,96,1024]{2,1,0:T(8,128)(2,1)}, ...), branch_computations={%region_1.2_spmd, %region_2.8_spmd} | conditional | flops 1180712 | bytes 77861928 | solution.py:311
  168.0 3.6 %pick_items.36 = bf16[4,3,96,1024]{3,2,1,0:T(8,128)(2,1)} custom-call(s32[2,128]{1,0:T(2,128)S(1)} %get-tuple-element.290.refs_0_, bf16[4,3,96,1024]{3,2,1,0:T(8,128)(2,1)} %get-tuple-element.291.refs_1_, bf16[3,96,1024]{2,1,0:T(8,128)(2,1)} %get-tuple-element.292.refs_2_, bf16[3,96,1024]{2,1,0:T(8,128)(2,1)} %get-tuple-element.293.refs_3_, ...), custom_call_target="tpu_custom_call" | custom-call | bytes 9437184 | tf_op jit(solution)/shard_map/cond/branch_0_fun/pick_items/pallas_call | solution.py:234
  171.7 5.6 %all-to-all-start.2 = ((bf16[4,3,96,1024]{3,2,1,0:T(8,128)(2,1)}), bf16[4,3,96,1024]{3,2,1,0:T(8,128)(2,1)S(1)}, u32[]{:S(2)}, u32[]{:S(2)}) async-start(bf16[4,3,96,1024]{3,2,1,0:T(8,128)(2,1)} %get-tuple-element.638), calls=%async_computation.2 | async-start | bytes 4718592 | tf_op jit(solution)/shard_map/all_to_all | solution.py:260
  178.5 3.9 %conditional.9 = (bf16[4,3,96,1024]{3,2,1,0:T(8,128)(2,1)}) conditional(s32[]{:T(128)} %bitcast.17, (s32[2,128]{1,0:T(2,128)S(1)}, bf16[4,3,96,1024]{3,2,1,0:T(8,128)(2,1)}, bf16[3,96,1024]{2,1,0:T(8,128)(2,1)S(1)}, bf16[3,96,1024]{2,1,0:T(8,128)(2,1)}, bf16[3,96,1024]{2,1,0:T(8,128)(2,1)}, /*index=5*/bf16[3,96,1024]{2,1,0:T(8,128)(2,1)S(1)}, ...), branch_computations={%region_7.10_spmd, %region_8.19_spmd} | conditional | flops 1180716 | bytes 87299400 | solution.py:311
  178.5 3.7 %pick_items.43 = bf16[4,3,96,1024]{3,2,1,0:T(8,128)(2,1)} custom-call(s32[2,128]{1,0:T(2,128)S(1)} %get-tuple-element.462.refs_0_, bf16[4,3,96,1024]{3,2,1,0:T(8,128)(2,1)} %get-tuple-element.463.refs_1_, bf16[3,96,1024]{2,1,0:T(8,128)(2,1)S(1)} %get-tuple-element.464.refs_2_, bf16[3,96,1024]{2,1,0:T(8,128)(2,1)} %get-tuple-element.465.refs_3_, ...), custom_call_target="tpu_custom_call" | custom-call | bytes 9437184 | tf_op jit(solution)/shard_map/cond/branch_0_fun/pick_items/pallas_call | solution.py:234
  182.4 22.5 %all-to-all-done.2.blocks_ref = bf16[4,3,96,1024]{3,2,1,0:T(8,128)(2,1)S(1)} async-done(((bf16[4,3,96,1024]{3,2,1,0:T(8,128)(2,1)}), bf16[4,3,96,1024]{3,2,1,0:T(8,128)(2,1)S(1)}, u32[]{:S(2)}, u32[]{:S(2)}) %all-to-all-start.2) | async-done | bytes 2359328 | tf_op jit(solution)/shard_map/all_to_all | solution.py:260
  204.9 5.4 %all-to-all-start.4 = ((bf16[4,3,96,1024]{3,2,1,0:T(8,128)(2,1)}), bf16[4,3,96,1024]{3,2,1,0:T(8,128)(2,1)}, u32[]{:S(2)}, u32[]{:S(2)}) async-start(bf16[4,3,96,1024]{3,2,1,0:T(8,128)(2,1)} %get-tuple-element.639), calls=%async_computation.4 | async-start | bytes 4718592 | tf_op jit(solution)/shard_map/all_to_all | solution.py:260
  213.7 2.8 copy-done
  216.4 13.6 %run_document.2 = (bf16[384,1024]{1,0:T(8,128)(2,1)}, bf16[1,3,1024,1024]{3,2,1,0:T(8,128)(2,1)S(1)}) custom-call(s32[1]{0:T(128)} %constant.99.clone.1.live_ref, bf16[4,3,96,1024]{3,2,1,0:T(8,128)(2,1)S(1)} %all-to-all-done.2.blocks_ref, f32[384,1]{1,0:T(8,128)S(1)} %copy.19.rates_ref, bf16[1,3,1024,1024]{3,2,1,0:T(8,128)(2,1)S(1)} %copy-done, ...), custom_call_target="tpu_custom_call" | custom-call | flops 7247757312 | bytes 15728640 | tf_op jit(solution)/shard_map/run_document/pallas_call | solution.py:113
  230.0 2.6 copy-done.1
  232.6 5.3 %all-to-all-done.4.blocks_ref = bf16[4,3,96,1024]{3,2,1,0:T(8,128)(2,1)} async-done(((bf16[4,3,96,1024]{3,2,1,0:T(8,128)(2,1)}), bf16[4,3,96,1024]{3,2,1,0:T(8,128)(2,1)}, u32[]{:S(2)}, u32[]{:S(2)}) %all-to-all-start.4) | async-done | bytes 2359328 | tf_op jit(solution)/shard_map/all_to_all | solution.py:260
  238.0 4.9 %all-to-all-start.3 = ((bf16[16,24,1024]{2,1,0:T(8,128)(2,1)}), bf16[16,24,1024]{2,1,0:T(8,128)(2,1)}, u32[]{:S(2)}, u32[]{:S(2)}) async-start(bf16[16,24,1024]{2,1,0:T(8,128)(2,1)} %bitcast.15), calls=%async_computation.3 | async-start | bytes 1572864 | tf_op jit(solution)/shard_map/all_to_all | solution.py:260
  243.7 2.8 copy-done.2
  246.4 14.9 %run_document.3 = bf16[384,1024]{1,0:T(8,128)(2,1)S(1)} custom-call(s32[1]{0:T(128)} %dynamic_slice.16.live_ref, bf16[4,3,96,1024]{3,2,1,0:T(8,128)(2,1)} %all-to-all-done.4.blocks_ref, f32[384,1]{1,0:T(8,128)S(1)} %copy.20.rates_ref, bf16[1,3,1024,1024]{3,2,1,0:T(8,128)(2,1)S(1)} %copy-done.2, bf16[1,3,1024,1024]{3,2,1,0:T(8,128)(2,1)S(1)} %copy-done.2, ...), custom_call_target="tpu_custom_call" | custom-call | flops 7247757312 | bytes 15728640 | tf_op jit(solution)/shard_map/run_document/pallas_call | solution.py:113
  261.6 1.7 gather_fusion.2
  264.8 6.0 %all-to-all-start.5 = ((bf16[16,2,24,1024]{3,2,1,0:T(8,128)(2,1)}), bf16[16,2,24,1024]{3,2,1,0:T(8,128)(2,1)S(1)}, u32[]{:S(2)}, u32[]{:S(2)}) async-start(bf16[16,2,24,1024]{3,2,1,0:T(8,128)(2,1)} %pad_maximum_fusion), calls=%async_computation.5 | async-start | bytes 3145728 | tf_op jit(solution)/shard_map/all_to_all | solution.py:260
  270.8 32.3 %all-to-all-done.5 = bf16[16,2,24,1024]{3,2,1,0:T(8,128)(2,1)S(1)} async-done(((bf16[16,2,24,1024]{3,2,1,0:T(8,128)(2,1)}), bf16[16,2,24,1024]{3,2,1,0:T(8,128)(2,1)S(1)}, u32[]{:S(2)}, u32[]{:S(2)}) %all-to-all-start.5) | async-done | bytes 1572896 | tf_op jit(solution)/shard_map/all_to_all | solution.py:260
  304.9 29.2 %all_to_all.35 = bf16[16,24,1024]{2,1,0:T(8,128)(2,1)S(1)} all-to-all(bf16[16,24,1024]{2,1,0:T(8,128)(2,1)S(1)} %broadcast_select_fusion.2), channel_id=1, replica_groups=mesh['grp'=2,'z'=4,'x'=2,'core'=2] {'z','x','core'}, dimensions={0} | all-to-all | bytes 1572864 | tf_op jit(solution)/shard_map/all_to_all | solution.py:260
  (99 shorter events, 36.6 us)
Async XLA Ops:
  9.9 32.5 %all-to-all-start = ((bf16[4,3,96,1024]{3,2,1,0:T(8,128)(2,1)}), bf16[4,3,96,1024]{3,2,1,0:T(8,128)(2,1)}, u32[]{:S(2)}, u32[]{:S(2)}) async-start(bf16[4,3,96,1024]{3,2,1,0:T(8,128)(2,1)} %pack_blocks.2), calls=%async_computation | async-start | bytes 4718592 | tf_op jit(solution)/shard_map/all_to_all | solution.py:260
  14.4 2.7 copy-start.22
  14.4 3.4 copy-start.21
  14.4 3.4 copy-start.23
  17.9 24.5 %copy-start.24 = (s32[16]{0:T(128)}, s32[16]{0:T(128)S(1)}, u32[]{:S(2)}) copy-start(s32[16]{0:T(128)S(1)} %select_reduce_fusion) | copy-start | bytes 196
  45.7 33.5 %all-to-all-start.1 = ((bf16[4,3,96,1024]{3,2,1,0:T(8,128)(2,1)}), bf16[4,3,96,1024]{3,2,1,0:T(8,128)(2,1)}, u32[]{:S(2)}, u32[]{:S(2)}) async-start(bf16[4,3,96,1024]{3,2,1,0:T(8,128)(2,1)} %pack_blocks.3), calls=%async_computation.1 | async-start | bytes 4718592 | tf_op jit(solution)/shard_map/all_to_all | solution.py:260
  51.4 16.7 %collective-permute-start.12 = (bf16[3,96,1024]{2,1,0:T(8,128)(2,1)S(1)}, bf16[3,96,1024]{2,1,0:T(8,128)(2,1)S(1)}, u32[]{:S(2)}, u32[]{:S(2)}) collective-permute-start(bf16[3,96,1024]{2,1,0:T(8,128)(2,1)S(1)} %pick_items.56), channel_id=1, source_target_pairs={{0,4},{4,8},{8,12},{1,5},{5,9},{9,13},{2,6},{6,10},{10,14},{3,7},{... | collective-permute-start | bytes 1769480 | tf_op jit(solution)/shard_map/ppermute | solution.py:290
  55.5 19.3 %collective-permute-start.13 = (bf16[3,96,1024]{2,1,0:T(8,128)(2,1)S(1)}, bf16[3,96,1024]{2,1,0:T(8,128)(2,1)S(1)}, u32[]{:S(2)}, u32[]{:S(2)}) collective-permute-start(bf16[3,96,1024]{2,1,0:T(8,128)(2,1)S(1)} %pick_items.57), channel_id=1, source_target_pairs={{4,0},{8,4},{12,8},{5,1},{9,5},{13,9},{6,2},{10,6},{14,10},{7,3},{... | collective-permute-start | bytes 1769480 | tf_op jit(solution)/shard_map/ppermute | solution.py:290
  68.1 19.8 %copy-start.7 = (bf16[3,96,1024]{2,1,0:T(8,128)(2,1)}, bf16[3,96,1024]{2,1,0:T(8,128)(2,1)S(1)}, u32[]{:S(2)}) copy-start(bf16[3,96,1024]{2,1,0:T(8,128)(2,1)S(1)} %collective-permute-done.12.refs_2_) | copy-start | bytes 1769476
  69.7 18.2 %collective-permute-start.14 = (bf16[3,96,1024]{2,1,0:T(8,128)(2,1)S(1)}, bf16[3,96,1024]{2,1,0:T(8,128)(2,1)}, u32[]{:S(2)}, u32[]{:S(2)}) collective-permute-start(bf16[3,96,1024]{2,1,0:T(8,128)(2,1)S(1)} %pick_items.58), channel_id=1, source_target_pairs={{0,4},{4,8},{8,12},{1,5},{5,9},{9,13},{2,6},{6,10},{10,14},{3,7},{... | collective-permute-start | bytes 1769480 | tf_op jit(solution)/shard_map/ppermute | solution.py:290
  74.8 6.0 %copy-start.10 = (bf16[3,96,1024]{2,1,0:T(8,128)(2,1)}, bf16[3,96,1024]{2,1,0:T(8,128)(2,1)S(1)}, u32[]{:S(2)}) copy-start(bf16[3,96,1024]{2,1,0:T(8,128)(2,1)S(1)} %collective-permute-done.13.refs_2_) | copy-start | bytes 1769476
  76.4 17.2 %collective-permute-start.15 = (bf16[3,96,1024]{2,1,0:T(8,128)(2,1)S(1)}, bf16[3,96,1024]{2,1,0:T(8,128)(2,1)}, u32[]{:S(2)}, u32[]{:S(2)}) collective-permute-start(bf16[3,96,1024]{2,1,0:T(8,128)(2,1)S(1)} %pick_items.59), channel_id=1, source_target_pairs={{4,0},{8,4},{12,8},{5,1},{9,5},{13,9},{6,2},{10,6},{14,10},{7,3},{... | collective-permute-start | bytes 1769480 | tf_op jit(solution)/shard_map/ppermute | solution.py:290
  80.8 17.7 %collective-permute-start.16 = (bf16[3,96,1024]{2,1,0:T(8,128)(2,1)S(1)}, bf16[3,96,1024]{2,1,0:T(8,128)(2,1)S(1)}, u32[]{:S(2)}, u32[]{:S(2)}) collective-permute-start(bf16[3,96,1024]{2,1,0:T(8,128)(2,1)S(1)} %pick_items.60), channel_id=1, source_target_pairs={{0,4},{4,8},{8,12},{1,5},{5,9},{9,13},{2,6},{6,10},{10,14},{3,7},{... | collective-permute-start | bytes 1769480 | tf_op jit(solution)/shard_map/ppermute | solution.py:290
  86.5 7.1 %copy-start.11 = (bf16[3,96,1024]{2,1,0:T(8,128)(2,1)S(1)}, bf16[3,96,1024]{2,1,0:T(8,128)(2,1)}, u32[]{:S(2)}) copy-start(bf16[3,96,1024]{2,1,0:T(8,128)(2,1)} %copy-done.10) | copy-start | bytes 1769476
  86.5 18.2 %collective-permute-start.17 = (bf16[3,96,1024]{2,1,0:T(8,128)(2,1)S(1)}, bf16[3,96,1024]{2,1,0:T(8,128)(2,1)S(1)}, u32[]{:S(2)}, u32[]{:S(2)}) collective-permute-start(bf16[3,96,1024]{2,1,0:T(8,128)(2,1)S(1)} %pick_items.61), channel_id=1, source_target_pairs={{4,0},{8,4},{12,8},{5,1},{9,5},{13,9},{6,2},{10,6},{14,10},{7,3},{... | collective-permute-start | bytes 1769480 | tf_op jit(solution)/shard_map/ppermute | solution.py:290
  89.6 21.5 %collective-permute-start.18 = (bf16[3,96,1024]{2,1,0:T(8,128)(2,1)S(1)}, bf16[3,96,1024]{2,1,0:T(8,128)(2,1)S(1)}, u32[]{:S(2)}, u32[]{:S(2)}) collective-permute-start(bf16[3,96,1024]{2,1,0:T(8,128)(2,1)S(1)} %pick_items.62), channel_id=1, source_target_pairs={{0,4},{4,8},{8,12},{1,5},{5,9},{9,13},{2,6},{6,10},{10,14},{3,7},{... | collective-permute-start | bytes 1769480 | tf_op jit(solution)/shard_map/ppermute | solution.py:290
  95.3 22.1 %collective-permute-start.19 = (bf16[3,96,1024]{2,1,0:T(8,128)(2,1)S(1)}, bf16[3,96,1024]{2,1,0:T(8,128)(2,1)S(1)}, u32[]{:S(2)}, u32[]{:S(2)}) collective-permute-start(bf16[3,96,1024]{2,1,0:T(8,128)(2,1)S(1)} %pick_items.63), channel_id=1, source_target_pairs={{4,0},{8,4},{12,8},{5,1},{9,5},{13,9},{6,2},{10,6},{14,10},{7,3},{... | collective-permute-start | bytes 1769480 | tf_op jit(solution)/shard_map/ppermute | solution.py:290
  100.1 11.0 %copy-start.8 = (bf16[3,96,1024]{2,1,0:T(8,128)(2,1)S(1)}, bf16[3,96,1024]{2,1,0:T(8,128)(2,1)}, u32[]{:S(2)}) copy-start(bf16[3,96,1024]{2,1,0:T(8,128)(2,1)} %copy-done.7) | copy-start | bytes 1769476
  100.1 23.6 %collective-permute-start.20 = (bf16[3,96,1024]{2,1,0:T(8,128)(2,1)S(1)}, bf16[3,96,1024]{2,1,0:T(8,128)(2,1)S(1)}, u32[]{:S(2)}, u32[]{:S(2)}) collective-permute-start(bf16[3,96,1024]{2,1,0:T(8,128)(2,1)S(1)} %pick_items.64), channel_id=1, source_target_pairs={{0,4},{4,8},{8,12},{1,5},{5,9},{9,13},{2,6},{6,10},{10,14},{3,7},{... | collective-permute-start | bytes 1769480 | tf_op jit(solution)/shard_map/ppermute | solution.py:290
  106.4 23.6 %collective-permute-start.22 = (bf16[3,96,1024]{2,1,0:T(8,128)(2,1)S(1)}, bf16[3,96,1024]{2,1,0:T(8,128)(2,1)S(1)}, u32[]{:S(2)}, u32[]{:S(2)}) collective-permute-start(bf16[3,96,1024]{2,1,0:T(8,128)(2,1)S(1)} %pick_items.65), channel_id=1, source_target_pairs={{4,0},{8,4},{12,8},{5,1},{9,5},{13,9},{6,2},{10,6},{14,10},{7,3},{... | collective-permute-start | bytes 1769480 | tf_op jit(solution)/shard_map/ppermute | solution.py:290
  111.1 26.6 %copy-start.13 = (bf16[3,96,1024]{2,1,0:T(8,128)(2,1)}, bf16[3,96,1024]{2,1,0:T(8,128)(2,1)S(1)}, u32[]{:S(2)}) copy-start(bf16[3,96,1024]{2,1,0:T(8,128)(2,1)S(1)} %collective-permute-done.18.refs_4_) | copy-start | bytes 1769476
  112.8 25.0 %collective-permute-start.24 = (bf16[3,96,1024]{2,1,0:T(8,128)(2,1)S(1)}, bf16[3,96,1024]{2,1,0:T(8,128)(2,1)S(1)}, u32[]{:S(2)}, u32[]{:S(2)}) collective-permute-start(bf16[3,96,1024]{2,1,0:T(8,128)(2,1)S(1)} %pick_items.66), channel_id=1, source_target_pairs={{0,4},{4,8},{8,12},{1,5},{5,9},{9,13},{2,6},{6,10},{10,14},{3,7},{... | collective-permute-start | bytes 1769480 | tf_op jit(solution)/shard_map/ppermute | solution.py:290
  117.4 25.3 %copy-start.15 = (bf16[3,96,1024]{2,1,0:T(8,128)(2,1)}, bf16[3,96,1024]{2,1,0:T(8,128)(2,1)S(1)}, u32[]{:S(2)}) copy-start(bf16[3,96,1024]{2,1,0:T(8,128)(2,1)S(1)} %collective-permute-done.19.refs_4_) | copy-start | bytes 1769476
  119.0 23.6 %collective-permute-start.26 = (bf16[3,96,1024]{2,1,0:T(8,128)(2,1)S(1)}, bf16[3,96,1024]{2,1,0:T(8,128)(2,1)S(1)}, u32[]{:S(2)}, u32[]{:S(2)}) collective-permute-start(bf16[3,96,1024]{2,1,0:T(8,128)(2,1)S(1)} %pick_items.67), channel_id=1, source_target_pairs={{4,0},{8,4},{12,8},{5,1},{9,5},{13,9},{6,2},{10,6},{14,10},{7,3},{... | collective-permute-start | bytes 1769480 | tf_op jit(solution)/shard_map/ppermute | solution.py:290
  123.8 7.9 %copy-start.3 = (bf16[3,96,1024]{2,1,0:T(8,128)(2,1)}, bf16[3,96,1024]{2,1,0:T(8,128)(2,1)S(1)}, u32[]{:S(2)}) copy-start(bf16[3,96,1024]{2,1,0:T(8,128)(2,1)S(1)} %collective-permute-done.20.refs_3_) | copy-start | bytes 1769476
  130.0 14.3 %copy-start.5 = (bf16[3,96,1024]{2,1,0:T(8,128)(2,1)}, bf16[3,96,1024]{2,1,0:T(8,128)(2,1)S(1)}, u32[]{:S(2)}) copy-start(bf16[3,96,1024]{2,1,0:T(8,128)(2,1)S(1)} %collective-permute-done.22.refs_3_) | copy-start | bytes 1769476
  131.7 23.7 %collective-permute-start.23 = (bf16[3,96,1024]{2,1,0:T(8,128)(2,1)S(1)}, bf16[3,96,1024]{2,1,0:T(8,128)(2,1)}, u32[]{:S(2)}, u32[]{:S(2)}) collective-permute-start(bf16[3,96,1024]{2,1,0:T(8,128)(2,1)S(1)} %pick_items.69), channel_id=1, source_target_pairs={{4,0},{8,4},{12,8},{5,1},{9,5},{13,9},{6,2},{10,6},{14,10},{7,3},{... | collective-permute-start | bytes 1769480 | tf_op jit(solution)/shard_map/ppermute | solution.py:290
  133.0 22.4 %collective-permute-start.21 = (bf16[3,96,1024]{2,1,0:T(8,128)(2,1)S(1)}, bf16[3,96,1024]{2,1,0:T(8,128)(2,1)}, u32[]{:S(2)}, u32[]{:S(2)}) collective-permute-start(bf16[3,96,1024]{2,1,0:T(8,128)(2,1)S(1)} %pick_items.68), channel_id=1, source_target_pairs={{0,4},{4,8},{8,12},{1,5},{5,9},{9,13},{2,6},{6,10},{10,14},{3,7},{... | collective-permute-start | bytes 1769480 | tf_op jit(solution)/shard_map/ppermute | solution.py:290
  137.8 1.6 copy-start.17
  142.7 1.6 copy-start.19
  144.3 23.7 %collective-permute-start.27 = (bf16[3,96,1024]{2,1,0:T(8,128)(2,1)S(1)}, bf16[3,96,1024]{2,1,0:T(8,128)(2,1)}, u32[]{:S(2)}, u32[]{:S(2)}) collective-permute-start(bf16[3,96,1024]{2,1,0:T(8,128)(2,1)S(1)} %pick_items.71), channel_id=1, source_target_pairs={{4,0},{8,4},{12,8},{5,1},{9,5},{13,9},{6,2},{10,6},{14,10},{7,3},{... | collective-permute-start | bytes 1769480 | tf_op jit(solution)/shard_map/ppermute | solution.py:290
  145.6 22.4 %collective-permute-start.25 = (bf16[3,96,1024]{2,1,0:T(8,128)(2,1)S(1)}, bf16[3,96,1024]{2,1,0:T(8,128)(2,1)}, u32[]{:S(2)}, u32[]{:S(2)}) collective-permute-start(bf16[3,96,1024]{2,1,0:T(8,128)(2,1)S(1)} %pick_items.70), channel_id=1, source_target_pairs={{0,4},{4,8},{8,12},{1,5},{5,9},{9,13},{2,6},{6,10},{10,14},{3,7},{... | collective-permute-start | bytes 1769480 | tf_op jit(solution)/shard_map/ppermute | solution.py:290
  150.6 17.5 %copy-start.27 = (s32[16]{0:T(128)}, s32[16]{0:T(128)S(1)}, u32[]{:S(2)}) copy-start(s32[16]{0:T(128)S(1)} %select_reduce_fusion.1) | copy-start | bytes 196
  171.6 6.8 %copy-start.29 = (s32[4]{0:T(128)S(1)}, s32[4]{0:T(128)}, u32[]{:S(2)}) copy-start(s32[4]{0:T(128)} %dynamic_slice.13) | copy-start | bytes 52
  171.7 33.2 %all-to-all-start.2 = ((bf16[4,3,96,1024]{3,2,1,0:T(8,128)(2,1)}), bf16[4,3,96,1024]{3,2,1,0:T(8,128)(2,1)S(1)}, u32[]{:S(2)}, u32[]{:S(2)}) async-start(bf16[4,3,96,1024]{3,2,1,0:T(8,128)(2,1)} %get-tuple-element.638), calls=%async_computation.2 | async-start | bytes 4718592 | tf_op jit(solution)/shard_map/all_to_all | solution.py:260
  182.4 27.9 %copy-start.28 = (s32[16]{0:T(128)S(1)}, s32[16]{0:T(128)}, u32[]{:S(2)}) copy-start(s32[16]{0:T(128)} %copy-done.27) | copy-start | bytes 196
  204.9 33.1 %all-to-all-start.4 = ((bf16[4,3,96,1024]{3,2,1,0:T(8,128)(2,1)}), bf16[4,3,96,1024]{3,2,1,0:T(8,128)(2,1)}, u32[]{:S(2)}, u32[]{:S(2)}) async-start(bf16[4,3,96,1024]{3,2,1,0:T(8,128)(2,1)} %get-tuple-element.639), calls=%async_computation.4 | async-start | bytes 4718592 | tf_op jit(solution)/shard_map/all_to_all | solution.py:260
  213.6 2.8 copy-start
  216.4 26.6 %copy-start.26 = (s32[16]{0:T(128)S(1)}, s32[16]{0:T(128)}, u32[]{:S(2)}) copy-start(s32[16]{0:T(128)} %get-tuple-element.621) | copy-start | bytes 196
  230.0 2.6 copy-start.1
  238.0 23.6 %all-to-all-start.3 = ((bf16[16,24,1024]{2,1,0:T(8,128)(2,1)}), bf16[16,24,1024]{2,1,0:T(8,128)(2,1)}, u32[]{:S(2)}, u32[]{:S(2)}) async-start(bf16[16,24,1024]{2,1,0:T(8,128)(2,1)} %bitcast.15), calls=%async_computation.3 | async-start | bytes 1572864 | tf_op jit(solution)/shard_map/all_to_all | solution.py:260
  243.7 2.8 copy-start.2
  264.8 6.0 %copy-start.25 = (s32[16]{0:T(128)S(1)}, s32[16]{0:T(128)}, u32[]{:S(2)}) copy-start(s32[16]{0:T(128)} %copy-done.24) | copy-start | bytes 196
  264.8 38.3 %all-to-all-start.5 = ((bf16[16,2,24,1024]{3,2,1,0:T(8,128)(2,1)}), bf16[16,2,24,1024]{3,2,1,0:T(8,128)(2,1)S(1)}, u32[]{:S(2)}, u32[]{:S(2)}) async-start(bf16[16,2,24,1024]{3,2,1,0:T(8,128)(2,1)} %pad_maximum_fusion), calls=%async_computation.5 | async-start | bytes 3145728 | tf_op jit(solution)/shard_map/all_to_all | solution.py:260
